TPU v7x, 32 devices: a whole 2x2x4 slice. The times are simulated.
32 devices in a mesh: gz: 4 (over x, core), gy: 8 (over z, y).
Axes of the slice: x: 2, y: 2, z: 4, core: 2. Of those that a mesh axis runs over, the one named last changes fastest.
Arguments:
- velocity: float32 [3, 256, 256, 512], P(None, None, 'gy', 'gz'), may hold values from -0.3 to 0.3
- increment: float32 [3, 256, 256, 512], P(None, None, 'gy', 'gz'), may hold values from -4 to 4
- template: bfloat16 [256, 256, 512], P(None, 'gy', 'gz'), may hold values from 0 to 1
- deformed: bfloat16 [256, 256, 512], P(None, 'gy', 'gz'), may hold values from 0 to 1
Outputs:
- preconditioned: float32 [3, 256, 256, 512], P(None, None, 'gy', 'gz')
All inputs are finite; a program needn't handle non-finite values.
Results may differ from a plain program's by a relative error of at most 0.0003.
Values sent between devices are 32-bit elements; how exact they have to be, the bound alone decides.
No kernel may reach another device: no remote copies, remote signals or barrier semaphores. Data moves between devices by JAX's collectives and lax.ppermute only.
A program may use at most 576 MiB of HBM per device.

v0:
```python
import math

import jax
import jax.numpy as jnp
from jax import lax
from jax.sharding import PartitionSpec as P

STEP = 0.5
BETA = 0.02
GAMMA = 0.05
COARSE_BETA = 0.025
OMEGA = 1.0 / (0.05 + 42.0 * 0.02)


def extended(cells, sides, width):
    for axis, dim in sides:
        count = lax.axis_size(axis)
        head = lax.slice_in_dim(cells, 0, width, axis=dim)
        tail = lax.slice_in_dim(cells, cells.shape[dim] - width, cells.shape[dim], axis=dim)
        cells = jnp.concatenate(
            [
                lax.ppermute(tail, axis, [(i, (i + 1) % count) for i in range(count)]),
                cells,
                lax.ppermute(head, axis, [((i + 1) % count, i) for i in range(count)]),
            ],
            axis=dim,
        )
    return cells


def shifted(value, axis, by):
    peers = lax.axis_size(axis)
    return lax.ppermute(value, axis, [(i, (i + by) % peers) for i in range(peers)])


def cas_table(count):
    index = jnp.arange(count, dtype=jnp.int32)
    product = index[:, None] * index[None, :] % count
    angle = product.astype(jnp.float32) * (2.0 * math.pi / count)
    return jnp.cos(angle) + jnp.sin(angle)


def eigen_line(count):
    index = jnp.arange(count, dtype=jnp.int32).astype(jnp.float32)
    return 2.0 - 2.0 * jnp.cos(index * (2.0 * math.pi / count))


def with_rims(stacked):
    padded = extended(stacked, (("gy", 2),), 1)
    center = padded[:, :, 1:-1, :]
    first_plane = center[:, :, :, :1]
    last_plane = center[:, :, :, -1:]
    before_plane = shifted(last_plane, "gz", 1)
    after_plane = shifted(first_plane, "gz", -1)
    z_next = jnp.concatenate([center[:, :, :, 1:], after_plane], axis=3)
    z_prev = jnp.concatenate([before_plane, center[:, :, :, :-1]], axis=3)
    pairs = [
        (jnp.roll(center, -1, 1), jnp.roll(center, 1, 1)),
        (padded[:, :, 2:, :], padded[:, :, :-2, :]),
        (z_next, z_prev),
    ]
    return (center, pairs)


def expand(field):
    return jnp.repeat(jnp.repeat(jnp.repeat(field, 4, axis=1), 4, axis=2), 4, axis=3)


def fine_filter(field):
    high = lax.Precision.HIGHEST
    groups_z = lax.axis_size("gz")
    groups_y = lax.axis_size("gy")
    devices = groups_z * groups_y
    xlen, ylen, zlen = (field.shape[1], field.shape[2], field.shape[3])
    xpart = xlen // devices
    full_y = ylen * groups_y
    full_z = zlen * groups_z
    table_x = cas_table(xlen)
    coeffs = jnp.einsum("xi,cijk->cxjk", table_x, field, precision=high)
    pencil = lax.all_to_all(
        lax.all_to_all(coeffs, "gz", split_axis=1, concat_axis=3, tiled=True),
        "gy",
        split_axis=1,
        concat_axis=2,
        tiled=True,
    )
    table_y = cas_table(full_y)
    table_z = cas_table(full_z)
    pencil = jnp.einsum("yj,cxjk->cxyk", table_y, pencil, precision=high)
    pencil = jnp.einsum("zk,cxyk->cxyz", table_z, pencil, precision=high)
    owner = lax.axis_index("gz") * groups_y + lax.axis_index("gy")
    line_x = lax.dynamic_slice_in_dim(eigen_line(xlen), owner * xpart, xpart, 0)
    total = (
        line_x[:, None, None]
        + eigen_line(full_y)[None, :, None]
        + eigen_line(full_z)[None, None, :]
    )
    pencil = pencil * (GAMMA + BETA * total * total)
    pencil = jnp.einsum("yj,cxjk->cxyk", table_y, pencil, precision=high)
    pencil = jnp.einsum("zk,cxyk->cxyz", table_z, pencil, precision=high)
    returned = lax.all_to_all(
        lax.all_to_all(pencil, "gz", split_axis=3, concat_axis=1, tiled=True),
        "gy",
        split_axis=2,
        concat_axis=1,
        tiled=True,
    )
    returned = returned.reshape(3, groups_y, groups_z, xpart, ylen, zlen)
    returned = jnp.transpose(returned, (0, 2, 1, 3, 4, 5)).reshape(3, xlen, ylen, zlen)
    returned = jnp.einsum("xi,cijk->cxjk", table_x, returned, precision=high)
    return returned / float(xlen * full_y * full_z)


def coarse_spread(restricted):
    high = lax.Precision.HIGHEST
    groups_z = lax.axis_size("gz")
    groups_y = lax.axis_size("gy")
    cxlen, cylen, czlen = (restricted.shape[1], restricted.shape[2], restricted.shape[3])
    full_y = groups_y * cylen
    full_z = groups_z * czlen
    xpart = cxlen // groups_y
    ypart = full_y // groups_z
    table_x = cas_table(cxlen)
    table_y = cas_table(full_y)
    table_z = cas_table(full_z)
    coeffs = jnp.einsum("xi,cijk->cxjk", table_x, restricted, precision=high)
    rows = lax.all_to_all(coeffs, "gy", split_axis=1, concat_axis=2, tiled=True)
    rows = jnp.einsum("yj,cxjk->cxyk", table_y, rows, precision=high)
    cols = lax.all_to_all(rows, "gz", split_axis=2, concat_axis=3, tiled=True)
    cols = jnp.einsum("zk,cxyk->cxyz", table_z, cols, precision=high)
    line_x = lax.dynamic_slice_in_dim(eigen_line(cxlen), lax.axis_index("gy") * xpart, xpart, 0)
    line_y = lax.dynamic_slice_in_dim(eigen_line(full_y), lax.axis_index("gz") * ypart, ypart, 0)
    total = line_x[:, None, None] + line_y[None, :, None] + eigen_line(full_z)[None, None, :]
    cols = cols / (GAMMA + COARSE_BETA * total * total)
    cols = jnp.einsum("zk,cxyk->cxyz", table_z, cols, precision=high)
    rows = lax.all_to_all(cols, "gz", split_axis=3, concat_axis=2, tiled=True)
    rows = jnp.einsum("yj,cxjk->cxyk", table_y, rows, precision=high)
    coeffs = lax.all_to_all(rows, "gy", split_axis=2, concat_axis=1, tiled=True)
    coeffs = jnp.einsum("xi,cijk->cxjk", table_x, coeffs, precision=high)
    return coeffs / float(cxlen * full_y * full_z)


def per_device(velocity, increment, template, deformed):
    stacked = jnp.concatenate(
        [template.astype(jnp.float32)[None], deformed.astype(jnp.float32)[None], velocity], axis=0
    )
    center, pairs = with_rims(stacked)
    grad_first = [0.5 * (pairs[d][0][0] - pairs[d][1][0]) for d in range(3)]
    grad_second = [0.5 * (pairs[d][0][1] - pairs[d][1][1]) for d in range(3)]
    speed = [center[2 + d] for d in range(3)]
    speed_next = [pairs[d][0][2 + d] for d in range(3)]
    speed_prev = [pairs[d][1][2 + d] for d in range(3)]
    state_one = -STEP * (
        increment[0] * grad_first[0] + increment[1] * grad_first[1] + increment[2] * grad_first[2]
    )
    state_center, state_pairs = with_rims(state_one[None])
    advect = jnp.zeros_like(state_one)
    for d in range(3):
        advect = advect + jnp.maximum(speed[d], 0.0) * (state_center[0] - state_pairs[d][1][0])
        advect = advect + jnp.minimum(speed[d], 0.0) * (state_pairs[d][0][0] - state_center[0])
    source = (
        increment[0] * grad_second[0]
        + increment[1] * grad_second[1]
        + increment[2] * grad_second[2]
    )
    state_two = state_one - STEP * (advect + source)
    adjoint_two = -state_two
    adjoint_center, adjoint_pairs = with_rims(adjoint_two[None])
    change = jnp.zeros_like(adjoint_two)
    for d in range(3):
        inflow = jnp.minimum(speed[d], 0.0) * adjoint_two
        inflow_prev = jnp.minimum(speed_prev[d], 0.0) * adjoint_pairs[d][1][0]
        outflow = jnp.maximum(speed[d], 0.0) * adjoint_two
        outflow_next = jnp.maximum(speed_next[d], 0.0) * adjoint_pairs[d][0][0]
        change = change + (inflow - inflow_prev) + (outflow_next - outflow)
    adjoint_one = adjoint_two + STEP * change
    force = jnp.stack(
        [STEP * (adjoint_one * grad_first[d] + adjoint_two * grad_second[d]) for d in range(3)]
    )
    hessian = fine_filter(increment) + force
    xlen, ylen, zlen = (hessian.shape[1], hessian.shape[2], hessian.shape[3])
    restricted = jnp.mean(
        hessian.reshape(3, xlen // 4, 4, ylen // 4, 4, zlen // 4, 4), axis=(2, 4, 6)
    )
    coarse = coarse_spread(restricted)
    return expand(coarse) + OMEGA * (hessian - expand(restricted))


def solution(mesh):
    placed = (
        P(None, None, "gy", "gz"),
        P(None, None, "gy", "gz"),
        P(None, "gy", "gz"),
        P(None, "gy", "gz"),
    )
    return jax.shard_map(
        per_device, mesh=mesh, in_specs=placed, out_specs=P(None, None, "gy", "gz"), check_vma=False
    )
```

profile of v0, /device:TPU:0, one launch (start us, length us, event | category | flops | bytes accessed | tf_op | source)
XLA Modules:
  0.0 2028.3 jit_solution(969209611665610586)
XLA Ops:
  0.0 23.4 %fusion.11 = f32[3,256,32,128]{3,1,2,0:T(8,128)} fusion(f32[3,256,32,128]{3,2,1,0:T(8,128)} %param.5), kind=kOutput, calls=%fused_computation.16 | convolution fusion | flops 9664659456 | bytes 25165824 | tf_op jit(solution)/shard_map/xi,cijk->cxjk/dot_general | solution.py:79
  23.4 16.4 copy.93
  39.8 143.1 %all_to_all.141 = f32[3,256,32,128]{3,2,0,1:T(8,128)S(1)} all-to-all(f32[3,256,32,128]{3,2,0,1:T(8,128)} %copy.93), channel_id=1, replica_groups=mesh['gz'=4,'gy'=8] {'gz'}, dimensions={1} | all-to-all | bytes 25165824 | tf_op jit(solution)/shard_map/all_to_all | solution.py:81
  182.9 13.4 copy.176
  196.2 15.1 all_to_all.105
  211.4 12.3 copy.95
  223.7 7.1 all-to-all-start.1
  233.6 269.9 %all-to-all-done.1 = f32[3,64,32,512]{3,2,0,1:T(8,128)} async-done(((f32[3,64,32,512]{3,2,0,1:T(8,128)}), f32[3,64,32,512]{3,2,0,1:T(8,128)}, u32[]{:S(2)}, u32[]{:S(2)}) %all-to-all-start.1) | async-done | bytes 12582944 | tf_op jit(solution)/shard_map/all_to_all | solution.py:80
  503.5 12.3 copy.97
  515.8 26.8 %fusion.83 = f32[3,8,512,256]{3,2,1,0:T(8,128)S(1)} fusion(f32[3,8,256,512]{3,2,1,0:T(8,128)} %bitcast.123), kind=kOutput, calls=%fused_computation.135 | convolution fusion | flops 9664659456 | bytes 25165824 | tf_op jit(solution)/shard_map/yj,cxjk->cxyk/dot_general | solution.py:89
  542.6 50.6 %fusion.2 = f32[3,8,256,512]{3,2,1,0:T(8,128)} fusion(f32[3,8,512,256]{3,2,1,0:T(8,128)S(1)} %fusion.83), kind=kOutput, calls=%fused_computation.4 | convolution fusion | flops 19331284992 | bytes 25165824 | tf_op jit(solution)/shard_map/zk,cxyk->cxyz/dot_general | solution.py:90
  593.3 26.7 %fusion.8 = f32[3,8,512,256]{3,2,1,0:T(8,128)S(1)} fusion(f32[3,8,256,512]{3,2,1,0:T(8,128)} %fusion.2, f32[8,256,512]{2,1,0:T(8,128)S(1)} %copy-done.6), kind=kOutput, calls=%fused_computation.12 | convolution fusion | flops 9667805184 | bytes 29360128 | tf_op jit(solution)/shard_map/yj,cxjk->cxyk/dot_general | solution.py:99
  620.0 50.6 %fusion = f32[3,8,256,512]{3,2,1,0:T(8,128)} fusion(f32[3,8,512,256]{3,2,1,0:T(8,128)S(1)} %fusion.8), kind=kOutput, calls=%fused_computation.2 | convolution fusion | flops 19331284992 | bytes 25165824 | tf_op jit(solution)/shard_map/zk,cxyk->cxyz/dot_general | solution.py:100
  670.6 12.8 copy.102
  683.4 147.4 %all_to_all.142 = f32[3,8,256,512]{2,1,0,3:T(8,128)} all-to-all(f32[3,8,256,512]{2,1,0,3:T(8,128)} %copy.102), channel_id=1, replica_groups=mesh['gz'=4,'gy'=8] {'gz'}, dimensions={3} | all-to-all | bytes 25165824 | tf_op jit(solution)/shard_map/all_to_all | solution.py:102
  830.8 12.6 copy.104
  843.4 16.4 copy.105
  859.8 5.4 all-to-all-start.3
  872.4 12.8 copy.113
  900.7 8.5 pad_maximum_fusion
  909.2 32.2 %fusion.164 = (f32[5,256,32,127]{1,3,2,0:T(8,128)}, f32[5,256,32,127]{1,3,2,0:T(8,128)}) fusion(f32[5,256,32,128]{1,3,2,0:T(8,128)} %pad_maximum_fusion), kind=kLoop, calls=%fused_computation.227 | loop fusion | bytes 83230720 | tf_op jit(solution)/shard_map/slice | solution.py:55
  941.4 14.9 fusion.165
  956.2 8.3 fusion.166
  964.5 9.6 fusion.167
  974.1 5.3 copy.156
  979.5 5.3 copy.157
  990.0 92.6 %collective-permute-done = f32[5,256,1,128]{1,3,2,0:T(8,128)S(1)} collective-permute-done((f32[5,256,1,128]{1,3,2,0:T(8,128)}, f32[5,256,1,128]{1,3,2,0:T(8,128)S(1)}, u32[]{:S(2)}, u32[]{:S(2)}) %collective-permute-start) | collective-permute-done | bytes 655392 | tf_op jit(solution)/shard_map/ppermute | solution.py:24
  1086.5 19.7 add_multiply_fusion.3
  1117.0 5.3 fusion.175
  1125.9 34.3 %fusion.51 = (f32[1,256,32,128]{1,3,2,0:T(8,128)}, f32[1,256,32,128]{1,3,2,0:T(8,128)}, f32[1,256,32,128]{1,3,2,0:T(8,128)}, f32[1,256,32,128]{1,3,2,0:T(8,128)}) fusion(f32[1,256,32,128]{1,3,2,0:T(8,128)} %copy-done.3, f32[1,256,1,128]{1,3,2,0:T(8,128)} %copy-done.14, f32[1,256,1,128]{1,3,2,0:T(8,128)S(1)} %collective-permute-done.4, ...), kind=kLoop, calls=%fused_computation.70 | loop fusion | flops 56623104 | bytes 169345024 | tf_op jit(solution)/shard_map/neg | solution.py:167
  1161.2 53.3 %collective-permute-start.8 = (f32[1,256,1,128]{1,3,2,0:T(8,128)S(1)}, f32[1,256,1,128]{1,3,2,0:T(8,128)S(1)}, u32[]{:S(2)}, u32[]{:S(2)}) collective-permute-start(f32[1,256,1,128]{1,3,2,0:T(8,128)S(1)} %get-tuple-element.34), channel_id=1, source_target_pairs={{0,1},{1,2},{2,3},{3,4},{4,5},{5,6},{6,7},{7,0},{8,9},{9,10},{10,1... | collective-permute-start | bytes 393224 | tf_op jit(solution)/shard_map/ppermute | solution.py:22
  1217.4 8.1 fusion.169
  1232.3 34.8 %add_multiply_fusion.2 = (f32[1,256,32,128]{1,3,2,0:T(8,128)}, f32[1,256,32,128]{1,3,2,0:T(8,128)}) fusion(f32[1,256,32,128]{1,3,2,0:T(8,128)} %get-tuple-element.7, f32[1,256,32,128]{1,3,2,0:T(8,128)} %get-tuple-element.8, f32[1,256,32,128]{1,3,2,0:T(8,128)} %get-tuple-element.12, f32[1,256,32,1]{1,3,2,0:T(1,128)} %copy-done.16, ...), kind=kLoop, calls=%fused_computation.92 | loop fusion | flops 59768832 | bytes 180240384 | tf_op jit(solution)/shard_map/mul | solution.py:178
  1267.1 13.7 add_multiply_fusion.1
  1280.9 16.8 copy.108
  1297.7 32.4 %maximum_add_fusion = f32[3,256,32,128]{1,3,2,0:T(8,128)} fusion(f32[1,256,32,128]{1,3,2,0:T(8,128)} %get-tuple-element.29, f32[1,256,32,128]{1,3,2,0:T(8,128)} %get-tuple-element.28, f32[1,256,32,128]{1,3,2,0:T(8,128)S(1)} %copy-done.7, f32[3,256,32,128]{3,2,1,0:T(8,128)} %bitcast.126), kind=kOutput, calls=%fused_computation.1 | convolution fusion | flops 9677242368 | bytes 37748736 | tf_op jit(solution)/shard_map/xi,cijk->cxjk/dot_general | solution.py:110
  1330.0 12.8 copy.119
  1342.8 417.8 %reshape.127 = f32[3,64,4,8,4,32,4]{6,5,4,3,2,1,0:T(8,128)} reshape(f32[3,256,32,128]{3,2,1,0:T(8,128)} %copy.119) | data formatting | bytes 25165824 | tf_op jit(solution)/shard_map/reshape | solution.py:183
  1760.6 119.9 %reduce_sum.9 = f32[3,64,8,32]{3,2,1,0:T(8,128)S(1)} reduce(f32[3,64,4,8,4,32,4]{6,5,4,3,2,1,0:T(8,128)} %reshape.127, f32[]{:T(128)} %constant.106.clone.1), dimensions={2,4,6}, to_apply=%region_0.1 | reduce | flops 3096576 | bytes 12779524 | tf_op jit(solution)/shard_map/reduce_sum | solution.py:182
  1884.3 16.1 all-to-all-start.4
  1900.7 7.5 all-to-all-done.4
  1925.9 7.9 all_to_all.143
  1946.8 5.8 broadcast_in_dim.61
  1952.6 14.7 reshape.133
  1976.1 5.8 broadcast_in_dim.28
  1981.9 14.7 reshape.130
  1996.6 18.5 multiply_add_fusion
  2015.1 12.8 copy.138
  (132 shorter events, 103.0 us)
Async XLA Ops:
  223.7 279.8 %all-to-all-start.1 = ((f32[3,64,32,512]{3,2,0,1:T(8,128)}), f32[3,64,32,512]{3,2,0,1:T(8,128)}, u32[]{:S(2)}, u32[]{:S(2)}) async-start(f32[3,64,32,512]{3,2,0,1:T(8,128)} %copy.95), calls=%async_computation.1 | async-start | bytes 25165824 | tf_op jit(solution)/shard_map/all_to_all | solution.py:80
  542.6 50.6 %copy-start.6 = (f32[8,256,512]{2,1,0:T(8,128)S(1)}, f32[8,256,512]{2,1,0:T(8,128)}, u32[]{:S(2)}) copy-start(f32[8,256,512]{2,1,0:T(8,128)} %fusion.14) | copy-start | bytes 12582916
  859.8 421.1 %all-to-all-start.3 = ((f32[3,32,256,128]{3,1,0,2:T(8,128)}), f32[3,32,256,128]{3,1,0,2:T(8,128)}, u32[]{:S(2)}, u32[]{:S(2)}) async-start(f32[3,32,256,128]{3,1,0,2:T(8,128)} %copy.105), calls=%async_computation.3 | async-start | bytes 25165824 | tf_op jit(solution)/shard_map/all_to_all | solution.py:101
  885.2 8.1 copy-start
  888.1 12.6 copy-start.4
  888.1 12.6 copy-start.5
  894.5 188.1 %collective-permute-start = (f32[5,256,1,128]{1,3,2,0:T(8,128)}, f32[5,256,1,128]{1,3,2,0:T(8,128)S(1)}, u32[]{:S(2)}, u32[]{:S(2)}) collective-permute-start(f32[5,256,1,128]{1,3,2,0:T(8,128)} %get-tuple-element.19), channel_id=1, source_target_pairs={{1,0},{2,1},{3,2},{4,3},{5,4},{6,5},{7,6},{0,7},{9,8},{10,9},{11,1... | collective-permute-start | bytes 1966088 | tf_op jit(solution)/shard_map/ppermute | solution.py:24
  899.2 187.4 %collective-permute-start.1 = (f32[5,256,1,128]{1,3,2,0:T(8,128)}, f32[5,256,1,128]{1,3,2,0:T(8,128)S(1)}, u32[]{:S(2)}, u32[]{:S(2)}) collective-permute-start(f32[5,256,1,128]{1,3,2,0:T(8,128)} %get-tuple-element.20), channel_id=1, source_target_pairs={{0,1},{1,2},{2,3},{3,4},{4,5},{5,6},{6,7},{7,0},{8,9},{9,10},{10,1... | collective-permute-start | bytes 1966088 | tf_op jit(solution)/shard_map/ppermute | solution.py:22
  900.1 89.8 %collective-permute-start.2 = (f32[5,256,32,1]{1,3,2,0:T(1,128)}, f32[5,256,32,1]{1,3,2,0:T(1,128)S(1)}, u32[]{:S(2)}, u32[]{:S(2)}) collective-permute-start(f32[5,256,32,1]{1,3,2,0:T(1,128)} %get-tuple-element.17), channel_id=1, source_target_pairs={{0,24},{8,0},{16,8},{24,16},{1,25},{9,1},{17,9},{25,17},{2,26},{10... | collective-permute-start | bytes 491528 | tf_op jit(solution)/shard_map/ppermute | solution.py:33
  900.1 89.8 %collective-permute-start.3 = (f32[5,256,32,1]{1,3,2,0:T(1,128)}, f32[5,256,32,1]{1,3,2,0:T(1,128)}, u32[]{:S(2)}, u32[]{:S(2)}) collective-permute-start(f32[5,256,32,1]{1,3,2,0:T(1,128)} %get-tuple-element.18), channel_id=1, source_target_pairs={{0,8},{8,16},{16,24},{24,0},{1,9},{9,17},{17,25},{25,1},{2,10},{10... | collective-permute-start | bytes 491528 | tf_op jit(solution)/shard_map/ppermute | solution.py:33
  909.1 32.2 %copy-start.1 = (f32[5,256,32,128]{1,3,2,0:T(8,128)S(1)}, f32[5,256,32,128]{1,3,2,0:T(8,128)}, u32[]{:S(2)}) copy-start(f32[5,256,32,128]{1,3,2,0:T(8,128)} %pad_maximum_fusion) | copy-start | bytes 62914564
  990.0 135.9 %copy-start.13 = (f32[5,256,32,1]{1,3,2,0:T(1,128)}, f32[5,256,32,1]{1,3,2,0:T(1,128)S(1)}, u32[]{:S(2)}) copy-start(f32[5,256,32,1]{1,3,2,0:T(1,128)S(1)} %collective-permute-done.2) | copy-start | bytes 491524
  1082.6 23.6 %copy-start.9 = (f32[5,256,1,128]{1,3,2,0:T(8,128)}, f32[5,256,1,128]{1,3,2,0:T(8,128)S(1)}, u32[]{:S(2)}) copy-start(f32[5,256,1,128]{1,3,2,0:T(8,128)S(1)} %collective-permute-done) | copy-start | bytes 1966084
  1086.5 19.7 copy-start.11
  1106.3 16.1 copy-start.3
  1106.3 18.9 collective-permute-start.4
  1106.4 18.9 collective-permute-start.5
  1111.1 14.1 collective-permute-start.6
  1111.2 14.0 collective-permute-start.7
  1117.0 8.9 slice-start
  1117.0 8.9 slice-start.1
  1122.3 3.6 slice-start.2
  1125.2 0.7 copy-start.17
  1125.2 0.7 copy-start.18
  1125.2 0.7 copy-start.14
  1161.2 70.5 %collective-permute-start.8 = (f32[1,256,1,128]{1,3,2,0:T(8,128)S(1)}, f32[1,256,1,128]{1,3,2,0:T(8,128)S(1)}, u32[]{:S(2)}, u32[]{:S(2)}) collective-permute-start(f32[1,256,1,128]{1,3,2,0:T(8,128)S(1)} %get-tuple-element.34), channel_id=1, source_target_pairs={{0,1},{1,2},{2,3},{3,4},{4,5},{5,6},{6,7},{7,0},{8,9},{9,10},{10,1... | collective-permute-start | bytes 393224 | tf_op jit(solution)/shard_map/ppermute | solution.py:22
  1214.5 17.2 collective-permute-start.9
  1215.6 16.1 collective-permute-start.10
  1215.6 16.1 collective-permute-start.11
  1217.4 8.1 copy-start.2
  1229.6 2.8 copy-start.10
  1229.6 2.8 copy-start.12
  1231.7 0.6 copy-start.15
  1231.7 0.6 copy-start.16
  1280.9 16.8 copy-start.7
  1880.6 0.9 copy-start.8
  1884.3 23.9 %all-to-all-start.4 = ((f32[8,1,6144]{2,1,0:T(1,128)}), f32[8,1,6144]{2,1,0:T(1,128)S(1)}, u32[]{:S(2)}, u32[]{:S(2)}) async-start(f32[8,1,6144]{2,1,0:T(1,128)} %reshape.140), calls=%async_computation.4 | async-start | bytes 393216 | tf_op jit(solution)/shard_map/all_to_all | solution.py:127
  1912.7 8.7 all-to-all-start.5
  1938.7 28.7 %all-to-all-start.7 = ((f32[8,1,6144]{2,1,0:T(1,128)}), f32[8,1,6144]{2,1,0:T(1,128)S(1)}, u32[]{:S(2)}, u32[]{:S(2)}) async-start(f32[8,1,6144]{2,1,0:T(1,128)} %reshape.146), calls=%async_computation.7 | async-start | bytes 393216 | tf_op jit(solution)/shard_map/all_to_all | solution.py:138
where the time goes:
time: 2040 us; the launch traced here: 2030 us
  local copies, waits for them, and re-layouts  769 us (38%)
  waiting for transfers between devices  379 us (19%)
  blocking collectives  298 us (15%)
  other arithmetic  262 us (13%)
  matrix products  217 us (11%)
  starting transfers between devices  102 us (5%)
    reshape x1, local copies, waits for them, and re-layouts, per_device(): hessian.reshape(3, xlen // 4, 4, ylen // 4, 4, zlen // 4, 4)  418 us
    all_to_all x1, waiting for transfers between devices, fine_filter(): lax.all_to_all(lax.all_to_all(coeffs, 'gz', split_axis=1, concat_axis=3,...  270 us
    all_to_all x1, blocking collectives, fine_filter(): lax.all_to_all(pencil, 'gz', split_axis=3, concat_axis=1, tiled=True)  147 us
    all_to_all x1, blocking collectives, fine_filter(): lax.all_to_all(coeffs, 'gz', split_axis=1, concat_axis=3, tiled=True)  143 us
    reduce_sum x1, other arithmetic, per_device(): jnp.mean(hessian.reshape(3, xlen // 4, 4, ylen // 4, 4, zlen // 4, 4), ax...  120 us
    dot_general x2, matrix products, fine_filter(): pencil = jnp.einsum('zk,cxyk->cxyz', table_z, pencil, precision=high)  101 us
    ppermute x3, waiting for transfers between devices, extended(): lax.ppermute(head, axis, [((i + 1) % count, i) for i in range(count)])  92.6 us
    dot_general x2, matrix products, fine_filter(): pencil = jnp.einsum('yj,cxjk->cxyk', table_y, pencil, precision=high)  53.5 us
  transfers between devices with their start and end apart: 17, of which 5 were waited for; matrix products, arithmetic and copies ran while one was open for 14% of the time, Pallas kernels for 0%

commit v1 on v0

v1 whole, which is shorter than its diff:
```python
import functools
import math

import jax
import jax.numpy as jnp
from jax import lax
from jax.experimental import pallas as pl
from jax.experimental.pallas import tpu as pltpu
from jax.sharding import PartitionSpec as P

STEP = 0.5
BETA = 0.02
GAMMA = 0.05
COARSE_BETA = 0.025
OMEGA = 1.0 / (0.05 + 42.0 * 0.02)
HIGH = lax.Precision.HIGHEST

PART = 32
GROUP = 4
LANES = 128
TOP = 8
PAIR = 2


def shifted(value, axis, by):
    peers = lax.axis_size(axis)
    return lax.ppermute(value, axis, [(i, (i + by) % peers) for i in range(peers)])


def cas_table(count):
    index = jnp.arange(count, dtype=jnp.int32)
    product = index[:, None] * index[None, :] % count
    angle = product.astype(jnp.float32) * (2.0 * math.pi / count)
    return jnp.cos(angle) + jnp.sin(angle)


def eigen_line(count):
    index = jnp.arange(count, dtype=jnp.int32).astype(jnp.float32)
    return 2.0 - 2.0 * jnp.cos(index * (2.0 * math.pi / count))


def lane_of(rows):
    return lax.broadcasted_iota(jnp.int32, (rows, LANES), 1)


def turn(value, by):
    return pltpu.roll(value, by % LANES if isinstance(by, int) else by, 1)


def turned_to(value, place):
    return pltpu.roll(value, lax.rem(place, LANES), 1)


def turned_from(value, place):
    return pltpu.roll(value, lax.rem(LANES - lax.rem(place, LANES), LANES), 1)


def z_sides(value, rim, lane):
    before = turn(jnp.where(lane == LANES - 1, rim, value), 1)
    after = turn(jnp.where(lane == 0, rim, value), -1)
    return before, after


def planes_loop(count, body, carry=0, step=PAIR):
    def several(k, carry):
        for j in range(step):
            carry = body(k * step + j, carry)
        return carry

    return lax.fori_loop(0, count // step, several, carry)


def call(body, grid, in_specs, out_specs, out_shape, scratch, flops, moved):
    return pl.pallas_call(
        body,
        grid=grid,
        in_specs=in_specs,
        out_specs=out_specs,
        out_shape=out_shape,
        scratch_shapes=scratch,
        cost_estimate=pl.CostEstimate(flops=flops, bytes_accessed=moved, transcendentals=0),
        compiler_params=pltpu.CompilerParams(
            vmem_limit_bytes=48 * 1024 * 1024,
            dimension_semantics=("arbitrary",) * len(grid),
        ),
    )


def f32(*shape):
    return jax.ShapeDtypeStruct(shape, jnp.float32)


def state_rims_body(first, second, packed, low0, low1, high0, high1):
    rows = first.shape[1]
    lane = lane_of(rows)
    owner = lane // GROUP
    spot = lane % GROUP

    def plane(i, edge):
        a = first[i].astype(jnp.float32)
        b = second[i].astype(jnp.float32)
        low0[pl.ds(i, 1), :] = a[:1]
        low1[pl.ds(i, 1), :] = b[:1]
        high0[pl.ds(i, 1), :] = a[rows - 1 :]
        high1[pl.ds(i, 1), :] = b[rows - 1 :]
        both = jnp.where(spot < 2, turned_to(a, GROUP * i + 1), turned_to(b, GROUP * i + 3))
        return jnp.where(owner == i, both, edge)

    packed[...] = planes_loop(PART, plane, jnp.zeros((rows, LANES), jnp.float32))


def state_rims(first, second):
    xlen, rows = first.shape[0], first.shape[1]
    block = pl.BlockSpec((PART, rows, LANES), lambda i: (i, 0, 0))
    slab = pl.BlockSpec((PART, LANES), lambda i: (i, 0))
    return call(
        state_rims_body,
        (xlen // PART,),
        [block, block],
        [pl.BlockSpec((rows, LANES), lambda i: (0, i))] + [slab] * 4,
        [f32(rows, GROUP * xlen)] + [f32(xlen, LANES)] * 4,
        [],
        8 * first.size,
        4 * first.size,
    )(first, second)


def stencil_body(before, cells, after, out, packed, padded, inner):
    rows = cells.shape[2]
    lane = lane_of(rows)
    owner = lane // GROUP
    here = pl.ds(TOP, rows)

    @pl.when((pl.program_id(0) == 0) & (pl.program_id(1) == 0))
    def _():
        padded[...] = jnp.zeros_like(padded)

    for j in range(2):
        padded[j, here] = before[0, j]
        padded[PART + 2 + j, here] = after[0, j]

    def fill(i, carry):
        padded[i + 2, here] = cells[0, i]
        return carry

    planes_loop(PART, fill)

    def middle(j):
        value = padded[j, here]
        near = turn(jnp.where(lane == LANES - 1, 0.0, value), 1) + turn(
            jnp.where(lane == 0, 0.0, value), -1
        )
        core = near - 6.0 * value
        around = (
            padded[j - 1, here]
            + padded[j + 1, here]
            + padded[j, TOP - 1 : TOP - 1 + rows]
            + padded[j, TOP + 1 : TOP + 1 + rows]
        )
        inner[j - 1, here] = core + 0.5 * around
        inner[j - 1, TOP - 1 : TOP] = 0.5 * value[:1]
        inner[j - 1, TOP + rows : TOP + rows + 1] = 0.5 * value[rows - 1 :]
        return value, core

    middle(1)
    middle(PART + 2)

    def plane(i, edge):
        value, core = middle(i + 2)
        far = turn(jnp.where(lane >= LANES - 2, 0.0, value), 2) + turn(
            jnp.where(lane < 2, 0.0, value), -2
        )
        out[0, i] = BETA * far - (12.0 * BETA) * core + (GAMMA - 34.0 * BETA) * value
        return jnp.where(owner == i, turned_to(value, GROUP * i + 2), edge)

    packed[0] = planes_loop(PART, plane, jnp.zeros((rows, LANES), jnp.float32))

    def finish(i, carry):
        around = (
            inner[i, here]
            + inner[i + 2, here]
            + inner[i + 1, TOP - 1 : TOP - 1 + rows]
            + inner[i + 1, TOP + 1 : TOP + 1 + rows]
        )
        out[0, i] = out[0, i] + (2.0 * BETA) * around
        return carry

    planes_loop(PART, finish)


def stencil(increment):
    parts, xlen, rows = increment.shape[:3]
    half = PART // 2
    pairs = xlen // 2
    block = pl.BlockSpec((1, PART, rows, LANES), lambda c, i: (c, i, 0, 0))
    return call(
        stencil_body,
        (parts, xlen // PART),
        [
            pl.BlockSpec(
                (1, 2, rows, LANES), lambda c, i: (c, lax.rem(half * i + pairs - 1, pairs), 0, 0)
            ),
            block,
            pl.BlockSpec(
                (1, 2, rows, LANES), lambda c, i: (c, lax.rem(half * i + half, pairs), 0, 0)
            ),
        ],
        [block, pl.BlockSpec((1, rows, LANES), lambda c, i: (c, 0, i))],
        [f32(parts, xlen, rows, LANES), f32(parts, rows, GROUP * xlen)],
        [
            pltpu.VMEM((PART + 4, rows + 2 * TOP, LANES), jnp.float32),
            pltpu.VMEM((PART + 2, rows + 2 * TOP, LANES), jnp.float32),
        ],
        24 * increment.size,
        8 * increment.size,
    )(increment, increment, increment)


def gradient(ref, before, after, i, low, high, rim, buffer, lane):
    rows = ref.shape[1]
    value = ref[i].astype(jnp.float32)
    buffer[TOP : TOP + rows] = value
    buffer[TOP - 1 : TOP] = low[pl.ds(i, 1), :]
    buffer[TOP + rows : TOP + rows + 1] = high[pl.ds(i, 1), :]
    prev = jnp.where(i == 0, before[0], ref[jnp.maximum(i - 1, 0)]).astype(jnp.float32)
    later = jnp.where(i == PART - 1, after[0], ref[jnp.minimum(i + 1, PART - 1)]).astype(
        jnp.float32
    )
    left, right = z_sides(value, rim, lane)
    return (
        later - prev,
        buffer[TOP + 1 : TOP + 1 + rows] - buffer[TOP - 1 : TOP - 1 + rows],
        right - left,
    )


def merged_rims(left, right, rows):
    spot = lane_of(rows) % GROUP
    return jnp.where(spot % 2 == 0, left[...], right[...])


def first_state_body(
    increment, m0, m0b, m0a, m1, m1b, m1a, low0, low1, high0, high1, left, right,
    state, source, packed, low, high, pad0, pad1,
):
    rows = m0.shape[1]
    lane = lane_of(rows)
    owner = lane // GROUP
    rims = merged_rims(left, right, rows)

    def plane(i, edge):
        g0 = gradient(
            m0, m0b, m0a, i, low0, high0, turned_from(rims, GROUP * i + 1), pad0.at[i % PAIR], lane
        )
        g1 = gradient(
            m1, m1b, m1a, i, low1, high1, turned_from(rims, GROUP * i + 3), pad1.at[i % PAIR], lane
        )
        u = [increment[d, i] for d in range(3)]
        one = (-0.5 * STEP) * (u[0] * g0[0] + u[1] * g0[1] + u[2] * g0[2])
        state[i] = one
        source[i] = (0.5 * STEP) * (u[0] * g1[0] + u[1] * g1[1] + u[2] * g1[2])
        low[pl.ds(i, 1), :] = one[:1]
        high[pl.ds(i, 1), :] = one[rows - 1 :]
        return jnp.where(owner == i, turned_to(one, GROUP * i + 1), edge)

    packed[...] = planes_loop(PART, plane, jnp.zeros((rows, LANES), jnp.float32))


def around_specs(xlen, rows):
    return [
        pl.BlockSpec((PART, rows, LANES), lambda i: (i, 0, 0)),
        pl.BlockSpec((1, rows, LANES), lambda i: (lax.rem(PART * i + xlen - 1, xlen), 0, 0)),
        pl.BlockSpec((1, rows, LANES), lambda i: (lax.rem(PART * i + PART, xlen), 0, 0)),
    ]


def first_state(increment, first, second, slabs, left, right):
    xlen, rows = first.shape[0], first.shape[1]
    triple = pl.BlockSpec((3, PART, rows, LANES), lambda i: (0, i, 0, 0))
    block = pl.BlockSpec((PART, rows, LANES), lambda i: (i, 0, 0))
    slab = pl.BlockSpec((PART, LANES), lambda i: (i, 0))
    rim = pl.BlockSpec((rows, LANES), lambda i: (0, i))
    return call(
        first_state_body,
        (xlen // PART,),
        [triple] + around_specs(xlen, rows) * 2 + [slab] * 4 + [rim, rim],
        [block, block, rim, slab, slab],
        [f32(xlen, rows, LANES)] * 2 + [f32(rows, GROUP * xlen)] + [f32(xlen, LANES)] * 2,
        [pltpu.VMEM((PAIR, rows + 2 * TOP, LANES), jnp.float32)] * 2,
        24 * first.size,
        24 * first.size,
    )(increment, first, first, first, second, second, second, *slabs, left, right)


def second_state_body(
    velocity, source, state, state_b, state_a, low, high, left, right,
    adjoint, packed, out_low, out_high, pad,
):
    rows = state.shape[1]
    lane = lane_of(rows)
    owner = lane // GROUP
    rims = merged_rims(left, right, rows)

    def plane(i, edge):
        value = state[i]
        buffer = pad.at[i % PAIR]
        buffer[TOP : TOP + rows] = value
        buffer[TOP - 1 : TOP] = low[pl.ds(i, 1), :]
        buffer[TOP + rows : TOP + rows + 1] = high[pl.ds(i, 1), :]
        prev = jnp.where(i == 0, state_b[0], state[jnp.maximum(i - 1, 0)])
        later = jnp.where(i == PART - 1, state_a[0], state[jnp.minimum(i + 1, PART - 1)])
        sides = [
            (prev, later),
            (buffer[TOP - 1 : TOP - 1 + rows], buffer[TOP + 1 : TOP + 1 + rows]),
            z_sides(value, turned_from(rims, GROUP * i + 1), lane),
        ]
        total = source[i] - value
        for d in range(3):
            speed = velocity[d, i]
            slope = jnp.where(speed > 0.0, value - sides[d][0], sides[d][1] - value)
            total = total + (STEP * speed) * slope
        adjoint[i] = total
        along = velocity[1, i]
        out_low[pl.ds(i, 1), :] = jnp.maximum(along[:1], 0.0) * total[:1]
        out_high[pl.ds(i, 1), :] = jnp.minimum(along[rows - 1 :], 0.0) * total[rows - 1 :]
        along = velocity[2, i]
        across = total * jnp.where(
            lane == LANES - 1, jnp.minimum(along, 0.0), jnp.maximum(along, 0.0)
        )
        return jnp.where(owner == i, turned_to(across, GROUP * i + 1), edge)

    packed[...] = planes_loop(PART, plane, jnp.zeros((rows, LANES), jnp.float32))


def second_state(velocity, source, state, low, high, left, right):
    xlen, rows = state.shape[0], state.shape[1]
    triple = pl.BlockSpec((3, PART, rows, LANES), lambda i: (0, i, 0, 0))
    block = pl.BlockSpec((PART, rows, LANES), lambda i: (i, 0, 0))
    slab = pl.BlockSpec((PART, LANES), lambda i: (i, 0))
    rim = pl.BlockSpec((rows, LANES), lambda i: (0, i))
    return call(
        second_state_body,
        (xlen // PART,),
        [triple, block] + around_specs(xlen, rows) + [slab, slab, rim, rim],
        [block, rim, slab, slab],
        [f32(xlen, rows, LANES), f32(rows, GROUP * xlen)] + [f32(xlen, LANES)] * 2,
        [pltpu.VMEM((PAIR, rows + 2 * TOP, LANES), jnp.float32)],
        30 * state.size,
        24 * state.size,
    )(velocity, source, state, state, state, low, high, left, right)


def hessian_body(
    filtered, velocity, speed_b, speed_a, adjoint, adjoint_b, adjoint_a,
    m0, m0b, m0a, m1, m1b, m1a, low0, low1, high0, high1, left, right,
    flow_low, flow_high, flow_left, flow_right, edge_low, edge_high, edge_lanes, fold_y, fold_z,
    out, restricted, pad0, pad1, pad2, pad3, sums,
):
    rows = m0.shape[1]
    lane = lane_of(rows)
    rims = merged_rims(left, right, rows)
    flows = merged_rims(flow_left, flow_right, rows)
    outer = (lane < 2) | (lane >= LANES - 2)

    def plane(i, carry):
        slot = i % PAIR
        g0 = gradient(
            m0, m0b, m0a, i, low0, high0, turned_from(rims, GROUP * i + 1), pad0.at[slot], lane
        )
        g1 = gradient(
            m1, m1b, m1a, i, low1, high1, turned_from(rims, GROUP * i + 3), pad1.at[slot], lane
        )
        value = adjoint[i]
        sx, sy, sz = (velocity[d, i] for d in range(3))
        kept = jnp.abs(sx) + jnp.abs(sy) + jnp.abs(sz)
        before, after = jnp.maximum(i - 1, 0), jnp.minimum(i + 1, PART - 1)
        prev = jnp.where(
            i == 0,
            jnp.minimum(speed_b[0, 0], 0.0) * adjoint_b[0],
            jnp.minimum(velocity[0, before], 0.0) * adjoint[before],
        )
        later = jnp.where(
            i == PART - 1,
            jnp.maximum(speed_a[0, 0], 0.0) * adjoint_a[0],
            jnp.maximum(velocity[0, after], 0.0) * adjoint[after],
        )
        change = later - prev
        inflow = pad2.at[slot]
        outflow = pad3.at[slot]
        inflow[TOP : TOP + rows] = jnp.minimum(sy, 0.0) * value
        inflow[TOP - 1 : TOP] = flow_low[pl.ds(i, 1), :]
        outflow[TOP : TOP + rows] = jnp.maximum(sy, 0.0) * value
        outflow[TOP + rows : TOP + rows + 1] = flow_high[pl.ds(i, 1), :]
        change = change + (
            outflow[TOP + 1 : TOP + 1 + rows] - inflow[TOP - 1 : TOP - 1 + rows]
        )
        rim = turned_from(flows, GROUP * i + 1)
        change = change + turn(
            jnp.where(lane == 0, rim, jnp.maximum(sz, 0.0) * value), -1
        )
        change = change - turn(
            jnp.where(lane == LANES - 1, rim, jnp.minimum(sz, 0.0) * value), 1
        )
        half_two = (0.5 * STEP) * value
        half_one = half_two + (0.5 * STEP * STEP) * (change - kept * value)
        for d in range(3):
            cyclic = turned_from(edge_lanes[d], GROUP * i + 2)
            out[d, i] = (
                filtered[d, i]
                + jnp.where(outer, cyclic, 0.0)
                + half_one * g0[d]
                + half_two * g1[d]
            )
            out[d, i, 0:2] = out[d, i, 0:2] + edge_low[d, pl.ds(2 * i, 2), :]
            out[d, i, rows - 2 : rows] = out[d, i, rows - 2 : rows] + edge_high[d, pl.ds(2 * i, 2), :]
        return carry

    planes_loop(PART, plane)

    for d in range(3):

        def fold(k, carry):
            sums[k] = (out[d, 4 * k] + out[d, 4 * k + 1]) + (out[d, 4 * k + 2] + out[d, 4 * k + 3])
            return carry

        lax.fori_loop(0, PART // 4, fold, 0)
        block = sums[...].reshape(PART // 4 * rows, LANES)
        block = jnp.dot(block, fold_z[...], precision=HIGH, preferred_element_type=jnp.float32)
        block = jnp.dot(fold_y[...], block, precision=HIGH, preferred_element_type=jnp.float32)
        restricted[d] = block * (1.0 / 64.0)


def hessian_pass(
    filtered, velocity, adjoint, first, second, slabs, left, right, flow_low, flow_high, flow_left,
    flow_right, edge_low, edge_high, edge_lanes, fold_y, fold_z,
):
    xlen, rows = first.shape[0], first.shape[1]
    triple = pl.BlockSpec((3, PART, rows, LANES), lambda i: (0, i, 0, 0))
    slab = pl.BlockSpec((PART, LANES), lambda i: (i, 0))
    rim = pl.BlockSpec((rows, LANES), lambda i: (0, i))
    rows_two = pl.BlockSpec((3, 2 * PART, LANES), lambda i: (0, i, 0))
    whole = lambda a: pl.BlockSpec(a.shape, lambda i: (0, 0))
    coarse_rows = PART // 4 * (rows // 4)
    around = around_specs(xlen, rows)
    pad = pltpu.VMEM((PAIR, rows + 2 * TOP, LANES), jnp.float32)
    return call(
        hessian_body,
        (xlen // PART,),
        [
            triple,
            triple,
            pl.BlockSpec(
                (1, 1, rows, LANES), lambda i: (0, lax.rem(PART * i + xlen - 1, xlen), 0, 0)
            ),
            pl.BlockSpec((1, 1, rows, LANES), lambda i: (0, lax.rem(PART * i + PART, xlen), 0, 0)),
        ]
        + around * 3
        + [slab] * 4
        + [rim, rim, slab, slab, rim, rim, rows_two, rows_two]
        + [pl.BlockSpec((3, rows, LANES), lambda i: (0, 0, i)), whole(fold_y), whole(fold_z)],
        [triple, pl.BlockSpec((3, coarse_rows, LANES // 4), lambda i: (0, i, 0))],
        [f32(3, xlen, rows, LANES), f32(3, xlen // 4 * (rows // 4), LANES // 4)],
        [pad, pad, pad, pad, pltpu.VMEM((PART // 4, rows, LANES), jnp.float32)],
        90 * first.size,
        48 * first.size,
    )(
        filtered, velocity, velocity, velocity, adjoint, adjoint, adjoint,
        first, first, first, second, second, second, *slabs, left, right,
        flow_low, flow_high, flow_left, flow_right, edge_low, edge_high, edge_lanes, fold_y, fold_z,
    )


def final_body(hessian, coarse, spread_y, spread_z, out, wide):
    rows = hessian.shape[2]
    block = jnp.dot(spread_y[...], coarse[0], precision=HIGH, preferred_element_type=jnp.float32)
    block = jnp.dot(block, spread_z[...], precision=HIGH, preferred_element_type=jnp.float32)
    wide[...] = block.reshape(PART // 4, rows, LANES)

    def fold(k, carry):
        add = wide[k]
        for j in range(4):
            out[0, 4 * k + j] = OMEGA * hessian[0, 4 * k + j] + add
        return carry

    lax.fori_loop(0, PART // 4, fold, 0)


def final_pass(hessian, coarse, spread_y, spread_z):
    parts, xlen, rows = hessian.shape[:3]
    block = pl.BlockSpec((1, PART, rows, LANES), lambda c, i: (c, i, 0, 0))
    coarse_rows = PART // 4 * (rows // 4)
    whole = lambda a: pl.BlockSpec(a.shape, lambda c, i: (0, 0))
    return call(
        final_body,
        (parts, xlen // PART),
        [
            block,
            pl.BlockSpec((1, coarse_rows, LANES // 4), lambda c, i: (c, i, 0)),
            whole(spread_y),
            whole(spread_z),
        ],
        block,
        f32(parts, xlen, rows, LANES),
        [pltpu.VMEM((PART // 4, rows, LANES), jnp.float32)],
        2 * hessian.size,
        8 * hessian.size,
    )(hessian, coarse, spread_y, spread_z)


def coarse_spread(restricted):
    both = ("gz", "gy")
    groups_z = lax.axis_size("gz")
    groups_y = lax.axis_size("gy")
    devices = groups_z * groups_y
    cxlen, cylen, czlen = (restricted.shape[1], restricted.shape[2], restricted.shape[3])
    full_y = groups_y * cylen
    full_z = groups_z * czlen
    each = -(-3 * cxlen // devices)
    table_x = cas_table(cxlen)
    table_y = cas_table(full_y)
    table_z = cas_table(full_z)
    coeffs = jnp.einsum("xi,cijk->cxjk", table_x, restricted, precision=HIGH)
    coeffs = coeffs.reshape(3 * cxlen, cylen, czlen)
    coeffs = jnp.pad(coeffs, ((0, each * devices - 3 * cxlen), (0, 0), (0, 0)))
    planes = lax.all_to_all(coeffs, both, 0, 0, tiled=True)
    planes = planes.reshape(groups_z, groups_y, each, cylen, czlen)
    planes = planes.transpose(2, 1, 3, 0, 4).reshape(each, full_y, full_z)
    planes = jnp.einsum("yj,pjk->pyk", table_y, planes, precision=HIGH)
    planes = jnp.einsum("zk,pyk->pyz", table_z, planes, precision=HIGH)
    line_x = jnp.tile(eigen_line(cxlen), -(-each * devices // cxlen))
    line_x = lax.dynamic_slice_in_dim(line_x, lax.axis_index(both) * each, each, 0)
    total = (
        line_x[:, None, None] + eigen_line(full_y)[None, :, None] + eigen_line(full_z)[None, None, :]
    )
    planes = planes / (GAMMA + COARSE_BETA * total * total)
    planes = jnp.einsum("zk,pyk->pyz", table_z, planes, precision=HIGH)
    planes = jnp.einsum("yj,pjk->pyk", table_y, planes, precision=HIGH)
    planes = planes.reshape(each, groups_y, cylen, groups_z, czlen).transpose(3, 1, 0, 2, 4)
    planes = planes.reshape(devices * each, cylen, czlen)
    coeffs = lax.all_to_all(planes, both, 0, 0, tiled=True)[: 3 * cxlen]
    coeffs = coeffs.reshape(3, cxlen, cylen, czlen)
    coeffs = jnp.einsum("xi,cijk->cxjk", table_x, coeffs, precision=HIGH)
    return coeffs / float(cxlen * full_y * full_z)


def slab_curve(row, inward, left, right):
    lane = lax.broadcasted_iota(jnp.int32, row.shape, 2)
    before = jnp.where(lane == 0, left[:, :, None], jnp.roll(row, 1, 2))
    after = jnp.where(lane == LANES - 1, right[:, :, None], jnp.roll(row, -1, 2))
    near = jnp.roll(row, 1, 1) + jnp.roll(row, -1, 1) + before + after
    return inward - 12.0 * row + 2.0 * near


def lane_curve(left, right):
    spot = lax.broadcasted_iota(jnp.int32, left.shape, 2) % GROUP
    rims = jnp.where(spot < 2, left, right)
    rows = rims.shape[1]
    empty = jnp.zeros_like(rims[:, :1])
    up = jnp.concatenate([rims[:, 1:], empty], axis=1)
    down = jnp.concatenate([empty, rims[:, : rows - 1]], axis=1)
    bent = -2.0 * (
        6.0 * rims - jnp.roll(rims, GROUP, 2) - jnp.roll(rims, -GROUP, 2) - up - down
    )
    plain = jnp.where(spot < 2, jnp.roll(rims, -2, 2), jnp.roll(rims, 2, 2))
    curve = jnp.where(spot == 1, jnp.roll(bent, -1, 2), jnp.roll(bent, 1, 2))
    return BETA * (plain + jnp.where((spot == 1) | (spot == 2), curve, 0.0))


def per_device(velocity, increment, template, deformed):
    xlen, rows = template.shape[0], template.shape[1]

    packed, low0, low1, high0, high1 = state_rims(template, deformed)
    left = shifted(packed, "gz", 1)
    right = shifted(packed, "gz", -1)
    below = shifted(jnp.stack([high0, high1]), "gy", 1)
    above = shifted(jnp.stack([low0, low1]), "gy", -1)
    slabs = (below[0], below[1], above[0], above[1])

    filtered, inc_packed = stencil(increment)

    state, source, s_packed, s_low, s_high = first_state(
        increment, template, deformed, slabs, left, right
    )
    s_left = shifted(s_packed, "gz", 1)
    s_right = shifted(s_packed, "gz", -1)
    s_below = shifted(s_high, "gy", 1)
    s_above = shifted(s_low, "gy", -1)

    inc_left = shifted(inc_packed, "gz", 1)
    inc_right = shifted(inc_packed, "gz", -1)
    edge_lanes = lane_curve(inc_left, inc_right)
    from_left = inc_left.reshape(3, rows, xlen, GROUP)
    from_right = inc_right.reshape(3, rows, xlen, GROUP)
    first_row, last_row = increment[:, :, 0], increment[:, :, rows - 1]
    low_curve = slab_curve(first_row, increment[:, :, 1], from_left[:, 0, :, 1], from_right[:, 0, :, 2])
    high_curve = slab_curve(
        last_row, increment[:, :, rows - 2], from_left[:, rows - 1, :, 1], from_right[:, rows - 1, :, 2]
    )
    from_below = shifted(jnp.stack([high_curve, last_row], axis=2), "gy", 1)
    from_above = shifted(jnp.stack([first_row, low_curve], axis=2), "gy", -1)
    edge_low = BETA * from_below.reshape(3, 2 * xlen, LANES)
    edge_high = BETA * from_above.reshape(3, 2 * xlen, LANES)

    adjoint, f_packed, f_low, f_high = second_state(
        velocity, source, state, s_below, s_above, s_left, s_right
    )
    f_left = shifted(f_packed, "gz", 1)
    f_right = shifted(f_packed, "gz", -1)
    f_below = shifted(f_high, "gy", 1)
    f_above = shifted(f_low, "gy", -1)

    coarse_x = PART // 4
    fold_y = jnp.repeat(jnp.eye(coarse_x * (rows // 4), dtype=jnp.float32), 4, axis=1)
    fold_z = jnp.repeat(jnp.eye(LANES // 4, dtype=jnp.float32), 4, axis=0)
    hessian, restricted = hessian_pass(
        filtered, velocity, adjoint, template, deformed, slabs, left, right, f_below, f_above,
        f_left, f_right, edge_low, edge_high, edge_lanes, fold_y, fold_z,
    )
    coarse = coarse_spread(restricted.reshape(3, xlen // 4, rows // 4, LANES // 4))
    mixed = coarse.reshape(restricted.shape) - OMEGA * restricted
    return final_pass(hessian, mixed, fold_y.T, fold_z.T)


def solution(mesh):
    placed = (
        P(None, None, "gy", "gz"),
        P(None, None, "gy", "gz"),
        P(None, "gy", "gz"),
        P(None, "gy", "gz"),
    )
    return jax.shard_map(
        per_device, mesh=mesh, in_specs=placed, out_specs=P(None, None, "gy", "gz"), check_vma=False
    )
```

time: 2040 us -> 350 us (0.17)
  local copies, waits for them, and re-layouts: 769 us -> 40.4 us
  waiting for transfers between devices: 379 us -> 55.7 us
  blocking collectives: 298 us -> 0 us
  other arithmetic: 262 us -> 7 us
  matrix products: 217 us -> 4.99 us
  Pallas kernels: 0 us -> 204 us
  starting transfers between devices: 102 us -> 36.4 us
    reshape x5 -> x6, local copies, waits for them, and re-layouts: 451 us -> 1.22 us  [the longest x2 0.41 us: coarse_spread(): planes.reshape(each, groups_y, cylen, groups_z, czlen)]
    all_to_all x3 -> x0, blocking collectives: 298 us -> none  [the longest x1 147 us: fine_filter(): lax.all_to_all(pencil, 'gz', split_axis=3, concat_axis=1, tiled=True)]
    all_to_all x5 -> x2, waiting for transfers between devices: 283 us -> 16.4 us  [the longest x1 8.23 us: coarse_spread(): coeffs = lax.all_to_all(planes, both, 0, 0, tiled=True)[:3 * cxlen]]
    dot_general x12 -> x6, matrix products: 217 us -> 4.99 us  [the longest x1 1.44 us: coarse_spread(): coeffs = jnp.einsum('xi,cijk->cxjk', table_x, coeffs, precision=HIGH)]
    pallas_call x0 -> x6, Pallas kernels: none -> 204 us  [the longest x1 56.1 us: stencil(): call(stencil_body, (parts, xlen // PART), [pl.BlockSpec((1, 2, rows, LANE...]
    reduce_sum x1 -> x0, other arithmetic: 120 us -> none  [per_device(): jnp.mean(hessian.reshape(3, xlen // 4, 4, ylen // 4, 4, zlen // 4, 4), ax...]
    ppermute x6 -> x0, waiting for transfers between devices: 96.6 us -> none  [the longest x3 92.6 us: extended(): lax.ppermute(head, axis, [((i + 1) % count, i) for i in range(count)])]
    all_to_all x11 -> x1, local copies, waits for them, and re-layouts: 84.1 us -> 0.5 us  [coarse_spread(): planes = lax.all_to_all(coeffs, both, 0, 0, tiled=True)]
  transfers between devices with their start and end apart: 17 -> 18, of which waited for: 5 -> 8; matrix products, arithmetic and copies ran while one was open for 14% -> 12% of each run, Pallas kernels for 0% -> 22%
where the time goes in v1:
time: 350 us; the launch traced here: 349 us
  Pallas kernels  204 us (58%)
  waiting for transfers between devices  55.7 us (16%)
  local copies, waits for them, and re-layouts  40.4 us (12%)
  starting transfers between devices  36.4 us (10%)
  other arithmetic  7 us (2%)
  matrix products  4.99 us (1%)
    pallas_call x1, Pallas kernels, stencil(): call(stencil_body, (parts, xlen // PART), [pl.BlockSpec((1, 2, rows, LANE...  56.1 us
    pallas_call x1, Pallas kernels, hessian_pass(): call(hessian_body, (xlen // PART,), [triple, triple, pl.BlockSpec((1, 1,...  47.3 us
    ppermute x16, waiting for transfers between devices, shifted(): lax.ppermute(value, axis, [(i, (i + by) % peers) for i in range(peers)])  39.2 us
    pallas_call x1, Pallas kernels, first_state(): call(first_state_body, (xlen // PART,), [triple] + around_specs(xlen, row...  32.7 us
    pallas_call x1, Pallas kernels, second_state(): call(second_state_body, (xlen // PART,), [triple, block] + around_specs(x...  32 us
    ppermute x16, starting transfers between devices, shifted(): lax.ppermute(value, axis, [(i, (i + by) % peers) for i in range(peers)])  27.5 us
    pallas_call x1, Pallas kernels, final_pass(): call(final_body, (parts, xlen // PART), [block, pl.BlockSpec((1, coarse_r...  25.1 us
    slice x1, local copies, waits for them, and re-layouts, per_device(): from_right[:, 0, :, 2]  14 us
  transfers between devices with their start and end apart: 18, of which 8 were waited for; matrix products, arithmetic and copies ran while one was open for 12% of the time, Pallas kernels for 22%

profile of v1, /device:TPU:0, one launch (start us, length us, event | category | flops | bytes accessed | tf_op | source)
XLA Modules:
  0.0 349.0 jit_solution(14712250012340071494)
XLA Ops:
  0.0 56.1 %shard_map.46 = (f32[3,256,32,128]{3,2,1,0:T(8,128)}, f32[3,32,1024]{2,1,0:T(8,128)S(1)}) custom-call(f32[3,256,32,128]{3,2,1,0:T(8,128)} %increment.1, f32[3,256,32,128]{3,2,1,0:T(8,128)} %increment.1, f32[3,256,32,128]{3,2,1,0:T(8,128)} %increment.1), custom_call_target="tpu_custom_call" | custom-call | flops 75497472 | bytes 25165824 | tf_op jit(solution)/shard_map/pallas_call | solution.py:196
  56.6 1.9 collective-permute-start.13
  58.5 10.8 %shard_map.47 = (f32[32,1024]{1,0:T(8,128)S(1)}, f32[256,128]{1,0:T(8,128)S(1)}, f32[256,128]{1,0:T(8,128)S(1)}, f32[256,128]{1,0:T(8,128)S(1)}, f32[256,128]{1,0:T(8,128)S(1)}) custom-call(bf16[256,32,128]{2,1,0:T(8,128)(2,1)S(1)} %copy-done, bf16[256,32,128]{2,1,0:T(8,128)(2,1)S(1)} %copy-done.1), custom_call_target="tpu_custom_call" | custom-call | flops 8388608 | bytes 4194304 | tf_op jit(solution)/shard_map/pallas_call | solution.py:116
  69.4 5.4 %collective-permute-start.1 = (f32[2,256,128]{2,1,0:T(8,128)S(1)}, f32[2,256,128]{2,1,0:T(8,128)S(1)}, u32[]{:S(2)}, u32[]{:S(2)}) collective-permute-start(f32[2,256,128]{2,1,0:T(8,128)S(1)} %pad_maximum_fusion.3), channel_id=1, source_target_pairs={{0,7},{1,0},{2,1},{3,2},{4,3},{5,4},{6,5},{7,6},{8,15},{9,8},{10,9... | collective-permute-start | bytes 786440 | tf_op jit(solution)/shard_map/ppermute | solution.py:27
  75.0 7.0 %fusion.72 = (f32[3,256,1,128]{3,2,1,0:T(1,128)}, f32[3,256,1,128]{3,2,1,0:T(1,128)S(1)}, f32[3,256,1,128]{3,2,1,0:T(1,128)S(1)}, f32[3,256,1,128]{3,2,1,0:T(1,128)}) fusion(f32[3,256,32,128]{3,2,1,0:T(8,128)} %increment.1), kind=kLoop, calls=%fused_computation.135 | loop fusion | bytes 3145728 | tf_op jit(solution)/shard_map/slice | solution.py:595
  82.0 1.0 slice_bitcast_fusion.1
  83.0 1.0 slice_bitcast_fusion
  84.0 0.9 slice_bitcast_fusion.4
  85.0 1.0 slice_bitcast_fusion.7
  86.0 1.0 slice_bitcast_fusion.6
  87.0 0.9 slice_bitcast_fusion.10
  87.9 1.8 collective-permute-start.3
  89.8 2.5 collective-permute-done.3.right
  92.2 32.7 %shard_map.48 = (f32[256,32,128]{2,1,0:T(8,128)}, f32[256,32,128]{2,1,0:T(8,128)}, f32[32,1024]{1,0:T(8,128)}, f32[256,128]{1,0:T(8,128)S(1)}, f32[256,128]{1,0:T(8,128)S(1)}) custom-call(f32[3,256,32,128]{3,2,1,0:T(8,128)} %increment.1, bf16[256,32,128]{2,1,0:T(8,128)(2,1)S(1)} %copy-done, bf16[256,32,128]{2,1,0:T(8,128)(2,1)S(1)} %copy-done, ...), custom_call_target="tpu_custom_call" | custom-call | flops 25165824 | bytes 25165824 | tf_op jit(solution)/shard_map/pallas_call | solution.py:283
  124.9 1.7 collective-permute-start.6
  126.9 2.8 collective-permute-done.6.left
  129.6 4.7 %collective-permute-start.5 = (f32[256,128]{1,0:T(8,128)S(1)}, f32[256,128]{1,0:T(8,128)S(1)}, u32[]{:S(2)}, u32[]{:S(2)}) collective-permute-start(f32[256,128]{1,0:T(8,128)S(1)} %get-tuple-element.32), channel_id=1, source_target_pairs={{0,7},{1,0},{2,1},{3,2},{4,3},{5,4},{6,5},{7,6},{8,15},{9,8},{10,9... | collective-permute-start | bytes 393224 | tf_op jit(solution)/shard_map/ppermute | solution.py:27
  134.4 1.2 collective-permute-done.4.low
  135.6 2.0 collective-permute-done.5.high
  137.6 32.0 %shard_map.49 = (f32[256,32,128]{2,1,0:T(8,128)S(1)}, f32[32,1024]{1,0:T(8,128)S(1)}, f32[256,128]{1,0:T(8,128)S(1)}, f32[256,128]{1,0:T(8,128)S(1)}) custom-call(f32[3,256,32,128]{3,2,1,0:T(8,128)} %speed_a.1, f32[256,32,128]{2,1,0:T(8,128)} %get-tuple-element.29.source, f32[256,32,128]{2,1,0:T(8,128)} %get-tuple-element.30.state.state_b.state_a, ...), custom_call_target="tpu_custom_call" | custom-call | flops 31457280 | bytes 25165824 | tf_op jit(solution)/shard_map/pallas_call | solution.py:341
  169.7 1.7 collective-permute-start.11
  171.4 1.2 fusion.4
  173.1 1.0 fusion.74
  174.2 2.7 copy.65
  176.9 2.7 copy.67
  179.6 14.0 %slice_reduce_fusion = (f32[3,256]{1,0:T(4,128)S(1)}, f32[3,256]{1,0:T(4,128)S(1)}, f32[3,256]{1,0:T(4,128)S(1)}, f32[3,256]{1,0:T(4,128)S(1)}) fusion(f32[3,32,256,4]{1,3,2,0:T(4,128)} %bitcast.126, f32[3,32,256,4]{1,3,2,0:T(4,128)} %bitcast.125), kind=kLoop, calls=%fused_computation.23 | loop fusion | bytes 24576 | tf_op jit(solution)/shard_map/slice | solution.py:595
  193.6 2.2 fusion.17
  195.9 4.8 %collective-permute-start.15 = (f32[3,256,2,128]{3,1,0,2:T(8,128)S(1)}, f32[3,256,2,128]{3,1,0,2:T(8,128)S(1)}, u32[]{:S(2)}, u32[]{:S(2)}) collective-permute-start(f32[3,256,2,128]{3,1,0,2:T(8,128)S(1)} %pad_maximum_fusion.1), channel_id=1, source_target_pairs={{0,7},{1,0},{2,1},{3,2},{4,3},{5,4},{6,5},{7,6},{8,15},{9,8},{10,9... | collective-permute-start | bytes 2359304 | tf_op jit(solution)/shard_map/ppermute | solution.py:27
  202.1 29.7 %collective-permute-done.15 = f32[3,256,2,128]{3,1,0,2:T(8,128)S(1)} collective-permute-done((f32[3,256,2,128]{3,1,0,2:T(8,128)S(1)}, f32[3,256,2,128]{3,1,0,2:T(8,128)S(1)}, u32[]{:S(2)}, u32[]{:S(2)}) %collective-permute-start.15) | collective-permute-done | bytes 786464 | tf_op jit(solution)/shard_map/ppermute | solution.py:27
  231.8 4.4 %collective-permute-start.9 = (f32[256,128]{1,0:T(8,128)S(1)}, f32[256,128]{1,0:T(8,128)S(1)}, u32[]{:S(2)}, u32[]{:S(2)}) collective-permute-start(f32[256,128]{1,0:T(8,128)S(1)} %get-tuple-element.36), channel_id=1, source_target_pairs={{0,7},{1,0},{2,1},{3,2},{4,3},{5,4},{6,5},{7,6},{8,15},{9,8},{10,9... | collective-permute-start | bytes 393224 | tf_op jit(solution)/shard_map/ppermute | solution.py:27
  236.4 0.6 copy.74
  237.0 0.6 copy.69
  237.6 1.1 collective-permute-done.9.flow_high
  238.7 47.3 %shard_map.50 = (f32[3,256,32,128]{3,2,1,0:T(8,128)}, f32[3,512,32]{2,1,0:T(8,128)S(1)}) custom-call(f32[3,256,32,128]{3,2,1,0:T(8,128)} %get-tuple-element.23.filtered, f32[3,256,32,128]{3,2,1,0:T(8,128)} %speed_a.1, f32[3,256,32,128]{3,2,1,0:T(8,128)} %speed_a.1, f32[3,256,32,128]{3,2,1,0:T(8,128)} %speed_a.1, f32[256,32,128]{2,1,0:T(8,128)} %copy-done.2, ...), custom_call_target="tpu_custom_call" | custom-call | flops 94371840 | bytes 50331648 | tf_op jit(solution)/shard_map/pallas_call | solution.py:446
  286.1 1.4 convolution_bitcast_fusion
  287.8 1.0 reshape.370
  288.9 5.5 %all-to-all-start = ((f32[32,1,1536]{2,1,0:T(1,128)}), f32[32,1,1536]{2,1,0:T(1,128)S(1)}, u32[]{:S(2)}, u32[]{:S(2)}) async-start(f32[32,1,1536]{2,1,0:T(1,128)} %reshape.370), calls=%async_computation | async-start | bytes 393216 | tf_op jit(solution)/shard_map/all_to_all | solution.py:525
  294.7 8.2 %all-to-all-done = f32[32,1,1536]{2,1,0:T(1,128)S(1)} async-done(((f32[32,1,1536]{2,1,0:T(1,128)}), f32[32,1,1536]{2,1,0:T(1,128)S(1)}, u32[]{:S(2)}, u32[]{:S(2)}) %all-to-all-start) | async-done | bytes 196640 | tf_op jit(solution)/shard_map/all_to_all | solution.py:525
  303.4 1.0 reduce.8
  304.7 0.5 copy.79
  306.1 0.6 convolution_divide_fusion
  306.6 0.6 fusion.26
  308.1 1.0 reshape.372
  309.2 3.3 all-to-all-start.1
  312.5 8.2 %all-to-all-done.1 = f32[32,1,1536]{2,1,0:T(1,128)S(1)} async-done(((f32[32,1,1536]{2,1,0:T(1,128)}), f32[32,1,1536]{2,1,0:T(1,128)S(1)}, u32[]{:S(2)}, u32[]{:S(2)}) %all-to-all-start.1) | async-done | bytes 196640 | tf_op jit(solution)/shard_map/all_to_all | solution.py:540
  320.8 1.0 reduce.9
  322.0 1.4 fusion
  323.9 25.1 %shard_map.51 = f32[3,256,32,128]{3,2,1,0:T(8,128)} custom-call(f32[3,256,32,128]{3,2,1,0:T(8,128)} %get-tuple-element.39.hessian, f32[3,512,32]{2,1,0:T(8,128)S(1)} %bitcast_subtract_fusion.coarse, f32[256,64]{1,0:T(8,128)S(1)} %bitcast.105, f32[32,128]{1,0:T(8,128)S(1)} %bitcast.112), custom_call_target="tpu_custom_call" | custom-call | flops 6291456 | bytes 25165824 | tf_op jit(solution)/shard_map/pallas_call | solution.py:493
  (88 shorter events, 7.1 us)
Async XLA Ops:
  0.0 58.5 %copy-start = (bf16[256,32,128]{2,1,0:T(8,128)(2,1)S(1)}, bf16[256,32,128]{2,1,0:T(8,128)(2,1)}, u32[]{:S(2)}) copy-start(bf16[256,32,128]{2,1,0:T(8,128)(2,1)} %m0a.3) | copy-start | bytes 6291460
  0.0 58.5 %copy-start.1 = (bf16[256,32,128]{2,1,0:T(8,128)(2,1)S(1)}, bf16[256,32,128]{2,1,0:T(8,128)(2,1)}, u32[]{:S(2)}) copy-start(bf16[256,32,128]{2,1,0:T(8,128)(2,1)} %m1a.3) | copy-start | bytes 6291460
  56.1 115.3 %collective-permute-start.12 = (f32[3,32,1024]{2,1,0:T(8,128)S(1)}, f32[3,32,1024]{2,1,0:T(8,128)}, u32[]{:S(2)}, u32[]{:S(2)}) collective-permute-start(f32[3,32,1024]{2,1,0:T(8,128)S(1)} %get-tuple-element.38), channel_id=1, source_target_pairs={{0,8},{8,16},{16,24},{24,0},{1,9},{9,17},{17,25},{25,1},{2,10},{10... | collective-permute-start | bytes 1179656 | tf_op jit(solution)/shard_map/ppermute | solution.py:27
  56.6 114.8 %collective-permute-start.13 = (f32[3,32,1024]{2,1,0:T(8,128)S(1)}, f32[3,32,1024]{2,1,0:T(8,128)}, u32[]{:S(2)}, u32[]{:S(2)}) collective-permute-start(f32[3,32,1024]{2,1,0:T(8,128)S(1)} %get-tuple-element.38), channel_id=1, source_target_pairs={{0,24},{8,0},{16,8},{24,16},{1,25},{9,1},{17,9},{25,17},{2,26},{10... | collective-permute-start | bytes 1179656 | tf_op jit(solution)/shard_map/ppermute | solution.py:27
  69.4 18.5 %collective-permute-start.1 = (f32[2,256,128]{2,1,0:T(8,128)S(1)}, f32[2,256,128]{2,1,0:T(8,128)S(1)}, u32[]{:S(2)}, u32[]{:S(2)}) collective-permute-start(f32[2,256,128]{2,1,0:T(8,128)S(1)} %pad_maximum_fusion.3), channel_id=1, source_target_pairs={{0,7},{1,0},{2,1},{3,2},{4,3},{5,4},{6,5},{7,6},{8,15},{9,8},{10,9... | collective-permute-start | bytes 786440 | tf_op jit(solution)/shard_map/ppermute | solution.py:27
  74.8 14.9 %collective-permute-start = (f32[2,256,128]{2,1,0:T(8,128)S(1)}, f32[2,256,128]{2,1,0:T(8,128)S(1)}, u32[]{:S(2)}, u32[]{:S(2)}) collective-permute-start(f32[2,256,128]{2,1,0:T(8,128)S(1)} %pad_maximum_fusion.2), channel_id=1, source_target_pairs={{0,1},{1,2},{2,3},{3,4},{4,5},{5,6},{6,7},{7,0},{8,9},{9,10},{10,1... | collective-permute-start | bytes 786440 | tf_op jit(solution)/shard_map/ppermute | solution.py:27
  74.9 14.8 %collective-permute-start.2 = (f32[32,1024]{1,0:T(8,128)S(1)}, f32[32,1024]{1,0:T(8,128)S(1)}, u32[]{:S(2)}, u32[]{:S(2)}) collective-permute-start(f32[32,1024]{1,0:T(8,128)S(1)} %get-tuple-element.28), channel_id=1, source_target_pairs={{0,8},{8,16},{16,24},{24,0},{1,9},{9,17},{17,25},{25,1},{2,10},{10... | collective-permute-start | bytes 393224 | tf_op jit(solution)/shard_map/ppermute | solution.py:27
  87.9 4.3 %collective-permute-start.3 = (f32[32,1024]{1,0:T(8,128)S(1)}, f32[32,1024]{1,0:T(8,128)S(1)}, u32[]{:S(2)}, u32[]{:S(2)}) collective-permute-start(f32[32,1024]{1,0:T(8,128)S(1)} %get-tuple-element.28), channel_id=1, source_target_pairs={{0,24},{8,0},{16,8},{24,16},{1,25},{9,1},{17,9},{25,17},{2,26},{10... | collective-permute-start | bytes 393224 | tf_op jit(solution)/shard_map/ppermute | solution.py:27
  124.9 4.7 %collective-permute-start.6 = (f32[32,1024]{1,0:T(8,128)}, f32[32,1024]{1,0:T(8,128)S(1)}, u32[]{:S(2)}, u32[]{:S(2)}) collective-permute-start(f32[32,1024]{1,0:T(8,128)} %get-tuple-element.33), channel_id=1, source_target_pairs={{0,8},{8,16},{16,24},{24,0},{1,9},{9,17},{17,25},{25,1},{2,10},{10... | collective-permute-start | bytes 393224 | tf_op jit(solution)/shard_map/ppermute | solution.py:27
  126.6 7.8 %collective-permute-start.7 = (f32[32,1024]{1,0:T(8,128)}, f32[32,1024]{1,0:T(8,128)S(1)}, u32[]{:S(2)}, u32[]{:S(2)}) collective-permute-start(f32[32,1024]{1,0:T(8,128)} %get-tuple-element.33), channel_id=1, source_target_pairs={{0,24},{8,0},{16,8},{24,16},{1,25},{9,1},{17,9},{25,17},{2,26},{10... | collective-permute-start | bytes 393224 | tf_op jit(solution)/shard_map/ppermute | solution.py:27
  126.9 8.8 %collective-permute-start.4 = (f32[256,128]{1,0:T(8,128)S(1)}, f32[256,128]{1,0:T(8,128)S(1)}, u32[]{:S(2)}, u32[]{:S(2)}) collective-permute-start(f32[256,128]{1,0:T(8,128)S(1)} %get-tuple-element.31), channel_id=1, source_target_pairs={{0,1},{1,2},{2,3},{3,4},{4,5},{5,6},{6,7},{7,0},{8,9},{9,10},{10,1... | collective-permute-start | bytes 393224 | tf_op jit(solution)/shard_map/ppermute | solution.py:27
  129.6 8.0 %collective-permute-start.5 = (f32[256,128]{1,0:T(8,128)S(1)}, f32[256,128]{1,0:T(8,128)S(1)}, u32[]{:S(2)}, u32[]{:S(2)}) collective-permute-start(f32[256,128]{1,0:T(8,128)S(1)} %get-tuple-element.32), channel_id=1, source_target_pairs={{0,7},{1,0},{2,1},{3,2},{4,3},{5,4},{6,5},{7,6},{8,15},{9,8},{10,9... | collective-permute-start | bytes 393224 | tf_op jit(solution)/shard_map/ppermute | solution.py:27
  169.6 4.5 %copy-start.2 = (f32[256,32,128]{2,1,0:T(8,128)}, f32[256,32,128]{2,1,0:T(8,128)S(1)}, u32[]{:S(2)}) copy-start(f32[256,32,128]{2,1,0:T(8,128)S(1)} %get-tuple-element.34.adjoint.adjoint_b.adjoint_a) | copy-start | bytes 12582916
  169.6 68.0 %collective-permute-start.10 = (f32[32,1024]{1,0:T(8,128)S(1)}, f32[32,1024]{1,0:T(8,128)S(1)}, u32[]{:S(2)}, u32[]{:S(2)}) collective-permute-start(f32[32,1024]{1,0:T(8,128)S(1)} %get-tuple-element.37), channel_id=1, source_target_pairs={{0,8},{8,16},{16,24},{24,0},{1,9},{9,17},{17,25},{25,1},{2,10},{10... | collective-permute-start | bytes 393224 | tf_op jit(solution)/shard_map/ppermute | solution.py:27
  169.7 68.0 %collective-permute-start.11 = (f32[32,1024]{1,0:T(8,128)S(1)}, f32[32,1024]{1,0:T(8,128)S(1)}, u32[]{:S(2)}, u32[]{:S(2)}) collective-permute-start(f32[32,1024]{1,0:T(8,128)S(1)} %get-tuple-element.37), channel_id=1, source_target_pairs={{0,24},{8,0},{16,8},{24,16},{1,25},{9,1},{17,9},{25,17},{2,26},{10... | collective-permute-start | bytes 393224 | tf_op jit(solution)/shard_map/ppermute | solution.py:27
  171.4 66.2 %collective-permute-start.8 = (f32[256,128]{1,0:T(8,128)S(1)}, f32[256,128]{1,0:T(8,128)S(1)}, u32[]{:S(2)}, u32[]{:S(2)}) collective-permute-start(f32[256,128]{1,0:T(8,128)S(1)} %get-tuple-element.35), channel_id=1, source_target_pairs={{0,1},{1,2},{2,3},{3,4},{4,5},{5,6},{6,7},{7,0},{8,9},{9,10},{10,1... | collective-permute-start | bytes 393224 | tf_op jit(solution)/shard_map/ppermute | solution.py:27
  176.9 23.7 %copy-start.3 = (f32[3,256,1,128]{3,2,1,0:T(1,128)S(1)}, f32[3,256,1,128]{3,2,1,0:T(1,128)}, u32[]{:S(2)}) copy-start(f32[3,256,1,128]{3,2,1,0:T(1,128)} %get-tuple-element.48) | copy-start | bytes 1179652
  179.6 21.1 %copy-start.4 = (f32[3,256,1,127]{3,1,0,2:T(8,128)S(1)}, f32[3,256,1,127]{3,1,0,2:T(8,128)}, u32[]{:S(2)}) copy-start(f32[3,256,1,127]{3,1,0,2:T(8,128)} %get-tuple-element.71) | copy-start | bytes 1170436
  179.6 21.1 %copy-start.5 = (f32[3,256,1,127]{3,1,0,2:T(8,128)S(1)}, f32[3,256,1,127]{3,1,0,2:T(8,128)}, u32[]{:S(2)}) copy-start(f32[3,256,1,127]{3,1,0,2:T(8,128)} %get-tuple-element.72) | copy-start | bytes 1170436
  179.6 21.1 %copy-start.6 = (f32[3,256,1,1]{3,1,0,2:T(8,128)S(1)}, f32[3,256,1,1]{3,1,0,2:T(8,128)}, u32[]{:S(2)}) copy-start(f32[3,256,1,1]{3,1,0,2:T(8,128)} %get-tuple-element.73) | copy-start | bytes 9220
  179.6 21.1 %copy-start.7 = (f32[3,256,1,1]{3,1,0,2:T(8,128)S(1)}, f32[3,256,1,1]{3,1,0,2:T(8,128)}, u32[]{:S(2)}) copy-start(f32[3,256,1,1]{3,1,0,2:T(8,128)} %get-tuple-element.74) | copy-start | bytes 9220
  179.6 21.1 %copy-start.8 = (f32[3,255,1,128]{3,1,0,2:T(8,128)S(1)}, f32[3,255,1,128]{3,1,0,2:T(8,128)}, u32[]{:S(2)}) copy-start(f32[3,255,1,128]{3,1,0,2:T(8,128)} %get-tuple-element.75) | copy-start | bytes 1175044
  179.6 21.1 %copy-start.9 = (f32[3,255,1,128]{3,1,0,2:T(8,128)S(1)}, f32[3,255,1,128]{3,1,0,2:T(8,128)}, u32[]{:S(2)}) copy-start(f32[3,255,1,128]{3,1,0,2:T(8,128)} %get-tuple-element.76) | copy-start | bytes 1175044
  195.8 6.0 %copy-start.10 = (f32[3,32,1023]{2,1,0:T(8,128)S(1)}, f32[3,32,1023]{2,1,0:T(8,128)}, u32[]{:S(2)}) copy-start(f32[3,32,1023]{2,1,0:T(8,128)} %get-tuple-element.51) | copy-start | bytes 1178500
  195.8 6.0 %copy-start.11 = (f32[3,32,1023]{2,1,0:T(8,128)S(1)}, f32[3,32,1023]{2,1,0:T(8,128)}, u32[]{:S(2)}) copy-start(f32[3,32,1023]{2,1,0:T(8,128)} %get-tuple-element.52) | copy-start | bytes 1178500
  195.9 36.0 %collective-permute-start.15 = (f32[3,256,2,128]{3,1,0,2:T(8,128)S(1)}, f32[3,256,2,128]{3,1,0,2:T(8,128)S(1)}, u32[]{:S(2)}, u32[]{:S(2)}) collective-permute-start(f32[3,256,2,128]{3,1,0,2:T(8,128)S(1)} %pad_maximum_fusion.1), channel_id=1, source_target_pairs={{0,7},{1,0},{2,1},{3,2},{4,3},{5,4},{6,5},{7,6},{8,15},{9,8},{10,9... | collective-permute-start | bytes 2359304 | tf_op jit(solution)/shard_map/ppermute | solution.py:27
  201.2 35.1 %collective-permute-start.14 = (f32[3,256,2,128]{3,1,0,2:T(8,128)S(1)}, f32[3,256,2,128]{3,1,0,2:T(8,128)S(1)}, u32[]{:S(2)}, u32[]{:S(2)}) collective-permute-start(f32[3,256,2,128]{3,1,0,2:T(8,128)S(1)} %pad_maximum_fusion), channel_id=1, source_target_pairs={{0,1},{1,2},{2,3},{3,4},{4,5},{5,6},{6,7},{7,0},{8,9},{9,10},{10,1... | collective-permute-start | bytes 2359304 | tf_op jit(solution)/shard_map/ppermute | solution.py:27
  231.8 6.9 %collective-permute-start.9 = (f32[256,128]{1,0:T(8,128)S(1)}, f32[256,128]{1,0:T(8,128)S(1)}, u32[]{:S(2)}, u32[]{:S(2)}) collective-permute-start(f32[256,128]{1,0:T(8,128)S(1)} %get-tuple-element.36), channel_id=1, source_target_pairs={{0,7},{1,0},{2,1},{3,2},{4,3},{5,4},{6,5},{7,6},{8,15},{9,8},{10,9... | collective-permute-start | bytes 393224 | tf_op jit(solution)/shard_map/ppermute | solution.py:27
  288.9 14.1 %all-to-all-start = ((f32[32,1,1536]{2,1,0:T(1,128)}), f32[32,1,1536]{2,1,0:T(1,128)S(1)}, u32[]{:S(2)}, u32[]{:S(2)}) async-start(f32[32,1,1536]{2,1,0:T(1,128)} %reshape.370), calls=%async_computation | async-start | bytes 393216 | tf_op jit(solution)/shard_map/all_to_all | solution.py:525
  309.2 11.6 %all-to-all-start.1 = ((f32[32,1,1536]{2,1,0:T(1,128)}), f32[32,1,1536]{2,1,0:T(1,128)S(1)}, u32[]{:S(2)}, u32[]{:S(2)}) async-start(f32[32,1,1536]{2,1,0:T(1,128)} %reshape.372), calls=%async_computation.1 | async-start | bytes 393216 | tf_op jit(solution)/shard_map/all_to_all | solution.py:540

commit v2 on v1

v2 whole, which is shorter than its diff:
```python
import functools
import math

import jax
import jax.numpy as jnp
import numpy as np
from jax import lax
from jax.experimental import pallas as pl
from jax.experimental.pallas import tpu as pltpu
from jax.sharding import PartitionSpec as P

STEP = 0.5
BETA = 0.02
GAMMA = 0.05
COARSE_BETA = 0.025
OMEGA = 1.0 / (0.05 + 42.0 * 0.02)
HIGH = lax.Precision.HIGHEST

PART = 32
GROUP = 4
LANES = 128
TOP = 8
RUN = 8
BATCH = 32
LONG = 64
WIDE = 128
LARGE = 1 << 20


def shifted(value, axis, by):
    peers = lax.axis_size(axis)
    return lax.ppermute(value, axis, [(i, (i + by) % peers) for i in range(peers)])


def cas_table(count):
    index = np.arange(count)
    angle = (index[:, None] * index[None, :] % count) * (2.0 * math.pi / count)
    return jnp.asarray(np.cos(angle) + np.sin(angle), jnp.float32)


def eigen_line(count):
    return jnp.asarray(2.0 - 2.0 * np.cos(np.arange(count) * (2.0 * math.pi / count)), jnp.float32)


def lane_of(rows):
    return lax.broadcasted_iota(jnp.int32, (rows, LANES), 1)


def turn(value, by):
    return pltpu.roll(value, by % LANES if isinstance(by, int) else by, 1)


def turned_to(value, place):
    return pltpu.roll(value, lax.rem(place, LANES), 1)


def turned_from(value, place):
    return pltpu.roll(value, lax.rem(LANES - lax.rem(place, LANES), LANES), 1)


def z_sides(value, rim, lane):
    before = turn(jnp.where(lane == LANES - 1, rim, value), 1)
    after = turn(jnp.where(lane == 0, rim, value), -1)
    return before, after


def planes_loop(count, body, carry=0, step=RUN):
    def several(k, carry):
        for j in range(step):
            carry = body(k * step + j, carry)
        return carry

    return lax.fori_loop(0, count // step, several, carry)


def y_sides(value, low, high):
    rows = value.shape[0]
    row = lax.broadcasted_iota(jnp.int32, value.shape, 0)
    before = jnp.where(row == 0, low, pltpu.roll(value, 1, 0))
    after = jnp.where(row == rows - 1, high, pltpu.roll(value, rows - 1, 0))
    return before, after


def halves(value):
    large = value.astype(jnp.bfloat16)
    small = (value - large.astype(jnp.float32)).astype(jnp.bfloat16)
    return jnp.concatenate([large, small], axis=1)


def doubled(table):
    return jnp.asarray(np.concatenate([table, table], axis=0), jnp.bfloat16)


def product(left, right):
    return jnp.dot(left, right, preferred_element_type=jnp.float32)


def call(body, grid, streamed, kept, out_streamed, out_kept, scratch, flops, moved, grant=12, reused=None):
    counts = [len(streamed), len(kept), len(out_streamed), len(out_kept)]

    def kernel(*refs):
        groups = []
        for count in counts:
            groups.append(refs[:count])
            refs = refs[count:]

        def step(*blocks):
            body(*blocks[: counts[0]], *groups[1], *blocks[counts[0] :], *groups[3], *refs)

        pltpu.emit_pipeline(
            step,
            grid=grid,
            in_specs=[spec for _, spec in streamed],
            out_specs=[spec for _, spec in out_streamed],
        )(*groups[0], *groups[2])

    def placed(array):
        return pltpu.with_memory_space_constraint(array, pltpu.HBM) if array.size >= LARGE else array

    far = pl.BlockSpec(memory_space=pl.ANY)
    near = pl.BlockSpec(memory_space=pltpu.VMEM)
    return pl.pallas_call(
        kernel,
        in_specs=[far] * counts[0] + [near] * counts[1],
        out_specs=[far] * counts[2] + [near] * counts[3],
        out_shape=[jax.ShapeDtypeStruct(shape, jnp.float32) for shape, _ in out_streamed]
        + [pltpu.VMEM(shape, jnp.float32) for shape in out_kept],
        scratch_shapes=scratch,
        input_output_aliases={} if reused is None else {counts[0] + reused[0]: counts[2] + reused[1]},
        cost_estimate=pl.CostEstimate(flops=flops, bytes_accessed=moved, transcendentals=0),
        compiler_params=pltpu.CompilerParams(vmem_limit_bytes=grant * 1024 * 1024),
    )(
        *[placed(array) for array, _ in streamed],
        *[pltpu.with_memory_space_constraint(array, pltpu.VMEM) for array in kept],
    )


def state_rims_body(first, second, packed, low, high):
    rows = first.shape[1]
    lane = lane_of(rows)
    owner = lane // GROUP
    spot = lane % GROUP

    def plane(i, edge):
        a = first[i].astype(jnp.float32)
        b = second[i].astype(jnp.float32)
        low[0, pl.ds(i, 1), :] = a[:1]
        low[1, pl.ds(i, 1), :] = b[:1]
        high[0, pl.ds(i, 1), :] = a[rows - 1 :]
        high[1, pl.ds(i, 1), :] = b[rows - 1 :]
        both = jnp.where(spot < 2, turned_to(a, GROUP * i + 1), turned_to(b, GROUP * i + 3))
        return jnp.where(owner == i, both, edge)

    packed[...] = planes_loop(PART, plane, jnp.zeros((rows, LANES), jnp.float32), 16)


def state_rims(first, second):
    xlen, rows = first.shape[0], first.shape[1]
    block = pl.BlockSpec((PART, rows, LANES), lambda i: (i, 0, 0))
    slab = pl.BlockSpec((2, PART, LANES), lambda i: (0, i, 0))
    return call(
        state_rims_body,
        (xlen // PART,),
        [(first, block), (second, block)],
        [],
        [
            ((rows, GROUP * xlen), pl.BlockSpec((rows, LANES), lambda i: (0, i))),
            ((2, xlen, LANES), slab),
            ((2, xlen, LANES), slab),
        ],
        [],
        [],
        8 * first.size,
        4 * first.size,
    )


def stencil_table():
    cell = np.arange(LANES)
    gap = np.abs(cell[:, None] - cell[None, :])
    outer = np.where(gap == 0, 38.0, np.where(gap == 1, -12.0, np.where(gap == 2, 1.0, 0.0)))
    inner = np.where(gap == 0, -12.0, np.where(gap == 1, 2.0, 0.0))
    table = np.concatenate([outer, inner], axis=1)
    return doubled(table)


def stencil_body(
    before, cells, after, table, packed, low, high, low_curve, high_curve, out, padded, inner
):
    rows = cells.shape[2]
    comp = pl.program_id(0)
    base = pl.program_id(1) * LONG
    owner = lane_of(rows) // GROUP
    here = pl.ds(TOP, rows)

    @pl.when((comp == 0) & (base == 0))
    def _():
        padded[...] = jnp.zeros_like(padded)

    for j in range(2):
        padded[j, here] = before[0, j]
        padded[LONG + 2 + j, here] = after[0, j]

    def fill(i, carry):
        padded[i + 2, here] = cells[0, i]
        return carry

    planes_loop(LONG, fill)

    def middle(j, count):
        flat = padded[pl.ds(j, count), here].reshape(count * rows, LANES)
        both = product(halves(flat), table[...])
        found = []
        for k in range(count):
            value = padded[j + k, here]
            part = both[k * rows : (k + 1) * rows]
            along = padded[j + k - 1, here] + padded[j + k + 1, here]
            core = (
                part[:, LANES:]
                + along
                + (padded[j + k, pl.ds(TOP - 1, rows)] + padded[j + k, pl.ds(TOP + 1, rows)])
            )
            inner[j + k - 1, here] = core
            inner[j + k - 1, TOP - 1 : TOP] = value[:1]
            inner[j + k - 1, TOP + rows : TOP + rows + 1] = value[rows - 1 :]
            found.append((value, part[:, :LANES], core, along))
        return found

    middle(1, 1)
    middle(LONG + 2, 1)

    for b in range(LONG // PART):

        def several(k, edge):
            first = b * PART + k * BATCH
            for j, (value, outer, core, along) in enumerate(middle(first + 2, BATCH)):
                i = first + j
                out[comp, base + i] = GAMMA * value + BETA * outer
                low[0, pl.ds(i, 1), :] = value[:1]
                high[0, pl.ds(i, 1), :] = value[rows - 1 :]
                low_curve[0, pl.ds(i, 1), :] = core[:1] + along[:1]
                high_curve[0, pl.ds(i, 1), :] = core[rows - 1 :] + along[rows - 1 :]
                part = k * BATCH + j
                edge = jnp.where(owner == part, turned_to(value, GROUP * part + 2), edge)
            return edge

        packed[0, :, b * LANES : (b + 1) * LANES] = lax.fori_loop(
            0, PART // BATCH, several, jnp.zeros((rows, LANES), jnp.float32)
        )

    def finish(i, carry):
        around = (inner[i, here] + inner[i + 2, here]) + (
            inner[i + 1, pl.ds(TOP - 1, rows)] + inner[i + 1, pl.ds(TOP + 1, rows)]
        )
        out[comp, base + i] = out[comp, base + i] + BETA * around
        return carry

    planes_loop(LONG, finish)


def stencil(increment, table):
    parts, xlen, rows = increment.shape[:3]
    half = LONG // 2
    pairs = xlen // 2
    slab = pl.BlockSpec((1, LONG, LANES), lambda c, i: (c, i, 0))
    return call(
        stencil_body,
        (parts, xlen // LONG),
        [
            (
                increment,
                pl.BlockSpec(
                    (1, 2, rows, LANES),
                    lambda c, i: (c, lax.rem(half * i + pairs - 1, pairs), 0, 0),
                ),
            ),
            (increment, pl.BlockSpec((1, LONG, rows, LANES), lambda c, i: (c, i, 0, 0))),
            (
                increment,
                pl.BlockSpec(
                    (1, 2, rows, LANES), lambda c, i: (c, lax.rem(half * i + half, pairs), 0, 0)
                ),
            ),
        ],
        [table],
        [
            (
                (parts, rows, GROUP * xlen),
                pl.BlockSpec((1, rows, LONG // PART * LANES), lambda c, i: (c, 0, i)),
            ),
        ]
        + [((parts, xlen, LANES), slab)] * 4,
        [increment.shape],
        [
            pltpu.VMEM((LONG + 4, rows + 2 * TOP, LANES), jnp.float32),
            pltpu.VMEM((LONG + 2, rows + 2 * TOP, LANES), jnp.float32),
        ],
        24 * increment.size,
        4 * increment.size,
        12,
    )


def corner_table():
    table = np.zeros((LANES, LANES))
    table[1::GROUP, 0] = 2.0
    table[2::GROUP, LANES - 1] = 2.0
    return table


def corner_body(low, high, left, right, table, out_low, out_high):
    parts, xlen = low.shape[:2]
    rows = left.shape[1]
    row = lax.broadcasted_iota(jnp.int32, (PART, LANES), 0)
    lane = lax.broadcasted_iota(jnp.int32, (PART, LANES), 1)
    mine = lane // GROUP == row
    for c in range(parts):
        for b in range(xlen // PART):
            planes = slice(b * PART, (b + 1) * PART)
            lanes = slice(b * LANES, (b + 1) * LANES)
            for curve, out, at in ((low, out_low, 0), (high, out_high, rows - 1)):
                rim = jnp.where(
                    lane % GROUP == 1, left[c, at : at + 1, lanes], right[c, at : at + 1, lanes]
                )
                rim = halves(jnp.where(mine, rim, 0.0))
                out[c, planes] = BETA * (curve[c, planes] + product(rim, table[...]))


def corners(low, high, left, right):
    near = pl.BlockSpec(memory_space=pltpu.VMEM)
    return pl.pallas_call(
        corner_body,
        in_specs=[near] * 5,
        out_specs=[near] * 2,
        out_shape=[jax.ShapeDtypeStruct(low.shape, jnp.float32)] * 2,
        cost_estimate=pl.CostEstimate(
            flops=8 * low.size, bytes_accessed=16 * low.size, transcendentals=0
        ),
        compiler_params=pltpu.CompilerParams(vmem_limit_bytes=12 * 1024 * 1024),
    )(low, high, left, right, doubled(corner_table()))


def edges_body(
    low, high, low_curve, high_curve, lanes, filtered, out,
):
    rows = filtered.shape[2]
    base = pl.program_id(0) * PART
    lane = lane_of(rows)
    row = lax.broadcasted_iota(jnp.int32, (8, LANES), 0)
    outer = (lane < 2) | (lane >= LANES - 2)
    for d in range(3):

        def plane(i, carry):
            at = pl.ds(i, 1)
            cyclic = turned_from(lanes[d], GROUP * i + 2)
            value = filtered[d, base + i] + jnp.where(outer, cyclic, 0.0)
            first = jnp.where(row == 1, BETA * low[d, at], 0.0)
            first = jnp.where(row == 0, low_curve[d, at], first)
            last = jnp.where(row == 6, BETA * high[d, at], 0.0)
            last = jnp.where(row == 7, high_curve[d, at], last)
            if rows == 8:
                out[d, base + i] = value + first + last
            else:
                out[d, base + i, :8] = value[:8] + first
                out[d, base + i, 8 : rows - 8] = value[8 : rows - 8]
                out[d, base + i, rows - 8 :] = value[rows - 8 :] + last
            return carry

        planes_loop(PART, plane, 0, 16)


def edges_pass(filtered, low, high, low_curve, high_curve, lanes):
    parts, xlen, rows = filtered.shape[:3]
    slab = pl.BlockSpec((parts, PART, LANES), lambda i: (0, i, 0))
    return call(
        edges_body,
        (xlen // PART,),
        [(low, slab), (high, slab), (low_curve, slab), (high_curve, slab)]
        + [(lanes, pl.BlockSpec((parts, rows, LANES), lambda i: (0, 0, i)))],
        [filtered],
        [],
        [filtered.shape],
        [],
        4 * filtered.size,
        filtered.size,
        4,
        (0, 0),
    )[0]


def gradient_table():
    cell = np.arange(LANES)
    gap = cell[None, :] - cell[:, None]
    slope = (gap == -1).astype(np.float64) - (gap == 1)
    none = np.zeros_like(slope)
    rims = np.zeros((LANES, 2 * LANES))
    rims[0::GROUP, 0] = -1.0
    rims[1::GROUP, LANES - 1] = 1.0
    rims[2::GROUP, LANES] = -1.0
    rims[3::GROUP, 2 * LANES - 1] = 1.0
    return jnp.asarray(np.block([[slope, none], [none, slope], [rims]]), jnp.bfloat16)


def load_states(m0, m0b, m0a, m1, m1b, m1a, lows, highs, rims, table, pad0, pad1, slopes):
    rows = m0.shape[1]
    base = pl.program_id(0) * PART
    here = pl.ds(TOP, rows)
    owner = lane_of(rows) // GROUP
    for which, (ref, before, after, pad) in enumerate(((m0, m0b, m0a, pad0), (m1, m1b, m1a, pad1))):

        @pl.when(base == 0)
        def _():
            pad[0, here] = before[0].astype(jnp.float32)

        pad[base + PART + 1, here] = after[0].astype(jnp.float32)

        def fill(i, carry):
            pad[base + i + 1, here] = ref[i].astype(jnp.float32)
            pad[base + i + 1, pl.ds(TOP - 1, 1)] = lows[which, pl.ds(i, 1), :]
            pad[base + i + 1, pl.ds(TOP + rows, 1)] = highs[which, pl.ds(i, 1), :]
            return carry

        planes_loop(PART, fill)

    def several(k, carry):
        first = k * BATCH
        flat = [
            pad[pl.ds(base + first + 1, BATCH), here].reshape(BATCH * rows, LANES).astype(jnp.bfloat16)
            for pad in (pad0, pad1)
        ]
        edge = jnp.concatenate([jnp.where(owner == first + j, rims, 0.0) for j in range(BATCH)], axis=0)
        both = product(jnp.concatenate(flat + [edge.astype(jnp.bfloat16)], axis=1), table[...])
        slopes[pl.ds(base + first, BATCH)] = both.reshape(BATCH, rows, 2 * LANES)
        return carry

    lax.fori_loop(0, PART // BATCH, several, 0)


def gradients(pad, slope, i, rows):
    here = pl.ds(TOP, rows)
    return (
        pad[i + 2, here] - pad[i, here],
        pad[i + 1, pl.ds(TOP + 1, rows)] - pad[i + 1, pl.ds(TOP - 1, rows)],
        slope,
    )


def merged_rims(left, right, rows):
    spot = lane_of(rows) % GROUP
    return jnp.where(spot % 2 == 0, left[...], right[...])


def first_state_body(
    increment, m0, m0b, m0a, m1, m1b, m1a, lows, highs, left, right, table,
    packed, low, high, state, source, pad0, pad1, slopes,
):
    rows = m0.shape[1]
    base = pl.program_id(0) * PART
    owner = lane_of(rows) // GROUP
    rims = merged_rims(left, right, rows)
    load_states(m0, m0b, m0a, m1, m1b, m1a, lows, highs, rims, table, pad0, pad1, slopes)

    def plane(i, edge):
        g0 = gradients(pad0, slopes[base + i, :, :LANES], base + i, rows)
        g1 = gradients(pad1, slopes[base + i, :, LANES:], base + i, rows)
        u = [increment[d, i] for d in range(3)]
        one = (-0.5 * STEP) * (u[0] * g0[0] + u[1] * g0[1] + u[2] * g0[2])
        state[base + i] = one
        source[base + i] = (0.5 * STEP) * (u[0] * g1[0] + u[1] * g1[1] + u[2] * g1[2])
        low[pl.ds(i, 1), :] = one[:1]
        high[pl.ds(i, 1), :] = one[rows - 1 :]
        return jnp.where(owner == i, turned_to(one, GROUP * i + 1), edge)

    packed[...] = planes_loop(PART, plane, jnp.zeros((rows, LANES), jnp.float32), 16)


def around(array):
    xlen, rows = array.shape[:2]
    return [
        (array, pl.BlockSpec((PART, rows, LANES), lambda i: (i, 0, 0))),
        (array, pl.BlockSpec((1, rows, LANES), lambda i: (lax.rem(PART * i + xlen - 1, xlen), 0, 0))),
        (array, pl.BlockSpec((1, rows, LANES), lambda i: (lax.rem(PART * i + PART, xlen), 0, 0))),
    ]


def first_state(increment, first, second, lows, highs, left, right):
    xlen, rows = first.shape[0], first.shape[1]
    triple = pl.BlockSpec((3, PART, rows, LANES), lambda i: (0, i, 0, 0))
    slab = pl.BlockSpec((PART, LANES), lambda i: (i, 0))
    double = pl.BlockSpec((2, PART, LANES), lambda i: (0, i, 0))
    rim = pl.BlockSpec((rows, LANES), lambda i: (0, i))
    return call(
        first_state_body,
        (xlen // PART,),
        [(increment, triple)]
        + around(first)
        + around(second)
        + [(lows, double), (highs, double), (left, rim), (right, rim)],
        [gradient_table()],
        [((rows, GROUP * xlen), rim), ((xlen, LANES), slab), ((xlen, LANES), slab)],
        [first.shape, first.shape]
        + [(xlen + 2, rows + 2 * TOP, LANES)] * 2
        + [(xlen, rows, 2 * LANES)],
        [],
        24 * first.size,
        16 * first.size,
        6,
    )


def second_state_body(
    velocity, low, high, left, right, state, source, packed, out_low, out_high, adjoint, across
):
    xlen, rows = state.shape[0], state.shape[1]
    base = pl.program_id(0) * PART
    lane = lane_of(rows)
    owner = lane // GROUP
    rims = merged_rims(left, right, rows)

    def lanes_part(i, carry):
        value = state[base + i]
        speed = velocity[2, i]
        before, after = z_sides(value, turned_from(rims, GROUP * i + 1), lane)
        across[i] = (STEP * speed) * jnp.where(speed > 0.0, value - before, after - value)
        return carry

    planes_loop(PART, lanes_part)

    def plane(i, edge):
        value = state[base + i]
        total = (source[base + i] - value) + across[i]
        sides = [
            (
                state[lax.rem(base + i + xlen - 1, xlen)],
                state[lax.rem(base + i + 1, xlen)],
            ),
            y_sides(value, low[pl.ds(i, 1), :], high[pl.ds(i, 1), :]),
        ]
        for d in range(2):
            speed = velocity[d, i]
            slope = jnp.where(speed > 0.0, value - sides[d][0], sides[d][1] - value)
            total = total + (STEP * speed) * slope
        adjoint[base + i] = total
        along = velocity[1, i]
        out_low[pl.ds(i, 1), :] = jnp.maximum(along[:1], 0.0) * total[:1]
        out_high[pl.ds(i, 1), :] = jnp.minimum(along[rows - 1 :], 0.0) * total[rows - 1 :]
        along = velocity[2, i]
        flow = total * jnp.where(
            lane == LANES - 1, jnp.minimum(along, 0.0), jnp.maximum(along, 0.0)
        )
        return jnp.where(owner == i, turned_to(flow, GROUP * i + 1), edge)

    packed[...] = planes_loop(PART, plane, jnp.zeros((rows, LANES), jnp.float32), 16)


def second_state(velocity, source, state, low, high, left, right):
    xlen, rows = state.shape[0], state.shape[1]
    triple = pl.BlockSpec((3, PART, rows, LANES), lambda i: (0, i, 0, 0))
    slab = pl.BlockSpec((PART, LANES), lambda i: (i, 0))
    rim = pl.BlockSpec((rows, LANES), lambda i: (0, i))
    return call(
        second_state_body,
        (xlen // PART,),
        [(velocity, triple), (low, slab), (high, slab), (left, rim), (right, rim)],
        [state, source],
        [((rows, GROUP * xlen), rim), ((xlen, LANES), slab), ((xlen, LANES), slab)],
        [state.shape],
        [pltpu.VMEM((PART, rows, LANES), jnp.float32)],
        30 * state.size,
        12 * state.size,
        6,
        (1, 0),
    )


def fold_table(count):
    return np.repeat(np.eye(count), 4, axis=1)


def hessian_body(
    velocity, speed_b, speed_a, flow_low, flow_high, flow_left, flow_right,
    filtered, adjoint, pad0, pad1, slopes, fold_z, out, restricted, flows, sums, few,
):
    xlen, rows = adjoint.shape[0], adjoint.shape[1]
    base = pl.program_id(0) * PART
    lane = lane_of(rows)
    row = lax.broadcasted_iota(jnp.int32, (rows, LANES), 0)
    ends = merged_rims(flow_left, flow_right, rows)

    def across(i, carry):
        value = adjoint[base + i]
        speed = velocity[2, i]
        rim = turned_from(ends, GROUP * i + 1)
        flows[i] = turn(jnp.where(lane == 0, rim, jnp.maximum(speed, 0.0) * value), -1) - turn(
            jnp.where(lane == LANES - 1, rim, jnp.minimum(speed, 0.0) * value), 1
        )
        return carry

    planes_loop(PART, across)

    def plane(i, carry):
        g0 = gradients(pad0, slopes[base + i, :, :LANES], base + i, rows)
        g1 = gradients(pad1, slopes[base + i, :, LANES:], base + i, rows)
        value = adjoint[base + i]
        sx, sy, sz = (velocity[d, i] for d in range(3))
        before, after = jnp.maximum(i - 1, 0), jnp.minimum(i + 1, PART - 1)
        speed_before = jnp.where(i == 0, speed_b[0, 0], velocity[0, before])
        speed_after = jnp.where(i == PART - 1, speed_a[0, 0], velocity[0, after])
        prev = jnp.minimum(speed_before, 0.0) * adjoint[lax.rem(base + i + xlen - 1, xlen)]
        later = jnp.maximum(speed_after, 0.0) * adjoint[lax.rem(base + i + 1, xlen)]
        inflow = pltpu.roll(jnp.minimum(sy, 0.0) * value, 1, 0)
        outflow = pltpu.roll(jnp.maximum(sy, 0.0) * value, rows - 1, 0)
        change = (
            (later - prev)
            + flows[i]
            + jnp.where(row == rows - 1, flow_high[pl.ds(i, 1), :], outflow)
            - jnp.where(row == 0, flow_low[pl.ds(i, 1), :], inflow)
            - (jnp.abs(sx) + jnp.abs(sy) + jnp.abs(sz)) * value
        )
        half_two = (0.5 * STEP) * value
        half_one = half_two + (0.5 * STEP * STEP) * change
        for d in range(3):
            out[d, i] = filtered[d, base + i] + half_one * g0[d] + half_two * g1[d]
        return carry

    planes_loop(PART, plane)

    count = PART // 4 * (rows // 4)
    for d in range(3):

        def fold(k, carry):
            total = (out[d, 4 * k] + out[d, 4 * k + 1]) + (out[d, 4 * k + 2] + out[d, 4 * k + 3])
            total = total + pltpu.roll(total, rows - 1, 0)
            sums[pl.ds(k * rows, rows)] = total + pltpu.roll(total, rows - 2, 0)
            return carry

        planes_loop(PART // 4, fold)
        few[pl.ds(d * count, count)] = sums[pl.ds(0, count, stride=4)]
    found = product(halves(few[...]), fold_z[...]) * (1.0 / 64.0)
    restricted[...] = found.reshape(3, count, LANES // 4)


def hessian_pass(
    filtered, velocity, adjoint, pads, flow_low, flow_high, flow_left, flow_right,
):
    xlen, rows = adjoint.shape[0], adjoint.shape[1]
    triple = pl.BlockSpec((3, PART, rows, LANES), lambda i: (0, i, 0, 0))
    slab = pl.BlockSpec((PART, LANES), lambda i: (i, 0))
    rim = pl.BlockSpec((rows, LANES), lambda i: (0, i))
    speed_b = pl.BlockSpec(
        (1, 1, rows, LANES), lambda i: (0, lax.rem(PART * i + xlen - 1, xlen), 0, 0)
    )
    speed_a = pl.BlockSpec((1, 1, rows, LANES), lambda i: (0, lax.rem(PART * i + PART, xlen), 0, 0))
    coarse_rows = PART // 4 * (rows // 4)
    return call(
        hessian_body,
        (xlen // PART,),
        [(velocity, triple), (velocity, speed_b), (velocity, speed_a)]
        + [(flow_low, slab), (flow_high, slab), (flow_left, rim), (flow_right, rim)],
        [filtered, adjoint, *pads, doubled(fold_table(LANES // 4).T)],
        [
            (filtered.shape, triple),
            (
                (3, xlen // 4 * (rows // 4), LANES // 4),
                pl.BlockSpec((3, coarse_rows, LANES // 4), lambda i: (0, i, 0)),
            ),
        ],
        [],
        [
            pltpu.VMEM((PART, rows, LANES), jnp.float32),
            pltpu.VMEM((PART // 4 * rows, LANES), jnp.float32),
            pltpu.VMEM((3 * coarse_rows, LANES), jnp.float32),
        ],
        70 * adjoint.size,
        24 * adjoint.size,
        9,
    )


def final_body(coarse, hessian, spread_z, out, wide):
    rows = hessian.shape[2]
    few = rows // 4
    wide[...] = product(halves(coarse[0]), spread_z[...])
    half = lax.broadcasted_iota(jnp.int32, (8, LANES), 0) < 4

    def fold(k, carry):
        add = [
            jnp.where(
                half, wide[pl.ds(k * few + 2 * r, 1), :], wide[pl.ds(k * few + 2 * r + 1, 1), :]
            )
            for r in range(rows // 8)
        ]
        add = jnp.concatenate(add, axis=0)
        for j in range(4):
            out[0, 4 * k + j] = OMEGA * hessian[0, 4 * k + j] + add
        return carry

    planes_loop(WIDE // 4, fold, 0, 2)


def final_pass(hessian, coarse):
    parts, xlen, rows = hessian.shape[:3]
    block = pl.BlockSpec((1, WIDE, rows, LANES), lambda c, i: (c, i, 0, 0))
    coarse_rows = WIDE // 4 * (rows // 4)
    return call(
        final_body,
        (parts, xlen // WIDE),
        [
            (coarse, pl.BlockSpec((1, coarse_rows, LANES // 4), lambda c, i: (c, i, 0))),
            (hessian, block),
        ],
        [doubled(fold_table(LANES // 4))],
        [(hessian.shape, block)],
        [],
        [pltpu.VMEM((coarse_rows, LANES), jnp.float32)],
        2 * hessian.size,
        8 * hessian.size,
        20,
    )[0]


def coarse_spread(restricted):
    both = ("gz", "gy")
    groups_z = lax.axis_size("gz")
    groups_y = lax.axis_size("gy")
    devices = groups_z * groups_y
    cxlen, cylen, czlen = (restricted.shape[1], restricted.shape[2], restricted.shape[3])
    full_y = groups_y * cylen
    full_z = groups_z * czlen
    each = -(-3 * cxlen // devices)
    table_x = cas_table(cxlen)
    table_y = cas_table(full_y)
    table_z = cas_table(full_z)
    coeffs = jnp.einsum("xi,cijk->cxjk", table_x, restricted, precision=HIGH)
    coeffs = coeffs.reshape(3 * cxlen, cylen, czlen)
    coeffs = jnp.pad(coeffs, ((0, each * devices - 3 * cxlen), (0, 0), (0, 0)))
    planes = lax.all_to_all(coeffs, both, 0, 0, tiled=True)
    planes = planes.reshape(groups_z, groups_y, each, cylen, czlen)
    planes = planes.transpose(2, 1, 3, 0, 4).reshape(each, full_y, full_z)
    planes = jnp.einsum("yj,pjk->pyk", table_y, planes, precision=HIGH)
    planes = jnp.einsum("zk,pyk->pyz", table_z, planes, precision=HIGH)
    line_x = jnp.tile(eigen_line(cxlen), -(-each * devices // cxlen))
    line_x = lax.dynamic_slice_in_dim(line_x, lax.axis_index(both) * each, each, 0)
    total = (
        line_x[:, None, None] + eigen_line(full_y)[None, :, None] + eigen_line(full_z)[None, None, :]
    )
    planes = planes / (GAMMA + COARSE_BETA * total * total)
    planes = jnp.einsum("zk,pyk->pyz", table_z, planes, precision=HIGH)
    planes = jnp.einsum("yj,pjk->pyk", table_y, planes, precision=HIGH)
    planes = planes.reshape(each, groups_y, cylen, groups_z, czlen).transpose(3, 1, 0, 2, 4)
    planes = planes.reshape(devices * each, cylen, czlen)
    coeffs = lax.all_to_all(planes, both, 0, 0, tiled=True)[: 3 * cxlen]
    coeffs = coeffs.reshape(3, cxlen, cylen, czlen)
    coeffs = jnp.einsum("xi,cijk->cxjk", table_x, coeffs, precision=HIGH)
    return coeffs / float(cxlen * full_y * full_z)


def lane_curve(left, right):
    spot = lax.broadcasted_iota(jnp.int32, left.shape, 2) % GROUP
    rims = jnp.where(spot < 2, left, right)
    rows = rims.shape[1]
    empty = jnp.zeros_like(rims[:, :1])
    up = jnp.concatenate([rims[:, 1:], empty], axis=1)
    down = jnp.concatenate([empty, rims[:, : rows - 1]], axis=1)
    bent = -2.0 * (
        6.0 * rims - jnp.roll(rims, GROUP, 2) - jnp.roll(rims, -GROUP, 2) - up - down
    )
    plain = jnp.where(spot < 2, jnp.roll(rims, -2, 2), jnp.roll(rims, 2, 2))
    curve = jnp.where(spot == 1, jnp.roll(bent, -1, 2), jnp.roll(bent, 1, 2))
    return BETA * (plain + jnp.where((spot == 1) | (spot == 2), curve, 0.0))


def per_device(velocity, increment, template, deformed):
    xlen, rows = template.shape[0], template.shape[1]

    packed, low, high = state_rims(template, deformed)
    packed, low, high, table = lax.optimization_barrier((packed, low, high, stencil_table()))
    left = shifted(packed, "gz", 1)
    right = shifted(packed, "gz", -1)
    lows = shifted(high, "gy", 1)
    highs = shifted(low, "gy", -1)

    inc_packed, inc_low, inc_high, low_curve, high_curve, filtered = stencil(increment, table)
    inc_packed, inc_low, inc_high, left, right, lows, highs = lax.optimization_barrier(
        (inc_packed, inc_low, inc_high, left, right, lows, highs)
    )
    inc_left = shifted(inc_packed, "gz", 1)
    inc_right = shifted(inc_packed, "gz", -1)
    inc_lows = shifted(inc_high, "gy", 1)
    inc_highs = shifted(inc_low, "gy", -1)

    s_packed, s_low, s_high, state, source, *pads = first_state(
        increment, template, deformed, lows, highs, left, right
    )
    s_left = shifted(s_packed, "gz", 1)
    s_right = shifted(s_packed, "gz", -1)
    s_below = shifted(s_high, "gy", 1)
    s_above = shifted(s_low, "gy", -1)

    low_curve, high_curve = corners(low_curve, high_curve, inc_left, inc_right)
    s_left, low_curve, high_curve = lax.optimization_barrier((s_left, low_curve, high_curve))
    low_curves = shifted(high_curve, "gy", 1)
    high_curves = shifted(low_curve, "gy", -1)

    f_packed, f_low, f_high, adjoint = second_state(
        velocity, source, state, s_below, s_above, s_left, s_right
    )
    f_packed, f_low, f_high, low_curves, high_curves = lax.optimization_barrier(
        (f_packed, f_low, f_high, low_curves, high_curves)
    )
    f_left = shifted(f_packed, "gz", 1)
    f_right = shifted(f_packed, "gz", -1)
    f_below = shifted(f_high, "gy", 1)
    f_above = shifted(f_low, "gy", -1)

    filtered = edges_pass(
        filtered, inc_lows, inc_highs, low_curves, high_curves, lane_curve(inc_left, inc_right)
    )
    hessian, restricted = hessian_pass(
        filtered, velocity, adjoint, pads, f_below, f_above, f_left, f_right
    )
    coarse = coarse_spread(restricted.reshape(3, xlen // 4, rows // 4, LANES // 4))
    mixed = coarse.reshape(restricted.shape) - OMEGA * restricted
    return final_pass(hessian, mixed)


def solution(mesh):
    placed = (
        P(None, None, "gy", "gz"),
        P(None, None, "gy", "gz"),
        P(None, "gy", "gz"),
        P(None, "gy", "gz"),
    )
    return jax.shard_map(
        per_device, mesh=mesh, in_specs=placed, out_specs=P(None, None, "gy", "gz"), check_vma=False
    )
```

time: 350 us -> 169 us (0.48)
  Pallas kernels: 204 us -> 88.2 us
  waiting for transfers between devices: 55.7 us -> 13.4 us
  local copies, waits for them, and re-layouts: 40.4 us -> 6.2 us
  blocking collectives: 0 us -> 11.3 us
  starting transfers between devices: 36.4 us -> 42 us
  other arithmetic: 7 us -> 2.94 us
    pallas_call x6 -> x8, Pallas kernels: 204 us -> 88.2 us  [the longest x7 87.6 us: call(): pl.pallas_call(kernel, in_specs=[far] * counts[0] + [near] * counts[1], o...]
    ppermute x16 -> x18, waiting for transfers between devices: 39.2 us -> 5.31 us  [shifted(): lax.ppermute(value, axis, [(i, (i + by) % peers) for i in range(peers)])]
    slice x2 -> x0, local copies, waits for them, and re-layouts: 21 us -> none  [the longest x1 14 us: per_device(): from_right[:, 0, :, 2]]
    ppermute x16 -> x18, starting transfers between devices: 27.5 us -> 39.1 us  [shifted(): lax.ppermute(value, axis, [(i, (i + by) % peers) for i in range(peers)])]
    all_to_all x0 -> x1, blocking collectives: none -> 11.3 us  [coarse_spread(): coeffs = lax.all_to_all(planes, both, 0, 0, tiled=True)[:3 * cxlen]]
    all_to_all x1 -> x0, waiting for transfers between devices: 8.23 us -> none  [coarse_spread(): coeffs = lax.all_to_all(planes, both, 0, 0, tiled=True)[:3 * cxlen]]
    concatenate x8 -> x0, local copies, waits for them, and re-layouts: 5.89 us -> none  [the longest x4 4.02 us: slab_curve(): jnp.roll(row, -1, 2)]
    ppermute x2 -> x0, local copies, waits for them, and re-layouts: 5.33 us -> none  [shifted(): lax.ppermute(value, axis, [(i, (i + by) % peers) for i in range(peers)])]
  transfers between devices with their start and end apart: 18 -> 19, of which waited for: 8 -> 3; matrix products, arithmetic and copies ran while one was open for 12% -> 1% of each run, Pallas kernels for 22% -> 31%
where the time goes in v2:
time: 169 us
  Pallas kernels  88.2 us (52%)
  starting transfers between devices  42 us (25%)
  waiting for transfers between devices  13.4 us (8%)
  blocking collectives  11.3 us (7%)
  local copies, waits for them, and re-layouts  6.2 us (4%)
  matrix products  4.08 us (2%)
  other arithmetic  2.94 us (2%)
    pallas_call x7, Pallas kernels, call(): pl.pallas_call(kernel, in_specs=[far] * counts[0] + [near] * counts[1], o...  87.6 us
    ppermute x18, starting transfers between devices, shifted(): lax.ppermute(value, axis, [(i, (i + by) % peers) for i in range(peers)])  39.1 us
    all_to_all x1, blocking collectives, coarse_spread(): coeffs = lax.all_to_all(planes, both, 0, 0, tiled=True)[:3 * cxlen]  11.3 us
    all_to_all x1, waiting for transfers between devices, coarse_spread(): planes = lax.all_to_all(coeffs, both, 0, 0, tiled=True)  8.1 us
    ppermute x18, waiting for transfers between devices, shifted(): lax.ppermute(value, axis, [(i, (i + by) % peers) for i in range(peers)])  5.31 us
  transfers between devices with their start and end apart: 19, of which 3 were waited for; matrix products, arithmetic and copies ran while one was open for 1% of the time, Pallas kernels for 31%

profile of v2, /device:TPU:0, one launch (start us, length us, event | category | flops | bytes accessed | tf_op | source)
XLA Modules:
  0.0 168.6 jit_solution(6054325246823854077)
XLA Ops:
  0.0 6.0 %shard_map.145 = (f32[32,1024]{1,0:T(8,128)S(1)}, f32[2,256,128]{2,1,0:T(8,128)S(1)}, f32[2,256,128]{2,1,0:T(8,128)S(1)}) custom-call(bf16[256,32,128]{2,1,0:T(8,128)(2,1)} %refs_3_.1, bf16[256,32,128]{2,1,0:T(8,128)(2,1)} %refs_6_.1), custom_call_target="tpu_custom_call" | custom-call | flops 8388608 | bytes 4194304 | tf_op jit(solution)/shard_map/pallas_call | solution.py:122
  6.0 3.0 %collective-permute-start.2 = (f32[2,256,128]{2,1,0:T(8,128)S(1)}, f32[2,256,128]{2,1,0:T(8,128)S(1)}, u32[]{:S(2)}, u32[]{:S(2)}) collective-permute-start(f32[2,256,128]{2,1,0:T(8,128)S(1)} %get-tuple-element.57), channel_id=1, source_target_pairs={{0,1},{1,2},{2,3},{3,4},{4,5},{5,6},{6,7},{7,0},{8,9},{9,10},{10,1... | collective-permute-start | bytes 786440 | tf_op jit(solution)/shard_map/ppermute | solution.py:32
  9.0 3.1 %collective-permute-start.3 = (f32[2,256,128]{2,1,0:T(8,128)S(1)}, f32[2,256,128]{2,1,0:T(8,128)S(1)}, u32[]{:S(2)}, u32[]{:S(2)}) collective-permute-start(f32[2,256,128]{2,1,0:T(8,128)S(1)} %get-tuple-element.58), channel_id=1, source_target_pairs={{0,7},{1,0},{2,1},{3,2},{4,3},{5,4},{6,5},{7,6},{8,15},{9,8},{10,9... | collective-permute-start | bytes 786440 | tf_op jit(solution)/shard_map/ppermute | solution.py:32
  12.2 1.7 %collective-permute-start.1 = (f32[32,1024]{1,0:T(8,128)S(1)}, f32[32,1024]{1,0:T(8,128)S(1)}, u32[]{:S(2)}, u32[]{:S(2)}) collective-permute-start(f32[32,1024]{1,0:T(8,128)S(1)} %get-tuple-element.56), channel_id=1, source_target_pairs={{0,24},{8,0},{16,8},{24,16},{1,25},{9,1},{17,9},{25,17},{2,26},{10... | collective-permute-start | bytes 393224 | tf_op jit(solution)/shard_map/ppermute | solution.py:32
  13.9 0.9 copy-done.2
  14.8 16.6 %shard_map.146 = (f32[3,32,1024]{2,1,0:T(8,128)S(1)}, f32[3,256,128]{2,1,0:T(8,128)S(1)}, f32[3,256,128]{2,1,0:T(8,128)S(1)}, f32[3,256,128]{2,1,0:T(8,128)S(1)}...) custom-call(f32[3,256,32,128]{3,2,1,0:T(8,128)} %refs_0_.7, f32[3,256,32,128]{3,2,1,0:T(8,128)} %refs_0_.7, ...), custom_call_target="tpu_custom_call" | custom-call | flops 75497472 | bytes 12582912 | tf_op jit(solution)/shard_map/pallas_call | solution.py:122
  31.5 1.7 %collective-permute-start.8 = (f32[3,32,1024]{2,1,0:T(8,128)S(1)}, f32[3,32,1024]{2,1,0:T(8,128)S(1)}, u32[]{:S(2)}, u32[]{:S(2)}) collective-permute-start(f32[3,32,1024]{2,1,0:T(8,128)S(1)} %get-tuple-element.68), channel_id=1, source_target_pairs={{0,24},{8,0},{16,8},{24,16},{1,25},{9,1},{17,9},{25,17},{2,26},{10... | collective-permute-start | bytes 1179656 | tf_op jit(solution)/shard_map/ppermute | solution.py:32
  33.3 12.0 %shard_map.147 = (f32[32,1024]{1,0:T(8,128)S(1)}, f32[256,128]{1,0:T(8,128)S(1)}, f32[256,128]{1,0:T(8,128)S(1)}, f32[256,32,128]{2,1,0:T(8,128)S(1)}, f32[256,3...) custom-call(f32[3,256,32,128]{3,2,1,0:T(8,128)} %refs_0_.7, ...), custom_call_target="tpu_custom_call" | custom-call | flops 25165824 | bytes 16777216 | tf_op jit(solution)/shard_map/pallas_call | solution.py:122
  45.3 1.7 %collective-permute-start.9 = (f32[32,1024]{1,0:T(8,128)S(1)}, f32[32,1024]{1,0:T(8,128)S(1)}, u32[]{:S(2)}, u32[]{:S(2)}) collective-permute-start(f32[32,1024]{1,0:T(8,128)S(1)} %get-tuple-element.65), channel_id=1, source_target_pairs={{0,24},{8,0},{16,8},{24,16},{1,25},{9,1},{17,9},{25,17},{2,26},{10... | collective-permute-start | bytes 393224 | tf_op jit(solution)/shard_map/ppermute | solution.py:32
  47.1 4.7 %collective-permute-start.5 = (f32[256,128]{1,0:T(8,128)S(1)}, f32[256,128]{1,0:T(8,128)S(1)}, u32[]{:S(2)}, u32[]{:S(2)}) collective-permute-start(f32[256,128]{1,0:T(8,128)S(1)} %get-tuple-element.64), channel_id=1, source_target_pairs={{0,7},{1,0},{2,1},{3,2},{4,3},{5,4},{6,5},{7,6},{8,15},{9,8},{10,9... | collective-permute-start | bytes 393224 | tf_op jit(solution)/shard_map/ppermute | solution.py:32
  51.9 0.2 fusion.22
  52.1 0.2 fusion.25
  52.3 0.5 shard_map.148
  52.9 4.8 %collective-permute-start.17 = (f32[3,256,128]{2,1,0:T(8,128)S(1)}, f32[3,256,128]{2,1,0:T(8,128)S(1)}, u32[]{:S(2)}, u32[]{:S(2)}) collective-permute-start(f32[3,256,128]{2,1,0:T(8,128)S(1)} %get-tuple-element.83), channel_id=1, source_target_pairs={{0,7},{1,0},{2,1},{3,2},{4,3},{5,4},{6,5},{7,6},{8,15},{9,8},{10,9... | collective-permute-start | bytes 1179656 | tf_op jit(solution)/shard_map/ppermute | solution.py:32
  57.7 0.2 fusion.13
  58.1 4.1 %collective-permute-done.4.refs_1_ = f32[256,128]{1,0:T(8,128)S(1)} collective-permute-done((f32[256,128]{1,0:T(8,128)S(1)}, f32[256,128]{1,0:T(8,128)S(1)}, u32[]{:S(2)}, u32[]{:S(2)}) %collective-permute-start.4) | collective-permute-done | bytes 131104 | tf_op jit(solution)/shard_map/ppermute | solution.py:32
  62.2 2.5 %collective-permute-start.10 = (f32[3,256,128]{2,1,0:T(8,128)S(1)}, f32[3,256,128]{2,1,0:T(8,128)S(1)}, u32[]{:S(2)}, u32[]{:S(2)}) collective-permute-start(f32[3,256,128]{2,1,0:T(8,128)S(1)} %get-tuple-element.77), channel_id=1, source_target_pairs={{0,1},{1,2},{2,3},{3,4},{4,5},{5,6},{6,7},{7,0},{8,9},{9,10},{10,1... | collective-permute-start | bytes 1179656 | tf_op jit(solution)/shard_map/ppermute | solution.py:32
  64.7 9.2 %collective-permute-start.11 = (f32[3,256,128]{2,1,0:T(8,128)S(1)}, f32[3,256,128]{2,1,0:T(8,128)S(1)}, u32[]{:S(2)}, u32[]{:S(2)}) collective-permute-start(f32[3,256,128]{2,1,0:T(8,128)S(1)} %get-tuple-element.78), channel_id=1, source_target_pairs={{0,7},{1,0},{2,1},{3,2},{4,3},{5,4},{6,5},{7,6},{8,15},{9,8},{10,9... | collective-permute-start | bytes 1179656 | tf_op jit(solution)/shard_map/ppermute | solution.py:32
  73.9 13.8 %shard_map.149 = (f32[32,1024]{1,0:T(8,128)S(1)}, f32[256,128]{1,0:T(8,128)S(1)}, f32[256,128]{1,0:T(8,128)S(1)}, f32[256,32,128]{2,1,0:T(8,128)S(1)}) custom-call(f32[3,256,32,128]{3,2,1,0:T(8,128)} %refs_2_.6, f32[256,128]{1,0:T(8,128)S(1)} %collective-permute-done.4.refs_1_, ...), custom_call_target="tpu_custom_call", output_to_operand_aliasing={{3}: (6, {})} | custom-call | flops 31457280 | bytes 12582912 | tf_op jit(solution)/shard_map/pallas_call | solution.py:122
  87.8 1.2 collective-permute-done.11.refs_3_
  89.0 1.7 %collective-permute-start.15 = (f32[32,1024]{1,0:T(8,128)S(1)}, f32[32,1024]{1,0:T(8,128)S(1)}, u32[]{:S(2)}, u32[]{:S(2)}) collective-permute-start(f32[32,1024]{1,0:T(8,128)S(1)} %get-tuple-element.81), channel_id=1, source_target_pairs={{0,24},{8,0},{16,8},{24,16},{1,25},{9,1},{17,9},{25,17},{2,26},{10... | collective-permute-start | bytes 393224 | tf_op jit(solution)/shard_map/ppermute | solution.py:32
  90.8 0.2 collective-permute-start.12
  91.0 4.5 %collective-permute-start.13 = (f32[256,128]{1,0:T(8,128)S(1)}, f32[256,128]{1,0:T(8,128)S(1)}, u32[]{:S(2)}, u32[]{:S(2)}) collective-permute-start(f32[256,128]{1,0:T(8,128)S(1)} %get-tuple-element.80), channel_id=1, source_target_pairs={{0,7},{1,0},{2,1},{3,2},{4,3},{5,4},{6,5},{7,6},{8,15},{9,8},{10,9... | collective-permute-start | bytes 393224 | tf_op jit(solution)/shard_map/ppermute | solution.py:32
  95.5 0.3 fusion.9.refs_4_
  95.8 8.8 %shard_map.150.refs_7_ = f32[3,256,32,128]{3,2,1,0:T(8,128)S(1)} custom-call(f32[3,256,128]{2,1,0:T(8,128)S(1)} %collective-permute-done.16.refs_0_, f32[3,256,128]{2,1,0:T(8,128)S(1)} %collective-permute-done.17.refs_1_, f32[3,256,128]{2,1,0:T(8,128)S(1)} %collective-permute-done.10.refs_2_, ...), custom_call_target="tpu_custom_call", output_to_operand_aliasing={{}: (5, {})} | custom-call | flops 12582912 | bytes 3145728 | tf_op jit(solution)/shard_map/pallas_call | solution.py:122
  104.7 18.9 %shard_map.151 = (f32[3,256,32,128]{3,2,1,0:T(8,128)}, f32[3,512,32]{2,1,0:T(8,128)S(1)}) custom-call(f32[3,256,32,128]{3,2,1,0:T(8,128)} %refs_2_.6, f32[3,256,32,128]{3,2,1,0:T(8,128)} %refs_2_.6, f32[3,256,32,128]{3,2,1,0:T(8,128)} %refs_2_.6, f32[256,128]{1,0:T(8,128)S(1)} %collective-permute-done.12.refs_3_, ...), custom_call_target="tpu_custom_call" | custom-call | flops 73400320 | bytes 25165824 | tf_op jit(solution)/shard_map/pallas_call | solution.py:122
  123.7 1.4 convolution_bitcast_fusion
  125.1 0.3 copy.44
  125.4 1.0 reshape.69
  126.4 2.9 %all-to-all-start = ((f32[32,1,1536]{2,1,0:T(1,128)}), f32[32,1,1536]{2,1,0:T(1,128)S(1)}, u32[]{:S(2)}, u32[]{:S(2)}) async-start(f32[32,1,1536]{2,1,0:T(1,128)} %reshape.69), calls=%async_computation | async-start | bytes 393216 | tf_op jit(solution)/shard_map/all_to_all | solution.py:737
  129.6 8.1 %all-to-all-done = f32[32,1,1536]{2,1,0:T(1,128)S(1)} async-done(((f32[32,1,1536]{2,1,0:T(1,128)}), f32[32,1,1536]{2,1,0:T(1,128)S(1)}, u32[]{:S(2)}, u32[]{:S(2)}) %all-to-all-start) | async-done | bytes 196640 | tf_op jit(solution)/shard_map/all_to_all | solution.py:737
  137.7 0.5 broadcast.57
  138.2 1.1 reduce
  139.3 0.2 reshape.70
  139.6 0.5 copy.38
  140.1 0.4 reshape.61
  140.4 0.3 convolution_bitcast_fusion.2
  140.8 0.3 convolution_divide_fusion
  141.1 0.3 fusion.26
  141.5 0.3 convolution_bitcast_fusion.1
  141.8 0.3 reshape.62
  142.2 0.4 reshape.71
  142.6 11.3 %all_to_all.10 = f32[32,1,1536]{2,1,0:T(1,128)S(1)} all-to-all(f32[32,1,1536]{2,1,0:T(1,128)S(1)} %reshape.71), channel_id=1, replica_groups=mesh['gz'=4,'gy'=8] {'gz','gy'}, dimensions={0} | all-to-all | bytes 393216 | tf_op jit(solution)/shard_map/all_to_all | solution.py:752
  153.9 1.1 reduce.1
  155.0 0.2 reshape.72
  155.2 1.4 fusion
  156.6 0.3 copy.42
  157.1 11.6 %shard_map.152 = f32[3,256,32,128]{3,2,1,0:T(8,128)} custom-call(f32[3,512,32]{2,1,0:T(8,128)S(1)} %bitcast_subtract_fusion.refs_0_, f32[3,256,32,128]{3,2,1,0:T(8,128)} %get-tuple-element.92.refs_1_, bf16[64,128]{1,0:T(8,128)(2,1)S(1)} %copy-done.5), custom_call_target="tpu_custom_call" | custom-call | flops 6291456 | bytes 25165824 | tf_op jit(solution)/shard_map/pallas_call | solution.py:122
  (63 shorter events, 1.2 us)
Async XLA Ops:
  6.0 27.2 %copy-start.1 = (bf16[384,256]{1,0:T(8,128)(2,1)S(1)}, bf16[384,256]{1,0:T(8,128)(2,1)}, u32[]{:S(2)}) copy-start(bf16[384,256]{1,0:T(8,128)(2,1)} %constant.72.clone.refs_11_) | copy-start | bytes 589828
  6.0 25.4 %collective-permute-start.2 = (f32[2,256,128]{2,1,0:T(8,128)S(1)}, f32[2,256,128]{2,1,0:T(8,128)S(1)}, u32[]{:S(2)}, u32[]{:S(2)}) collective-permute-start(f32[2,256,128]{2,1,0:T(8,128)S(1)} %get-tuple-element.57), channel_id=1, source_target_pairs={{0,1},{1,2},{2,3},{3,4},{4,5},{5,6},{6,7},{7,0},{8,9},{9,10},{10,1... | collective-permute-start | bytes 786440 | tf_op jit(solution)/shard_map/ppermute | solution.py:32
  9.0 22.4 %collective-permute-start.3 = (f32[2,256,128]{2,1,0:T(8,128)S(1)}, f32[2,256,128]{2,1,0:T(8,128)S(1)}, u32[]{:S(2)}, u32[]{:S(2)}) collective-permute-start(f32[2,256,128]{2,1,0:T(8,128)S(1)} %get-tuple-element.58), channel_id=1, source_target_pairs={{0,7},{1,0},{2,1},{3,2},{4,3},{5,4},{6,5},{7,6},{8,15},{9,8},{10,9... | collective-permute-start | bytes 786440 | tf_op jit(solution)/shard_map/ppermute | solution.py:32
  12.1 19.2 %collective-permute-start = (f32[32,1024]{1,0:T(8,128)S(1)}, f32[32,1024]{1,0:T(8,128)S(1)}, u32[]{:S(2)}, u32[]{:S(2)}) collective-permute-start(f32[32,1024]{1,0:T(8,128)S(1)} %get-tuple-element.56), channel_id=1, source_target_pairs={{0,8},{8,16},{16,24},{24,0},{1,9},{9,17},{17,25},{25,1},{2,10},{10... | collective-permute-start | bytes 393224 | tf_op jit(solution)/shard_map/ppermute | solution.py:32
  12.2 19.3 %collective-permute-start.1 = (f32[32,1024]{1,0:T(8,128)S(1)}, f32[32,1024]{1,0:T(8,128)S(1)}, u32[]{:S(2)}, u32[]{:S(2)}) collective-permute-start(f32[32,1024]{1,0:T(8,128)S(1)} %get-tuple-element.56), channel_id=1, source_target_pairs={{0,24},{8,0},{16,8},{24,16},{1,25},{9,1},{17,9},{25,17},{2,26},{10... | collective-permute-start | bytes 393224 | tf_op jit(solution)/shard_map/ppermute | solution.py:32
  13.9 0.9 copy-start.2
  31.4 15.6 %collective-permute-start.7 = (f32[3,32,1024]{2,1,0:T(8,128)S(1)}, f32[3,32,1024]{2,1,0:T(8,128)S(1)}, u32[]{:S(2)}, u32[]{:S(2)}) collective-permute-start(f32[3,32,1024]{2,1,0:T(8,128)S(1)} %get-tuple-element.68), channel_id=1, source_target_pairs={{0,8},{8,16},{16,24},{24,0},{1,9},{9,17},{17,25},{25,1},{2,10},{10... | collective-permute-start | bytes 1179656 | tf_op jit(solution)/shard_map/ppermute | solution.py:32
  31.5 20.3 %collective-permute-start.8 = (f32[3,32,1024]{2,1,0:T(8,128)S(1)}, f32[3,32,1024]{2,1,0:T(8,128)S(1)}, u32[]{:S(2)}, u32[]{:S(2)}) collective-permute-start(f32[3,32,1024]{2,1,0:T(8,128)S(1)} %get-tuple-element.68), channel_id=1, source_target_pairs={{0,24},{8,0},{16,8},{24,16},{1,25},{9,1},{17,9},{25,17},{2,26},{10... | collective-permute-start | bytes 1179656 | tf_op jit(solution)/shard_map/ppermute | solution.py:32
  33.3 19.0 %copy-start.3 = (bf16[256,128]{1,0:T(8,128)(2,1)S(1)}, bf16[256,128]{1,0:T(8,128)(2,1)}, u32[]{:S(2)}) copy-start(bf16[256,128]{1,0:T(8,128)(2,1)} %constant.73.clone.table) | copy-start | bytes 196612
  45.3 42.4 %copy-start = (f32[258,48,128]{2,1,0:T(8,128)}, f32[258,48,128]{2,1,0:T(8,128)S(1)}, u32[]{:S(2)}) copy-start(f32[258,48,128]{2,1,0:T(8,128)S(1)} %get-tuple-element.88.refs_9_) | copy-start | bytes 19021828
  45.3 7.7 %collective-permute-start.6 = (f32[32,1024]{1,0:T(8,128)S(1)}, f32[32,1024]{1,0:T(8,128)S(1)}, u32[]{:S(2)}, u32[]{:S(2)}) collective-permute-start(f32[32,1024]{1,0:T(8,128)S(1)} %get-tuple-element.65), channel_id=1, source_target_pairs={{0,8},{8,16},{16,24},{24,0},{1,9},{9,17},{17,25},{25,1},{2,10},{10... | collective-permute-start | bytes 393224 | tf_op jit(solution)/shard_map/ppermute | solution.py:32
  45.3 28.5 %collective-permute-start.9 = (f32[32,1024]{1,0:T(8,128)S(1)}, f32[32,1024]{1,0:T(8,128)S(1)}, u32[]{:S(2)}, u32[]{:S(2)}) collective-permute-start(f32[32,1024]{1,0:T(8,128)S(1)} %get-tuple-element.65), channel_id=1, source_target_pairs={{0,24},{8,0},{16,8},{24,16},{1,25},{9,1},{17,9},{25,17},{2,26},{10... | collective-permute-start | bytes 393224 | tf_op jit(solution)/shard_map/ppermute | solution.py:32
  47.1 15.1 %collective-permute-start.4 = (f32[256,128]{1,0:T(8,128)S(1)}, f32[256,128]{1,0:T(8,128)S(1)}, u32[]{:S(2)}, u32[]{:S(2)}) collective-permute-start(f32[256,128]{1,0:T(8,128)S(1)} %get-tuple-element.63), channel_id=1, source_target_pairs={{0,1},{1,2},{2,3},{3,4},{4,5},{5,6},{6,7},{7,0},{8,9},{9,10},{10,1... | collective-permute-start | bytes 393224 | tf_op jit(solution)/shard_map/ppermute | solution.py:32
  47.1 17.6 %collective-permute-start.5 = (f32[256,128]{1,0:T(8,128)S(1)}, f32[256,128]{1,0:T(8,128)S(1)}, u32[]{:S(2)}, u32[]{:S(2)}) collective-permute-start(f32[256,128]{1,0:T(8,128)S(1)} %get-tuple-element.64), channel_id=1, source_target_pairs={{0,7},{1,0},{2,1},{3,2},{4,3},{5,4},{6,5},{7,6},{8,15},{9,8},{10,9... | collective-permute-start | bytes 393224 | tf_op jit(solution)/shard_map/ppermute | solution.py:32
  51.8 39.2 %collective-permute-start.16 = (f32[3,256,128]{2,1,0:T(8,128)S(1)}, f32[3,256,128]{2,1,0:T(8,128)S(1)}, u32[]{:S(2)}, u32[]{:S(2)}) collective-permute-start(f32[3,256,128]{2,1,0:T(8,128)S(1)} %get-tuple-element.82), channel_id=1, source_target_pairs={{0,1},{1,2},{2,3},{3,4},{4,5},{5,6},{6,7},{7,0},{8,9},{9,10},{10,1... | collective-permute-start | bytes 1179656 | tf_op jit(solution)/shard_map/ppermute | solution.py:32
  52.9 42.9 %collective-permute-start.17 = (f32[3,256,128]{2,1,0:T(8,128)S(1)}, f32[3,256,128]{2,1,0:T(8,128)S(1)}, u32[]{:S(2)}, u32[]{:S(2)}) collective-permute-start(f32[3,256,128]{2,1,0:T(8,128)S(1)} %get-tuple-element.83), channel_id=1, source_target_pairs={{0,7},{1,0},{2,1},{3,2},{4,3},{5,4},{6,5},{7,6},{8,15},{9,8},{10,9... | collective-permute-start | bytes 1179656 | tf_op jit(solution)/shard_map/ppermute | solution.py:32
  62.2 25.7 %collective-permute-start.10 = (f32[3,256,128]{2,1,0:T(8,128)S(1)}, f32[3,256,128]{2,1,0:T(8,128)S(1)}, u32[]{:S(2)}, u32[]{:S(2)}) collective-permute-start(f32[3,256,128]{2,1,0:T(8,128)S(1)} %get-tuple-element.77), channel_id=1, source_target_pairs={{0,1},{1,2},{2,3},{3,4},{4,5},{5,6},{6,7},{7,0},{8,9},{9,10},{10,1... | collective-permute-start | bytes 1179656 | tf_op jit(solution)/shard_map/ppermute | solution.py:32
  64.7 24.4 %collective-permute-start.11 = (f32[3,256,128]{2,1,0:T(8,128)S(1)}, f32[3,256,128]{2,1,0:T(8,128)S(1)}, u32[]{:S(2)}, u32[]{:S(2)}) collective-permute-start(f32[3,256,128]{2,1,0:T(8,128)S(1)} %get-tuple-element.78), channel_id=1, source_target_pairs={{0,7},{1,0},{2,1},{3,2},{4,3},{5,4},{6,5},{7,6},{8,15},{9,8},{10,9... | collective-permute-start | bytes 1179656 | tf_op jit(solution)/shard_map/ppermute | solution.py:32
  89.0 15.6 %collective-permute-start.14 = (f32[32,1024]{1,0:T(8,128)S(1)}, f32[32,1024]{1,0:T(8,128)S(1)}, u32[]{:S(2)}, u32[]{:S(2)}) collective-permute-start(f32[32,1024]{1,0:T(8,128)S(1)} %get-tuple-element.81), channel_id=1, source_target_pairs={{0,8},{8,16},{16,24},{24,0},{1,9},{9,17},{17,25},{25,1},{2,10},{10... | collective-permute-start | bytes 393224 | tf_op jit(solution)/shard_map/ppermute | solution.py:32
  89.0 15.6 %collective-permute-start.15 = (f32[32,1024]{1,0:T(8,128)S(1)}, f32[32,1024]{1,0:T(8,128)S(1)}, u32[]{:S(2)}, u32[]{:S(2)}) collective-permute-start(f32[32,1024]{1,0:T(8,128)S(1)} %get-tuple-element.81), channel_id=1, source_target_pairs={{0,24},{8,0},{16,8},{24,16},{1,25},{9,1},{17,9},{25,17},{2,26},{10... | collective-permute-start | bytes 393224 | tf_op jit(solution)/shard_map/ppermute | solution.py:32
  90.8 13.8 %collective-permute-start.12 = (f32[256,128]{1,0:T(8,128)S(1)}, f32[256,128]{1,0:T(8,128)S(1)}, u32[]{:S(2)}, u32[]{:S(2)}) collective-permute-start(f32[256,128]{1,0:T(8,128)S(1)} %get-tuple-element.79), channel_id=1, source_target_pairs={{0,1},{1,2},{2,3},{3,4},{4,5},{5,6},{6,7},{7,0},{8,9},{9,10},{10,1... | collective-permute-start | bytes 393224 | tf_op jit(solution)/shard_map/ppermute | solution.py:32
  91.0 13.6 %collective-permute-start.13 = (f32[256,128]{1,0:T(8,128)S(1)}, f32[256,128]{1,0:T(8,128)S(1)}, u32[]{:S(2)}, u32[]{:S(2)}) collective-permute-start(f32[256,128]{1,0:T(8,128)S(1)} %get-tuple-element.80), channel_id=1, source_target_pairs={{0,7},{1,0},{2,1},{3,2},{4,3},{5,4},{6,5},{7,6},{8,15},{9,8},{10,9... | collective-permute-start | bytes 393224 | tf_op jit(solution)/shard_map/ppermute | solution.py:32
  95.5 9.1 %slice-start = ((s8[6340608]{0:T(1024)(128)(4,1)}), s8[2146304]{0:T(1024)(128)(4,1)S(1)}, s32[]{:S(2)}) async-start(s8[6340608]{0:T(1024)(128)(4,1)} %bitcast.34), calls=%async_computation.2 | async-start | bytes 4292608
  95.8 8.8 %slice-start.1 = ((s8[6340608]{0:T(1024)(128)(4,1)}), s8[4194304]{0:T(1024)(128)(4,1)S(1)}, s32[]{:S(2)}) async-start(s8[6340608]{0:T(1024)(128)(4,1)} %bitcast.34), calls=%async_computation.3 | async-start | bytes 8388608
  95.8 8.8 %copy-start.4 = (bf16[256,32]{1,0:T(8,128)(2,1)S(1)}, bf16[256,32]{1,0:T(8,128)(2,1)}, u32[]{:S(2)}) copy-start(bf16[256,32]{1,0:T(8,128)(2,1)} %constant.74.clone.refs_12_) | copy-start | bytes 49156
  104.7 19.0 %copy-start.6 = (f32[64,64,1,1]{1,0,3,2:T(8,128)S(1)}, f32[64,64,1,1]{1,0,3,2:T(8,128)}, u32[]{:S(2)}) copy-start(f32[64,64,1,1]{1,0,3,2:T(8,128)} %constant.84) | copy-start | bytes 49156
  104.7 24.7 %copy-start.9 = (f32[64]{0:T(128)S(1)}, f32[64]{0:T(128)}, u32[]{:S(2)}) copy-start(f32[64]{0:T(128)} %constant.77.clone) | copy-start | bytes 772
  104.7 35.7 %copy-start.7 = (f32[64,64,1]{1,0,2:T(8,128)S(1)}, f32[64,64,1]{1,0,2:T(8,128)}, u32[]{:S(2)}) copy-start(f32[64,64,1]{1,0,2:T(8,128)} %constant.85) | copy-start | bytes 49156
  104.7 36.1 %copy-start.8 = (f32[128,128,1]{1,0,2:T(8,128)S(1)}, f32[128,128,1]{1,0,2:T(8,128)}, u32[]{:S(2)}) copy-start(f32[128,128,1]{1,0,2:T(8,128)} %constant.86) | copy-start | bytes 196612
  104.7 36.1 %copy-start.10 = (f32[128]{0:T(128)S(1)}, f32[128]{0:T(128)}, u32[]{:S(2)}) copy-start(f32[128]{0:T(128)} %constant.78.clone) | copy-start | bytes 1540
  126.4 30.6 %copy-start.5 = (bf16[64,128]{1,0:T(8,128)(2,1)S(1)}, bf16[64,128]{1,0:T(8,128)(2,1)}, u32[]{:S(2)}) copy-start(bf16[64,128]{1,0:T(8,128)(2,1)} %constant.79.clone.refs_2_) | copy-start | bytes 49156
  126.4 11.3 %all-to-all-start = ((f32[32,1,1536]{2,1,0:T(1,128)}), f32[32,1,1536]{2,1,0:T(1,128)S(1)}, u32[]{:S(2)}, u32[]{:S(2)}) async-start(f32[32,1,1536]{2,1,0:T(1,128)} %reshape.69), calls=%async_computation | async-start | bytes 393216 | tf_op jit(solution)/shard_map/all_to_all | solution.py:737

commit v3 on v2

--- a/solution.py
+++ b/solution.py
@@ -59,8 +59,8 @@
 
 
 def z_sides(value, rim, lane):
-    before = turn(jnp.where(lane == LANES - 1, rim, value), 1)
-    after = turn(jnp.where(lane == 0, rim, value), -1)
+    before = jnp.where(lane == 0, rim, turn(value, 1))
+    after = jnp.where(lane == LANES - 1, rim, turn(value, -1))
     return before, after
 
 
@@ -151,7 +151,7 @@
         both = jnp.where(spot < 2, turned_to(a, GROUP * i + 1), turned_to(b, GROUP * i + 3))
         return jnp.where(owner == i, both, edge)
 
-    packed[...] = planes_loop(PART, plane, jnp.zeros((rows, LANES), jnp.float32), 16)
+    packed[...] = planes_loop(PART, plane, jnp.zeros((rows, LANES), jnp.float32), 32)
 
 
 def state_rims(first, second):
@@ -366,7 +366,7 @@
                 out[d, base + i, rows - 8 :] = value[rows - 8 :] + last
             return carry
 
-        planes_loop(PART, plane, 0, 16)
+        planes_loop(PART, plane, 0, 32)
 
 
 def edges_pass(filtered, low, high, low_curve, high_curve, lanes):
@@ -443,6 +443,11 @@
         pad[i + 1, pl.ds(TOP + 1, rows)] - pad[i + 1, pl.ds(TOP - 1, rows)],
         slope,
     )
+
+
+def crossed_rims(left, right, rows):
+    rims = merged_rims(left, right, rows)
+    return jnp.where(lane_of(rows) % 2 == 0, turn(rims, -1), turn(rims, 1))
 
 
 def merged_rims(left, right, rows):
@@ -515,7 +520,7 @@
     base = pl.program_id(0) * PART
     lane = lane_of(rows)
     owner = lane // GROUP
-    rims = merged_rims(left, right, rows)
+    rims = crossed_rims(left, right, rows)
 
     def lanes_part(i, carry):
         value = state[base + i]
@@ -524,7 +529,7 @@
         across[i] = (STEP * speed) * jnp.where(speed > 0.0, value - before, after - value)
         return carry
 
-    planes_loop(PART, lanes_part)
+    planes_loop(PART, lanes_part, 0, 16)
 
     def plane(i, edge):
         value = state[base + i]
@@ -585,18 +590,18 @@
     base = pl.program_id(0) * PART
     lane = lane_of(rows)
     row = lax.broadcasted_iota(jnp.int32, (rows, LANES), 0)
-    ends = merged_rims(flow_left, flow_right, rows)
+    ends = crossed_rims(flow_left, flow_right, rows)
 
     def across(i, carry):
         value = adjoint[base + i]
         speed = velocity[2, i]
         rim = turned_from(ends, GROUP * i + 1)
-        flows[i] = turn(jnp.where(lane == 0, rim, jnp.maximum(speed, 0.0) * value), -1) - turn(
-            jnp.where(lane == LANES - 1, rim, jnp.minimum(speed, 0.0) * value), 1
-        )
+        later = turn(jnp.maximum(speed, 0.0) * value, -1)
+        prev = turn(jnp.minimum(speed, 0.0) * value, 1)
+        flows[i] = jnp.where(lane == LANES - 1, rim, later) - jnp.where(lane == 0, rim, prev)
         return carry
 
-    planes_loop(PART, across)
+    planes_loop(PART, across, 0, 16)
 
     def plane(i, carry):
         g0 = gradients(pad0, slopes[base + i, :, :LANES], base + i, rows)
@@ -797,16 +802,21 @@
     s_below = shifted(s_high, "gy", 1)
     s_above = shifted(s_low, "gy", -1)
 
+    inc_left, inc_right, inc_lows, inc_highs = lax.optimization_barrier(
+        (inc_left, inc_right, inc_lows, inc_highs)
+    )
     low_curve, high_curve = corners(low_curve, high_curve, inc_left, inc_right)
-    s_left, low_curve, high_curve = lax.optimization_barrier((s_left, low_curve, high_curve))
+    s_left, s_right, s_below, s_above, low_curve, high_curve = lax.optimization_barrier(
+        (s_left, s_right, s_below, s_above, low_curve, high_curve)
+    )
     low_curves = shifted(high_curve, "gy", 1)
     high_curves = shifted(low_curve, "gy", -1)
 
     f_packed, f_low, f_high, adjoint = second_state(
         velocity, source, state, s_below, s_above, s_left, s_right
     )
-    f_packed, f_low, f_high, low_curves, high_curves = lax.optimization_barrier(
-        (f_packed, f_low, f_high, low_curves, high_curves)
+    f_packed, low_curves, high_curves = lax.optimization_barrier(
+        (f_packed, low_curves, high_curves)
     )
     f_left = shifted(f_packed, "gz", 1)
     f_right = shifted(f_packed, "gz", -1)

time: 169 us -> 153 us (0.905)
  starting transfers between devices: 42 us -> 35.1 us
  Pallas kernels: 88.2 us -> 82.1 us
  waiting for transfers between devices: 13.4 us -> 10.3 us
    ppermute x18, starting transfers between devices: 39.1 us -> 32.2 us  [shifted(): lax.ppermute(value, axis, [(i, (i + by) % peers) for i in range(peers)])]
    pallas_call x7, Pallas kernels: 87.6 us -> 81.6 us  [call(): pl.pallas_call(kernel, in_specs=[far] * counts[0] + [near] * counts[1], o...]
    ppermute x18, waiting for transfers between devices: 5.31 us -> 2.19 us  [shifted(): lax.ppermute(value, axis, [(i, (i + by) % peers) for i in range(peers)])]
where the time goes in v3:
time: 153 us
  Pallas kernels  82.1 us (54%)
  starting transfers between devices  35.1 us (23%)
  blocking collectives  11.3 us (7%)
  waiting for transfers between devices  10.3 us (7%)
  local copies, waits for them, and re-layouts  6.19 us (4%)
  matrix products  4.07 us (3%)
  other arithmetic  2.95 us (2%)
    pallas_call x7, Pallas kernels, call(): pl.pallas_call(kernel, in_specs=[far] * counts[0] + [near] * counts[1], o...  81.6 us
    ppermute x18, starting transfers between devices, shifted(): lax.ppermute(value, axis, [(i, (i + by) % peers) for i in range(peers)])  32.2 us
    all_to_all x1, blocking collectives, coarse_spread(): coeffs = lax.all_to_all(planes, both, 0, 0, tiled=True)[:3 * cxlen]  11.3 us
    all_to_all x1, waiting for transfers between devices, coarse_spread(): planes = lax.all_to_all(coeffs, both, 0, 0, tiled=True)  8.1 us
  transfers between devices with their start and end apart: 19, of which 3 were waited for; matrix products, arithmetic and copies ran while one was open for 1% of the time, Pallas kernels for 31%

profile of v3, /device:TPU:0, one launch (start us, length us, event | category | flops | bytes accessed | tf_op | source)
XLA Modules:
  0.0 152.6 jit_solution(10765613545790902198)
XLA Ops:
  0.0 5.6 %shard_map.145 = (f32[32,1024]{1,0:T(8,128)S(1)}, f32[2,256,128]{2,1,0:T(8,128)S(1)}, f32[2,256,128]{2,1,0:T(8,128)S(1)}) custom-call(bf16[256,32,128]{2,1,0:T(8,128)(2,1)} %refs_3_.1, bf16[256,32,128]{2,1,0:T(8,128)(2,1)} %refs_6_.1), custom_call_target="tpu_custom_call" | custom-call | flops 8388608 | bytes 4194304 | tf_op jit(solution)/shard_map/pallas_call | solution.py:122
  5.6 3.0 %collective-permute-start.2 = (f32[2,256,128]{2,1,0:T(8,128)S(1)}, f32[2,256,128]{2,1,0:T(8,128)S(1)}, u32[]{:S(2)}, u32[]{:S(2)}) collective-permute-start(f32[2,256,128]{2,1,0:T(8,128)S(1)} %get-tuple-element.62), channel_id=1, source_target_pairs={{0,1},{1,2},{2,3},{3,4},{4,5},{5,6},{6,7},{7,0},{8,9},{9,10},{10,1... | collective-permute-start | bytes 786440 | tf_op jit(solution)/shard_map/ppermute | solution.py:32
  8.6 3.1 %collective-permute-start.3 = (f32[2,256,128]{2,1,0:T(8,128)S(1)}, f32[2,256,128]{2,1,0:T(8,128)S(1)}, u32[]{:S(2)}, u32[]{:S(2)}) collective-permute-start(f32[2,256,128]{2,1,0:T(8,128)S(1)} %get-tuple-element.63), channel_id=1, source_target_pairs={{0,7},{1,0},{2,1},{3,2},{4,3},{5,4},{6,5},{7,6},{8,15},{9,8},{10,9... | collective-permute-start | bytes 786440 | tf_op jit(solution)/shard_map/ppermute | solution.py:32
  11.7 1.7 %collective-permute-start.1 = (f32[32,1024]{1,0:T(8,128)S(1)}, f32[32,1024]{1,0:T(8,128)S(1)}, u32[]{:S(2)}, u32[]{:S(2)}) collective-permute-start(f32[32,1024]{1,0:T(8,128)S(1)} %get-tuple-element.61), channel_id=1, source_target_pairs={{0,24},{8,0},{16,8},{24,16},{1,25},{9,1},{17,9},{25,17},{2,26},{10... | collective-permute-start | bytes 393224 | tf_op jit(solution)/shard_map/ppermute | solution.py:32
  13.5 0.9 copy-done.2
  14.4 16.6 %shard_map.146 = (f32[3,32,1024]{2,1,0:T(8,128)S(1)}, f32[3,256,128]{2,1,0:T(8,128)S(1)}, f32[3,256,128]{2,1,0:T(8,128)S(1)}, f32[3,256,128]{2,1,0:T(8,128)S(1)}...) custom-call(f32[3,256,32,128]{3,2,1,0:T(8,128)} %refs_0_.7, f32[3,256,32,128]{3,2,1,0:T(8,128)} %refs_0_.7, ...), custom_call_target="tpu_custom_call" | custom-call | flops 75497472 | bytes 12582912 | tf_op jit(solution)/shard_map/pallas_call | solution.py:122
  31.1 1.7 %collective-permute-start.9 = (f32[3,32,1024]{2,1,0:T(8,128)S(1)}, f32[3,32,1024]{2,1,0:T(8,128)S(1)}, u32[]{:S(2)}, u32[]{:S(2)}) collective-permute-start(f32[3,32,1024]{2,1,0:T(8,128)S(1)} %get-tuple-element.73), channel_id=1, source_target_pairs={{0,24},{8,0},{16,8},{24,16},{1,25},{9,1},{17,9},{25,17},{2,26},{10... | collective-permute-start | bytes 1179656 | tf_op jit(solution)/shard_map/ppermute | solution.py:32
  32.8 4.7 %collective-permute-start.11 = (f32[3,256,128]{2,1,0:T(8,128)S(1)}, f32[3,256,128]{2,1,0:T(8,128)S(1)}, u32[]{:S(2)}, u32[]{:S(2)}) collective-permute-start(f32[3,256,128]{2,1,0:T(8,128)S(1)} %get-tuple-element.75), channel_id=1, source_target_pairs={{0,7},{1,0},{2,1},{3,2},{4,3},{5,4},{6,5},{7,6},{8,15},{9,8},{10,9... | collective-permute-start | bytes 1179656 | tf_op jit(solution)/shard_map/ppermute | solution.py:32
  37.5 12.0 %shard_map.147 = (f32[32,1024]{1,0:T(8,128)S(1)}, f32[256,128]{1,0:T(8,128)S(1)}, f32[256,128]{1,0:T(8,128)S(1)}, f32[256,32,128]{2,1,0:T(8,128)S(1)}, f32[256,3...) custom-call(f32[3,256,32,128]{3,2,1,0:T(8,128)} %refs_0_.7, ...), custom_call_target="tpu_custom_call" | custom-call | flops 25165824 | bytes 16777216 | tf_op jit(solution)/shard_map/pallas_call | solution.py:122
  49.6 1.7 %collective-permute-start.5 = (f32[32,1024]{1,0:T(8,128)S(1)}, f32[32,1024]{1,0:T(8,128)S(1)}, u32[]{:S(2)}, u32[]{:S(2)}) collective-permute-start(f32[32,1024]{1,0:T(8,128)S(1)} %get-tuple-element.68), channel_id=1, source_target_pairs={{0,24},{8,0},{16,8},{24,16},{1,25},{9,1},{17,9},{25,17},{2,26},{10... | collective-permute-start | bytes 393224 | tf_op jit(solution)/shard_map/ppermute | solution.py:32
  51.4 4.7 %collective-permute-start.7 = (f32[256,128]{1,0:T(8,128)S(1)}, f32[256,128]{1,0:T(8,128)S(1)}, u32[]{:S(2)}, u32[]{:S(2)}) collective-permute-start(f32[256,128]{1,0:T(8,128)S(1)} %get-tuple-element.70), channel_id=1, source_target_pairs={{0,7},{1,0},{2,1},{3,2},{4,3},{5,4},{6,5},{7,6},{8,15},{9,8},{10,9... | collective-permute-start | bytes 393224 | tf_op jit(solution)/shard_map/ppermute | solution.py:32
  56.2 0.2 fusion.22
  56.5 0.2 fusion.13
  56.7 0.2 fusion.20
  56.9 0.5 shard_map.148
  57.5 2.1 %collective-permute-done.6.refs_1_ = f32[256,128]{1,0:T(8,128)S(1)} collective-permute-done((f32[256,128]{1,0:T(8,128)S(1)}, f32[256,128]{1,0:T(8,128)S(1)}, u32[]{:S(2)}, u32[]{:S(2)}) %collective-permute-start.6) | collective-permute-done | bytes 131104 | tf_op jit(solution)/shard_map/ppermute | solution.py:32
  59.7 0.2 collective-permute-start.14
  59.9 4.5 %collective-permute-start.15 = (f32[3,256,128]{2,1,0:T(8,128)S(1)}, f32[3,256,128]{2,1,0:T(8,128)S(1)}, u32[]{:S(2)}, u32[]{:S(2)}) collective-permute-start(f32[3,256,128]{2,1,0:T(8,128)S(1)} %get-tuple-element.90), channel_id=1, source_target_pairs={{0,7},{1,0},{2,1},{3,2},{4,3},{5,4},{6,5},{7,6},{8,15},{9,8},{10,9... | collective-permute-start | bytes 1179656 | tf_op jit(solution)/shard_map/ppermute | solution.py:32
  64.4 12.1 %shard_map.149 = (f32[32,1024]{1,0:T(8,128)S(1)}, f32[256,128]{1,0:T(8,128)S(1)}, f32[256,128]{1,0:T(8,128)S(1)}, f32[256,32,128]{2,1,0:T(8,128)S(1)}) custom-call(f32[3,256,32,128]{3,2,1,0:T(8,128)} %refs_2_.6, f32[256,128]{1,0:T(8,128)S(1)} %collective-permute-done.6.refs_1_, ...), custom_call_target="tpu_custom_call", output_to_operand_aliasing={{3}: (6, {})} | custom-call | flops 31457280 | bytes 12582912 | tf_op jit(solution)/shard_map/pallas_call | solution.py:122
  76.6 4.7 %collective-permute-start.13 = (f32[256,128]{1,0:T(8,128)S(1)}, f32[256,128]{1,0:T(8,128)S(1)}, u32[]{:S(2)}, u32[]{:S(2)}) collective-permute-start(f32[256,128]{1,0:T(8,128)S(1)} %get-tuple-element.87), channel_id=1, source_target_pairs={{0,7},{1,0},{2,1},{3,2},{4,3},{5,4},{6,5},{7,6},{8,15},{9,8},{10,9... | collective-permute-start | bytes 393224 | tf_op jit(solution)/shard_map/ppermute | solution.py:32
  81.4 0.2 fusion.25
  81.7 1.7 %collective-permute-start.17 = (f32[32,1024]{1,0:T(8,128)S(1)}, f32[32,1024]{1,0:T(8,128)S(1)}, u32[]{:S(2)}, u32[]{:S(2)}) collective-permute-start(f32[32,1024]{1,0:T(8,128)S(1)} %get-tuple-element.91), channel_id=1, source_target_pairs={{0,24},{8,0},{16,8},{24,16},{1,25},{9,1},{17,9},{25,17},{2,26},{10... | collective-permute-start | bytes 393224 | tf_op jit(solution)/shard_map/ppermute | solution.py:32
  83.4 0.3 fusion.9.refs_4_
  83.7 6.3 %shard_map.150.refs_7_ = f32[3,256,32,128]{3,2,1,0:T(8,128)S(1)} custom-call(f32[3,256,128]{2,1,0:T(8,128)S(1)} %collective-permute-done.10.refs_0_, f32[3,256,128]{2,1,0:T(8,128)S(1)} %collective-permute-done.11.refs_1_, f32[3,256,128]{2,1,0:T(8,128)S(1)} %collective-permute-done.14.refs_2_, ...), custom_call_target="tpu_custom_call", output_to_operand_aliasing={{}: (5, {})} | custom-call | flops 12582912 | bytes 3145728 | tf_op jit(solution)/shard_map/pallas_call | solution.py:122
  90.2 17.4 %shard_map.151 = (f32[3,256,32,128]{3,2,1,0:T(8,128)}, f32[3,512,32]{2,1,0:T(8,128)S(1)}) custom-call(f32[3,256,32,128]{3,2,1,0:T(8,128)} %refs_2_.6, f32[3,256,32,128]{3,2,1,0:T(8,128)} %refs_2_.6, f32[3,256,32,128]{3,2,1,0:T(8,128)} %refs_2_.6, f32[256,128]{1,0:T(8,128)S(1)} %collective-permute-done.12.refs_3_, ...), custom_call_target="tpu_custom_call" | custom-call | flops 73400320 | bytes 25165824 | tf_op jit(solution)/shard_map/pallas_call | solution.py:122
  107.6 1.4 convolution_bitcast_fusion
  109.0 0.3 copy.44
  109.4 1.0 reshape.69
  110.4 2.9 %all-to-all-start = ((f32[32,1,1536]{2,1,0:T(1,128)}), f32[32,1,1536]{2,1,0:T(1,128)S(1)}, u32[]{:S(2)}, u32[]{:S(2)}) async-start(f32[32,1,1536]{2,1,0:T(1,128)} %reshape.69), calls=%async_computation | async-start | bytes 393216 | tf_op jit(solution)/shard_map/all_to_all | solution.py:742
  113.5 8.1 %all-to-all-done = f32[32,1,1536]{2,1,0:T(1,128)S(1)} async-done(((f32[32,1,1536]{2,1,0:T(1,128)}), f32[32,1,1536]{2,1,0:T(1,128)S(1)}, u32[]{:S(2)}, u32[]{:S(2)}) %all-to-all-start) | async-done | bytes 196640 | tf_op jit(solution)/shard_map/all_to_all | solution.py:742
  121.6 0.5 broadcast.57
  122.2 1.1 reduce
  123.3 0.2 reshape.70
  123.5 0.5 copy.38
  124.0 0.4 reshape.61
  124.4 0.3 convolution_bitcast_fusion.2
  124.7 0.3 convolution_divide_fusion
  125.1 0.3 fusion.26
  125.4 0.3 convolution_bitcast_fusion.1
  125.7 0.3 reshape.62
  126.2 0.4 reshape.71
  126.5 11.3 %all_to_all.10 = f32[32,1,1536]{2,1,0:T(1,128)S(1)} all-to-all(f32[32,1,1536]{2,1,0:T(1,128)S(1)} %reshape.71), channel_id=1, replica_groups=mesh['gz'=4,'gy'=8] {'gz','gy'}, dimensions={0} | all-to-all | bytes 393216 | tf_op jit(solution)/shard_map/all_to_all | solution.py:757
  137.8 1.1 reduce.1
  138.9 0.2 reshape.72
  139.2 1.4 fusion
  140.6 0.3 copy.42
  140.9 0.1 bitcast_subtract_fusion.refs_0_
  141.0 11.6 %shard_map.152 = f32[3,256,32,128]{3,2,1,0:T(8,128)} custom-call(f32[3,512,32]{2,1,0:T(8,128)S(1)} %bitcast_subtract_fusion.refs_0_, f32[3,256,32,128]{3,2,1,0:T(8,128)} %get-tuple-element.102.refs_1_, bf16[64,128]{1,0:T(8,128)(2,1)S(1)} %copy-done.5), custom_call_target="tpu_custom_call" | custom-call | flops 6291456 | bytes 25165824 | tf_op jit(solution)/shard_map/pallas_call | solution.py:122
  (63 shorter events, 1.1 us)
Async XLA Ops:
  5.6 32.0 %copy-start.1 = (bf16[384,256]{1,0:T(8,128)(2,1)S(1)}, bf16[384,256]{1,0:T(8,128)(2,1)}, u32[]{:S(2)}) copy-start(bf16[384,256]{1,0:T(8,128)(2,1)} %constant.72.clone.refs_11_) | copy-start | bytes 589828
  5.6 25.4 %collective-permute-start.2 = (f32[2,256,128]{2,1,0:T(8,128)S(1)}, f32[2,256,128]{2,1,0:T(8,128)S(1)}, u32[]{:S(2)}, u32[]{:S(2)}) collective-permute-start(f32[2,256,128]{2,1,0:T(8,128)S(1)} %get-tuple-element.62), channel_id=1, source_target_pairs={{0,1},{1,2},{2,3},{3,4},{4,5},{5,6},{6,7},{7,0},{8,9},{9,10},{10,1... | collective-permute-start | bytes 786440 | tf_op jit(solution)/shard_map/ppermute | solution.py:32
  8.6 22.4 %collective-permute-start.3 = (f32[2,256,128]{2,1,0:T(8,128)S(1)}, f32[2,256,128]{2,1,0:T(8,128)S(1)}, u32[]{:S(2)}, u32[]{:S(2)}) collective-permute-start(f32[2,256,128]{2,1,0:T(8,128)S(1)} %get-tuple-element.63), channel_id=1, source_target_pairs={{0,7},{1,0},{2,1},{3,2},{4,3},{5,4},{6,5},{7,6},{8,15},{9,8},{10,9... | collective-permute-start | bytes 786440 | tf_op jit(solution)/shard_map/ppermute | solution.py:32
  11.7 19.2 %collective-permute-start = (f32[32,1024]{1,0:T(8,128)S(1)}, f32[32,1024]{1,0:T(8,128)S(1)}, u32[]{:S(2)}, u32[]{:S(2)}) collective-permute-start(f32[32,1024]{1,0:T(8,128)S(1)} %get-tuple-element.61), channel_id=1, source_target_pairs={{0,8},{8,16},{16,24},{24,0},{1,9},{9,17},{17,25},{25,1},{2,10},{10... | collective-permute-start | bytes 393224 | tf_op jit(solution)/shard_map/ppermute | solution.py:32
  11.7 19.3 %collective-permute-start.1 = (f32[32,1024]{1,0:T(8,128)S(1)}, f32[32,1024]{1,0:T(8,128)S(1)}, u32[]{:S(2)}, u32[]{:S(2)}) collective-permute-start(f32[32,1024]{1,0:T(8,128)S(1)} %get-tuple-element.61), channel_id=1, source_target_pairs={{0,24},{8,0},{16,8},{24,16},{1,25},{9,1},{17,9},{25,17},{2,26},{10... | collective-permute-start | bytes 393224 | tf_op jit(solution)/shard_map/ppermute | solution.py:32
  13.5 0.9 copy-start.2
  31.0 18.6 %collective-permute-start.8 = (f32[3,32,1024]{2,1,0:T(8,128)S(1)}, f32[3,32,1024]{2,1,0:T(8,128)S(1)}, u32[]{:S(2)}, u32[]{:S(2)}) collective-permute-start(f32[3,32,1024]{2,1,0:T(8,128)S(1)} %get-tuple-element.73), channel_id=1, source_target_pairs={{0,8},{8,16},{16,24},{24,0},{1,9},{9,17},{17,25},{25,1},{2,10},{10... | collective-permute-start | bytes 1179656 | tf_op jit(solution)/shard_map/ppermute | solution.py:32
  31.1 20.3 %collective-permute-start.9 = (f32[3,32,1024]{2,1,0:T(8,128)S(1)}, f32[3,32,1024]{2,1,0:T(8,128)S(1)}, u32[]{:S(2)}, u32[]{:S(2)}) collective-permute-start(f32[3,32,1024]{2,1,0:T(8,128)S(1)} %get-tuple-element.73), channel_id=1, source_target_pairs={{0,24},{8,0},{16,8},{24,16},{1,25},{9,1},{17,9},{25,17},{2,26},{10... | collective-permute-start | bytes 1179656 | tf_op jit(solution)/shard_map/ppermute | solution.py:32
  32.8 18.6 %collective-permute-start.10 = (f32[3,256,128]{2,1,0:T(8,128)S(1)}, f32[3,256,128]{2,1,0:T(8,128)S(1)}, u32[]{:S(2)}, u32[]{:S(2)}) collective-permute-start(f32[3,256,128]{2,1,0:T(8,128)S(1)} %get-tuple-element.74), channel_id=1, source_target_pairs={{0,1},{1,2},{2,3},{3,4},{4,5},{5,6},{6,7},{7,0},{8,9},{9,10},{10,1... | collective-permute-start | bytes 1179656 | tf_op jit(solution)/shard_map/ppermute | solution.py:32
  32.8 23.3 %collective-permute-start.11 = (f32[3,256,128]{2,1,0:T(8,128)S(1)}, f32[3,256,128]{2,1,0:T(8,128)S(1)}, u32[]{:S(2)}, u32[]{:S(2)}) collective-permute-start(f32[3,256,128]{2,1,0:T(8,128)S(1)} %get-tuple-element.75), channel_id=1, source_target_pairs={{0,7},{1,0},{2,1},{3,2},{4,3},{5,4},{6,5},{7,6},{8,15},{9,8},{10,9... | collective-permute-start | bytes 1179656 | tf_op jit(solution)/shard_map/ppermute | solution.py:32
  49.5 27.0 %copy-start = (f32[258,48,128]{2,1,0:T(8,128)}, f32[258,48,128]{2,1,0:T(8,128)S(1)}, u32[]{:S(2)}) copy-start(f32[258,48,128]{2,1,0:T(8,128)S(1)} %get-tuple-element.98.refs_9_) | copy-start | bytes 19021828
  49.6 7.3 %copy-start.3 = (bf16[256,128]{1,0:T(8,128)(2,1)S(1)}, bf16[256,128]{1,0:T(8,128)(2,1)}, u32[]{:S(2)}) copy-start(bf16[256,128]{1,0:T(8,128)(2,1)} %constant.73.clone.table) | copy-start | bytes 196612
  49.6 8.0 %collective-permute-start.4 = (f32[32,1024]{1,0:T(8,128)S(1)}, f32[32,1024]{1,0:T(8,128)S(1)}, u32[]{:S(2)}, u32[]{:S(2)}) collective-permute-start(f32[32,1024]{1,0:T(8,128)S(1)} %get-tuple-element.68), channel_id=1, source_target_pairs={{0,8},{8,16},{16,24},{24,0},{1,9},{9,17},{17,25},{25,1},{2,10},{10... | collective-permute-start | bytes 393224 | tf_op jit(solution)/shard_map/ppermute | solution.py:32
  49.6 7.9 %collective-permute-start.5 = (f32[32,1024]{1,0:T(8,128)S(1)}, f32[32,1024]{1,0:T(8,128)S(1)}, u32[]{:S(2)}, u32[]{:S(2)}) collective-permute-start(f32[32,1024]{1,0:T(8,128)S(1)} %get-tuple-element.68), channel_id=1, source_target_pairs={{0,24},{8,0},{16,8},{24,16},{1,25},{9,1},{17,9},{25,17},{2,26},{10... | collective-permute-start | bytes 393224 | tf_op jit(solution)/shard_map/ppermute | solution.py:32
  51.4 8.2 %collective-permute-start.6 = (f32[256,128]{1,0:T(8,128)S(1)}, f32[256,128]{1,0:T(8,128)S(1)}, u32[]{:S(2)}, u32[]{:S(2)}) collective-permute-start(f32[256,128]{1,0:T(8,128)S(1)} %get-tuple-element.69), channel_id=1, source_target_pairs={{0,1},{1,2},{2,3},{3,4},{4,5},{5,6},{6,7},{7,0},{8,9},{9,10},{10,1... | collective-permute-start | bytes 393224 | tf_op jit(solution)/shard_map/ppermute | solution.py:32
  51.4 8.3 %collective-permute-start.7 = (f32[256,128]{1,0:T(8,128)S(1)}, f32[256,128]{1,0:T(8,128)S(1)}, u32[]{:S(2)}, u32[]{:S(2)}) collective-permute-start(f32[256,128]{1,0:T(8,128)S(1)} %get-tuple-element.70), channel_id=1, source_target_pairs={{0,7},{1,0},{2,1},{3,2},{4,3},{5,4},{6,5},{7,6},{8,15},{9,8},{10,9... | collective-permute-start | bytes 393224 | tf_op jit(solution)/shard_map/ppermute | solution.py:32
  59.7 21.9 %collective-permute-start.14 = (f32[3,256,128]{2,1,0:T(8,128)S(1)}, f32[3,256,128]{2,1,0:T(8,128)S(1)}, u32[]{:S(2)}, u32[]{:S(2)}) collective-permute-start(f32[3,256,128]{2,1,0:T(8,128)S(1)} %get-tuple-element.89), channel_id=1, source_target_pairs={{0,1},{1,2},{2,3},{3,4},{4,5},{5,6},{6,7},{7,0},{8,9},{9,10},{10,1... | collective-permute-start | bytes 1179656 | tf_op jit(solution)/shard_map/ppermute | solution.py:32
  59.9 21.7 %collective-permute-start.15 = (f32[3,256,128]{2,1,0:T(8,128)S(1)}, f32[3,256,128]{2,1,0:T(8,128)S(1)}, u32[]{:S(2)}, u32[]{:S(2)}) collective-permute-start(f32[3,256,128]{2,1,0:T(8,128)S(1)} %get-tuple-element.90), channel_id=1, source_target_pairs={{0,7},{1,0},{2,1},{3,2},{4,3},{5,4},{6,5},{7,6},{8,15},{9,8},{10,9... | collective-permute-start | bytes 1179656 | tf_op jit(solution)/shard_map/ppermute | solution.py:32
  76.6 13.5 %collective-permute-start.12 = (f32[256,128]{1,0:T(8,128)S(1)}, f32[256,128]{1,0:T(8,128)S(1)}, u32[]{:S(2)}, u32[]{:S(2)}) collective-permute-start(f32[256,128]{1,0:T(8,128)S(1)} %get-tuple-element.86), channel_id=1, source_target_pairs={{0,1},{1,2},{2,3},{3,4},{4,5},{5,6},{6,7},{7,0},{8,9},{9,10},{10,1... | collective-permute-start | bytes 393224 | tf_op jit(solution)/shard_map/ppermute | solution.py:32
  76.6 13.5 %collective-permute-start.13 = (f32[256,128]{1,0:T(8,128)S(1)}, f32[256,128]{1,0:T(8,128)S(1)}, u32[]{:S(2)}, u32[]{:S(2)}) collective-permute-start(f32[256,128]{1,0:T(8,128)S(1)} %get-tuple-element.87), channel_id=1, source_target_pairs={{0,7},{1,0},{2,1},{3,2},{4,3},{5,4},{6,5},{7,6},{8,15},{9,8},{10,9... | collective-permute-start | bytes 393224 | tf_op jit(solution)/shard_map/ppermute | solution.py:32
  81.6 8.5 %collective-permute-start.16 = (f32[32,1024]{1,0:T(8,128)S(1)}, f32[32,1024]{1,0:T(8,128)S(1)}, u32[]{:S(2)}, u32[]{:S(2)}) collective-permute-start(f32[32,1024]{1,0:T(8,128)S(1)} %get-tuple-element.91), channel_id=1, source_target_pairs={{0,8},{8,16},{16,24},{24,0},{1,9},{9,17},{17,25},{25,1},{2,10},{10... | collective-permute-start | bytes 393224 | tf_op jit(solution)/shard_map/ppermute | solution.py:32
  81.7 8.4 %collective-permute-start.17 = (f32[32,1024]{1,0:T(8,128)S(1)}, f32[32,1024]{1,0:T(8,128)S(1)}, u32[]{:S(2)}, u32[]{:S(2)}) collective-permute-start(f32[32,1024]{1,0:T(8,128)S(1)} %get-tuple-element.91), channel_id=1, source_target_pairs={{0,24},{8,0},{16,8},{24,16},{1,25},{9,1},{17,9},{25,17},{2,26},{10... | collective-permute-start | bytes 393224 | tf_op jit(solution)/shard_map/ppermute | solution.py:32
  83.4 6.7 %slice-start = ((s8[6340608]{0:T(1024)(128)(4,1)}), s8[2146304]{0:T(1024)(128)(4,1)S(1)}, s32[]{:S(2)}) async-start(s8[6340608]{0:T(1024)(128)(4,1)} %bitcast.34), calls=%async_computation.2 | async-start | bytes 4292608
  83.7 6.4 %slice-start.1 = ((s8[6340608]{0:T(1024)(128)(4,1)}), s8[4194304]{0:T(1024)(128)(4,1)S(1)}, s32[]{:S(2)}) async-start(s8[6340608]{0:T(1024)(128)(4,1)} %bitcast.34), calls=%async_computation.3 | async-start | bytes 8388608
  83.7 6.4 %copy-start.4 = (bf16[256,32]{1,0:T(8,128)(2,1)S(1)}, bf16[256,32]{1,0:T(8,128)(2,1)}, u32[]{:S(2)}) copy-start(bf16[256,32]{1,0:T(8,128)(2,1)} %constant.74.clone.refs_12_) | copy-start | bytes 49156
  90.2 17.5 %copy-start.6 = (f32[64,64,1,1]{1,0,3,2:T(8,128)S(1)}, f32[64,64,1,1]{1,0,3,2:T(8,128)}, u32[]{:S(2)}) copy-start(f32[64,64,1,1]{1,0,3,2:T(8,128)} %constant.84) | copy-start | bytes 49156
  90.2 23.1 %copy-start.9 = (f32[64]{0:T(128)S(1)}, f32[64]{0:T(128)}, u32[]{:S(2)}) copy-start(f32[64]{0:T(128)} %constant.77.clone) | copy-start | bytes 772
  90.2 34.2 %copy-start.7 = (f32[64,64,1]{1,0,2:T(8,128)S(1)}, f32[64,64,1]{1,0,2:T(8,128)}, u32[]{:S(2)}) copy-start(f32[64,64,1]{1,0,2:T(8,128)} %constant.85) | copy-start | bytes 49156
  90.2 34.5 %copy-start.8 = (f32[128,128,1]{1,0,2:T(8,128)S(1)}, f32[128,128,1]{1,0,2:T(8,128)}, u32[]{:S(2)}) copy-start(f32[128,128,1]{1,0,2:T(8,128)} %constant.86) | copy-start | bytes 196612
  90.2 34.5 %copy-start.10 = (f32[128]{0:T(128)S(1)}, f32[128]{0:T(128)}, u32[]{:S(2)}) copy-start(f32[128]{0:T(128)} %constant.78.clone) | copy-start | bytes 1540
  110.4 30.6 %copy-start.5 = (bf16[64,128]{1,0:T(8,128)(2,1)S(1)}, bf16[64,128]{1,0:T(8,128)(2,1)}, u32[]{:S(2)}) copy-start(bf16[64,128]{1,0:T(8,128)(2,1)} %constant.79.clone.refs_2_) | copy-start | bytes 49156
  110.4 11.3 %all-to-all-start = ((f32[32,1,1536]{2,1,0:T(1,128)}), f32[32,1,1536]{2,1,0:T(1,128)S(1)}, u32[]{:S(2)}, u32[]{:S(2)}) async-start(f32[32,1,1536]{2,1,0:T(1,128)} %reshape.69), calls=%async_computation | async-start | bytes 393216 | tf_op jit(solution)/shard_map/all_to_all | solution.py:742

commit v4 on v3

--- a/solution.py
+++ b/solution.py
@@ -141,30 +141,34 @@
     owner = lane // GROUP
     spot = lane % GROUP
 
-    def plane(i, edge):
+    def plane(base, part, edge):
+        i = base + part
         a = first[i].astype(jnp.float32)
         b = second[i].astype(jnp.float32)
         low[0, pl.ds(i, 1), :] = a[:1]
         low[1, pl.ds(i, 1), :] = b[:1]
         high[0, pl.ds(i, 1), :] = a[rows - 1 :]
         high[1, pl.ds(i, 1), :] = b[rows - 1 :]
-        both = jnp.where(spot < 2, turned_to(a, GROUP * i + 1), turned_to(b, GROUP * i + 3))
-        return jnp.where(owner == i, both, edge)
-
-    packed[...] = planes_loop(PART, plane, jnp.zeros((rows, LANES), jnp.float32), 32)
+        both = jnp.where(spot < 2, turned_to(a, GROUP * part + 1), turned_to(b, GROUP * part + 3))
+        return jnp.where(owner == part, both, edge)
+
+    for b in range(LONG // PART):
+        packed[:, b * LANES : (b + 1) * LANES] = planes_loop(
+            PART, functools.partial(plane, b * PART), jnp.zeros((rows, LANES), jnp.float32), PART
+        )
 
 
 def state_rims(first, second):
     xlen, rows = first.shape[0], first.shape[1]
-    block = pl.BlockSpec((PART, rows, LANES), lambda i: (i, 0, 0))
-    slab = pl.BlockSpec((2, PART, LANES), lambda i: (0, i, 0))
+    block = pl.BlockSpec((LONG, rows, LANES), lambda i: (i, 0, 0))
+    slab = pl.BlockSpec((2, LONG, LANES), lambda i: (0, i, 0))
     return call(
         state_rims_body,
-        (xlen // PART,),
+        (xlen // LONG,),
         [(first, block), (second, block)],
         [],
         [
-            ((rows, GROUP * xlen), pl.BlockSpec((rows, LANES), lambda i: (0, i))),
+            ((rows, GROUP * xlen), pl.BlockSpec((rows, LONG // PART * LANES), lambda i: (0, i))),
             ((2, xlen, LANES), slab),
             ((2, xlen, LANES), slab),
         ],
@@ -476,7 +480,7 @@
         high[pl.ds(i, 1), :] = one[rows - 1 :]
         return jnp.where(owner == i, turned_to(one, GROUP * i + 1), edge)
 
-    packed[...] = planes_loop(PART, plane, jnp.zeros((rows, LANES), jnp.float32), 16)
+    packed[...] = planes_loop(PART, plane, jnp.zeros((rows, LANES), jnp.float32), 32)
 
 
 def around(array):
@@ -529,7 +533,7 @@
         across[i] = (STEP * speed) * jnp.where(speed > 0.0, value - before, after - value)
         return carry
 
-    planes_loop(PART, lanes_part, 0, 16)
+    planes_loop(PART, lanes_part, 0, 32)
 
     def plane(i, edge):
         value = state[base + i]
@@ -555,7 +559,7 @@
         )
         return jnp.where(owner == i, turned_to(flow, GROUP * i + 1), edge)
 
-    packed[...] = planes_loop(PART, plane, jnp.zeros((rows, LANES), jnp.float32), 16)
+    packed[...] = planes_loop(PART, plane, jnp.zeros((rows, LANES), jnp.float32), 32)
 
 
 def second_state(velocity, source, state, low, high, left, right):
@@ -601,7 +605,7 @@
         flows[i] = jnp.where(lane == LANES - 1, rim, later) - jnp.where(lane == 0, rim, prev)
         return carry
 
-    planes_loop(PART, across, 0, 16)
+    planes_loop(PART, across, 0, 32)
 
     def plane(i, carry):
         g0 = gradients(pad0, slopes[base + i, :, :LANES], base + i, rows)
@@ -628,7 +632,7 @@
             out[d, i] = filtered[d, base + i] + half_one * g0[d] + half_two * g1[d]
         return carry
 
-    planes_loop(PART, plane)
+    planes_loop(PART, plane, 0, 16)
 
     count = PART // 4 * (rows // 4)
     for d in range(3):

time: 153 us -> 150 us (0.980)
  Pallas kernels: 82.1 us -> 75.9 us
  waiting for transfers between devices: 10.3 us -> 13.3 us
    pallas_call x7, Pallas kernels: 81.6 us -> 75.3 us  [call(): pl.pallas_call(kernel, in_specs=[far] * counts[0] + [near] * counts[1], o...]
    ppermute x18, waiting for transfers between devices: 2.19 us -> 5.18 us  [shifted(): lax.ppermute(value, axis, [(i, (i + by) % peers) for i in range(peers)])]
  transfers between devices with their start and end apart: 19 -> 19, of which waited for: 3 -> 5; matrix products, arithmetic and copies ran while one was open for 1% -> 1% of each run, Pallas kernels for 31% -> 30%
where the time goes in v4:
time: 150 us
  Pallas kernels  75.9 us (51%)
  starting transfers between devices  35.4 us (24%)
  waiting for transfers between devices  13.3 us (9%)
  blocking collectives  11.3 us (8%)
  local copies, waits for them, and re-layouts  6.19 us (4%)
  matrix products  4.08 us (3%)
  other arithmetic  2.95 us (2%)
    pallas_call x7, Pallas kernels, call(): pl.pallas_call(kernel, in_specs=[far] * counts[0] + [near] * counts[1], o...  75.3 us
    ppermute x18, starting transfers between devices, shifted(): lax.ppermute(value, axis, [(i, (i + by) % peers) for i in range(peers)])  32.5 us
    all_to_all x1, blocking collectives, coarse_spread(): coeffs = lax.all_to_all(planes, both, 0, 0, tiled=True)[:3 * cxlen]  11.3 us
    all_to_all x1, waiting for transfers between devices, coarse_spread(): planes = lax.all_to_all(coeffs, both, 0, 0, tiled=True)  8.1 us
    ppermute x18, waiting for transfers between devices, shifted(): lax.ppermute(value, axis, [(i, (i + by) % peers) for i in range(peers)])  5.18 us
  transfers between devices with their start and end apart: 19, of which 5 were waited for; matrix products, arithmetic and copies ran while one was open for 1% of the time, Pallas kernels for 30%

profile of v4, /device:TPU:0, one launch (start us, length us, event | category | flops | bytes accessed | tf_op | source)
XLA Modules:
  0.0 149.6 jit_solution(14365792380588726825)
XLA Ops:
  0.0 3.8 %shard_map.145 = (f32[32,1024]{1,0:T(8,128)S(1)}, f32[2,256,128]{2,1,0:T(8,128)S(1)}, f32[2,256,128]{2,1,0:T(8,128)S(1)}) custom-call(bf16[256,32,128]{2,1,0:T(8,128)(2,1)} %refs_3_.1, bf16[256,32,128]{2,1,0:T(8,128)(2,1)} %refs_6_.1), custom_call_target="tpu_custom_call" | custom-call | flops 8388608 | bytes 4194304 | tf_op jit(solution)/shard_map/pallas_call | solution.py:122
  3.8 3.0 %collective-permute-start.2 = (f32[2,256,128]{2,1,0:T(8,128)S(1)}, f32[2,256,128]{2,1,0:T(8,128)S(1)}, u32[]{:S(2)}, u32[]{:S(2)}) collective-permute-start(f32[2,256,128]{2,1,0:T(8,128)S(1)} %get-tuple-element.62), channel_id=1, source_target_pairs={{0,1},{1,2},{2,3},{3,4},{4,5},{5,6},{6,7},{7,0},{8,9},{9,10},{10,1... | collective-permute-start | bytes 786440 | tf_op jit(solution)/shard_map/ppermute | solution.py:32
  6.9 3.1 %collective-permute-start.3 = (f32[2,256,128]{2,1,0:T(8,128)S(1)}, f32[2,256,128]{2,1,0:T(8,128)S(1)}, u32[]{:S(2)}, u32[]{:S(2)}) collective-permute-start(f32[2,256,128]{2,1,0:T(8,128)S(1)} %get-tuple-element.63), channel_id=1, source_target_pairs={{0,7},{1,0},{2,1},{3,2},{4,3},{5,4},{6,5},{7,6},{8,15},{9,8},{10,9... | collective-permute-start | bytes 786440 | tf_op jit(solution)/shard_map/ppermute | solution.py:32
  10.0 1.7 %collective-permute-start.1 = (f32[32,1024]{1,0:T(8,128)S(1)}, f32[32,1024]{1,0:T(8,128)S(1)}, u32[]{:S(2)}, u32[]{:S(2)}) collective-permute-start(f32[32,1024]{1,0:T(8,128)S(1)} %get-tuple-element.61), channel_id=1, source_target_pairs={{0,24},{8,0},{16,8},{24,16},{1,25},{9,1},{17,9},{25,17},{2,26},{10... | collective-permute-start | bytes 393224 | tf_op jit(solution)/shard_map/ppermute | solution.py:32
  11.7 0.9 copy-done.2
  12.6 16.6 %shard_map.146 = (f32[3,32,1024]{2,1,0:T(8,128)S(1)}, f32[3,256,128]{2,1,0:T(8,128)S(1)}, f32[3,256,128]{2,1,0:T(8,128)S(1)}, f32[3,256,128]{2,1,0:T(8,128)S(1)}...) custom-call(f32[3,256,32,128]{3,2,1,0:T(8,128)} %refs_0_.7, f32[3,256,32,128]{3,2,1,0:T(8,128)} %refs_0_.7, ...), custom_call_target="tpu_custom_call" | custom-call | flops 75497472 | bytes 12582912 | tf_op jit(solution)/shard_map/pallas_call | solution.py:122
  29.3 1.7 %collective-permute-start.9 = (f32[3,32,1024]{2,1,0:T(8,128)S(1)}, f32[3,32,1024]{2,1,0:T(8,128)S(1)}, u32[]{:S(2)}, u32[]{:S(2)}) collective-permute-start(f32[3,32,1024]{2,1,0:T(8,128)S(1)} %get-tuple-element.73), channel_id=1, source_target_pairs={{0,24},{8,0},{16,8},{24,16},{1,25},{9,1},{17,9},{25,17},{2,26},{10... | collective-permute-start | bytes 1179656 | tf_op jit(solution)/shard_map/ppermute | solution.py:32
  31.0 4.7 %collective-permute-start.11 = (f32[3,256,128]{2,1,0:T(8,128)S(1)}, f32[3,256,128]{2,1,0:T(8,128)S(1)}, u32[]{:S(2)}, u32[]{:S(2)}) collective-permute-start(f32[3,256,128]{2,1,0:T(8,128)S(1)} %get-tuple-element.75), channel_id=1, source_target_pairs={{0,7},{1,0},{2,1},{3,2},{4,3},{5,4},{6,5},{7,6},{8,15},{9,8},{10,9... | collective-permute-start | bytes 1179656 | tf_op jit(solution)/shard_map/ppermute | solution.py:32
  35.8 10.7 %shard_map.147 = (f32[32,1024]{1,0:T(8,128)S(1)}, f32[256,128]{1,0:T(8,128)S(1)}, f32[256,128]{1,0:T(8,128)S(1)}, f32[256,32,128]{2,1,0:T(8,128)S(1)}, f32[256,3...) custom-call(f32[3,256,32,128]{3,2,1,0:T(8,128)} %refs_0_.7, ...), custom_call_target="tpu_custom_call" | custom-call | flops 25165824 | bytes 16777216 | tf_op jit(solution)/shard_map/pallas_call | solution.py:122
  46.6 1.7 %collective-permute-start.5 = (f32[32,1024]{1,0:T(8,128)S(1)}, f32[32,1024]{1,0:T(8,128)S(1)}, u32[]{:S(2)}, u32[]{:S(2)}) collective-permute-start(f32[32,1024]{1,0:T(8,128)S(1)} %get-tuple-element.68), channel_id=1, source_target_pairs={{0,24},{8,0},{16,8},{24,16},{1,25},{9,1},{17,9},{25,17},{2,26},{10... | collective-permute-start | bytes 393224 | tf_op jit(solution)/shard_map/ppermute | solution.py:32
  48.4 5.1 %collective-permute-start.7 = (f32[256,128]{1,0:T(8,128)S(1)}, f32[256,128]{1,0:T(8,128)S(1)}, u32[]{:S(2)}, u32[]{:S(2)}) collective-permute-start(f32[256,128]{1,0:T(8,128)S(1)} %get-tuple-element.70), channel_id=1, source_target_pairs={{0,7},{1,0},{2,1},{3,2},{4,3},{5,4},{6,5},{7,6},{8,15},{9,8},{10,9... | collective-permute-start | bytes 393224 | tf_op jit(solution)/shard_map/ppermute | solution.py:32
  53.6 0.2 fusion.22
  53.8 0.2 fusion.13
  54.2 0.5 shard_map.148
  54.9 1.7 %collective-permute-done.6.refs_1_ = f32[256,128]{1,0:T(8,128)S(1)} collective-permute-done((f32[256,128]{1,0:T(8,128)S(1)}, f32[256,128]{1,0:T(8,128)S(1)}, u32[]{:S(2)}, u32[]{:S(2)}) %collective-permute-start.6) | collective-permute-done | bytes 131104 | tf_op jit(solution)/shard_map/ppermute | solution.py:32
  56.7 0.2 collective-permute-start.14
  56.9 4.5 %collective-permute-start.15 = (f32[3,256,128]{2,1,0:T(8,128)S(1)}, f32[3,256,128]{2,1,0:T(8,128)S(1)}, u32[]{:S(2)}, u32[]{:S(2)}) collective-permute-start(f32[3,256,128]{2,1,0:T(8,128)S(1)} %get-tuple-element.90), channel_id=1, source_target_pairs={{0,7},{1,0},{2,1},{3,2},{4,3},{5,4},{6,5},{7,6},{8,15},{9,8},{10,9... | collective-permute-start | bytes 1179656 | tf_op jit(solution)/shard_map/ppermute | solution.py:32
  61.4 10.1 %shard_map.149 = (f32[32,1024]{1,0:T(8,128)S(1)}, f32[256,128]{1,0:T(8,128)S(1)}, f32[256,128]{1,0:T(8,128)S(1)}, f32[256,32,128]{2,1,0:T(8,128)S(1)}) custom-call(f32[3,256,32,128]{3,2,1,0:T(8,128)} %refs_2_.6, f32[256,128]{1,0:T(8,128)S(1)} %collective-permute-done.6.refs_1_, ...), custom_call_target="tpu_custom_call", output_to_operand_aliasing={{3}: (6, {})} | custom-call | flops 31457280 | bytes 12582912 | tf_op jit(solution)/shard_map/pallas_call | solution.py:122
  71.6 4.7 %collective-permute-start.13 = (f32[256,128]{1,0:T(8,128)S(1)}, f32[256,128]{1,0:T(8,128)S(1)}, u32[]{:S(2)}, u32[]{:S(2)}) collective-permute-start(f32[256,128]{1,0:T(8,128)S(1)} %get-tuple-element.87), channel_id=1, source_target_pairs={{0,7},{1,0},{2,1},{3,2},{4,3},{5,4},{6,5},{7,6},{8,15},{9,8},{10,9... | collective-permute-start | bytes 393224 | tf_op jit(solution)/shard_map/ppermute | solution.py:32
  76.4 0.2 fusion.25
  76.5 0.6 collective-permute-done.14.refs_2_
  77.1 2.7 %collective-permute-done.15.refs_3_ = f32[3,256,128]{2,1,0:T(8,128)S(1)} collective-permute-done((f32[3,256,128]{2,1,0:T(8,128)S(1)}, f32[3,256,128]{2,1,0:T(8,128)S(1)}, u32[]{:S(2)}, u32[]{:S(2)}) %collective-permute-start.15) | collective-permute-done | bytes 393248 | tf_op jit(solution)/shard_map/ppermute | solution.py:32
  79.9 1.7 %collective-permute-start.17 = (f32[32,1024]{1,0:T(8,128)S(1)}, f32[32,1024]{1,0:T(8,128)S(1)}, u32[]{:S(2)}, u32[]{:S(2)}) collective-permute-start(f32[32,1024]{1,0:T(8,128)S(1)} %get-tuple-element.91), channel_id=1, source_target_pairs={{0,24},{8,0},{16,8},{24,16},{1,25},{9,1},{17,9},{25,17},{2,26},{10... | collective-permute-start | bytes 393224 | tf_op jit(solution)/shard_map/ppermute | solution.py:32
  81.6 0.3 fusion.9.refs_4_
  81.9 6.3 %shard_map.150.refs_7_ = f32[3,256,32,128]{3,2,1,0:T(8,128)S(1)} custom-call(f32[3,256,128]{2,1,0:T(8,128)S(1)} %collective-permute-done.10.refs_0_, f32[3,256,128]{2,1,0:T(8,128)S(1)} %collective-permute-done.11.refs_1_, f32[3,256,128]{2,1,0:T(8,128)S(1)} %collective-permute-done.14.refs_2_, ...), custom_call_target="tpu_custom_call", output_to_operand_aliasing={{}: (5, {})} | custom-call | flops 12582912 | bytes 3145728 | tf_op jit(solution)/shard_map/pallas_call | solution.py:122
  88.4 16.2 %shard_map.151 = (f32[3,256,32,128]{3,2,1,0:T(8,128)}, f32[3,512,32]{2,1,0:T(8,128)S(1)}) custom-call(f32[3,256,32,128]{3,2,1,0:T(8,128)} %refs_2_.6, f32[3,256,32,128]{3,2,1,0:T(8,128)} %refs_2_.6, f32[3,256,32,128]{3,2,1,0:T(8,128)} %refs_2_.6, f32[256,128]{1,0:T(8,128)S(1)} %collective-permute-done.12.refs_3_, ...), custom_call_target="tpu_custom_call" | custom-call | flops 73400320 | bytes 25165824 | tf_op jit(solution)/shard_map/pallas_call | solution.py:122
  104.6 1.4 convolution_bitcast_fusion
  106.0 0.3 copy.44
  106.3 1.0 reshape.69
  107.4 2.9 %all-to-all-start = ((f32[32,1,1536]{2,1,0:T(1,128)}), f32[32,1,1536]{2,1,0:T(1,128)S(1)}, u32[]{:S(2)}, u32[]{:S(2)}) async-start(f32[32,1,1536]{2,1,0:T(1,128)} %reshape.69), calls=%async_computation | async-start | bytes 393216 | tf_op jit(solution)/shard_map/all_to_all | solution.py:746
  110.5 8.1 %all-to-all-done = f32[32,1,1536]{2,1,0:T(1,128)S(1)} async-done(((f32[32,1,1536]{2,1,0:T(1,128)}), f32[32,1,1536]{2,1,0:T(1,128)S(1)}, u32[]{:S(2)}, u32[]{:S(2)}) %all-to-all-start) | async-done | bytes 196640 | tf_op jit(solution)/shard_map/all_to_all | solution.py:746
  118.6 0.5 broadcast.57
  119.1 1.1 reduce
  120.3 0.2 reshape.70
  120.5 0.5 copy.38
  121.0 0.4 reshape.61
  121.4 0.3 convolution_bitcast_fusion.2
  121.7 0.3 convolution_divide_fusion
  122.1 0.3 fusion.26
  122.4 0.3 convolution_bitcast_fusion.1
  122.7 0.3 reshape.62
  123.1 0.4 reshape.71
  123.5 11.3 %all_to_all.10 = f32[32,1,1536]{2,1,0:T(1,128)S(1)} all-to-all(f32[32,1,1536]{2,1,0:T(1,128)S(1)} %reshape.71), channel_id=1, replica_groups=mesh['gz'=4,'gy'=8] {'gz','gy'}, dimensions={0} | all-to-all | bytes 393216 | tf_op jit(solution)/shard_map/all_to_all | solution.py:761
  134.8 1.1 reduce.1
  135.9 0.2 reshape.72
  136.2 1.4 fusion
  137.6 0.3 copy.42
  138.0 11.6 %shard_map.152 = f32[3,256,32,128]{3,2,1,0:T(8,128)} custom-call(f32[3,512,32]{2,1,0:T(8,128)S(1)} %bitcast_subtract_fusion.refs_0_, f32[3,256,32,128]{3,2,1,0:T(8,128)} %get-tuple-element.102.refs_1_, bf16[64,128]{1,0:T(8,128)(2,1)S(1)} %copy-done.5), custom_call_target="tpu_custom_call" | custom-call | flops 6291456 | bytes 25165824 | tf_op jit(solution)/shard_map/pallas_call | solution.py:122
  (63 shorter events, 1.3 us)
Async XLA Ops:
  3.8 32.0 %copy-start.1 = (bf16[384,256]{1,0:T(8,128)(2,1)S(1)}, bf16[384,256]{1,0:T(8,128)(2,1)}, u32[]{:S(2)}) copy-start(bf16[384,256]{1,0:T(8,128)(2,1)} %constant.72.clone.refs_11_) | copy-start | bytes 589828
  3.8 25.4 %collective-permute-start.2 = (f32[2,256,128]{2,1,0:T(8,128)S(1)}, f32[2,256,128]{2,1,0:T(8,128)S(1)}, u32[]{:S(2)}, u32[]{:S(2)}) collective-permute-start(f32[2,256,128]{2,1,0:T(8,128)S(1)} %get-tuple-element.62), channel_id=1, source_target_pairs={{0,1},{1,2},{2,3},{3,4},{4,5},{5,6},{6,7},{7,0},{8,9},{9,10},{10,1... | collective-permute-start | bytes 786440 | tf_op jit(solution)/shard_map/ppermute | solution.py:32
  6.9 22.4 %collective-permute-start.3 = (f32[2,256,128]{2,1,0:T(8,128)S(1)}, f32[2,256,128]{2,1,0:T(8,128)S(1)}, u32[]{:S(2)}, u32[]{:S(2)}) collective-permute-start(f32[2,256,128]{2,1,0:T(8,128)S(1)} %get-tuple-element.63), channel_id=1, source_target_pairs={{0,7},{1,0},{2,1},{3,2},{4,3},{5,4},{6,5},{7,6},{8,15},{9,8},{10,9... | collective-permute-start | bytes 786440 | tf_op jit(solution)/shard_map/ppermute | solution.py:32
  10.0 19.2 %collective-permute-start = (f32[32,1024]{1,0:T(8,128)S(1)}, f32[32,1024]{1,0:T(8,128)S(1)}, u32[]{:S(2)}, u32[]{:S(2)}) collective-permute-start(f32[32,1024]{1,0:T(8,128)S(1)} %get-tuple-element.61), channel_id=1, source_target_pairs={{0,8},{8,16},{16,24},{24,0},{1,9},{9,17},{17,25},{25,1},{2,10},{10... | collective-permute-start | bytes 393224 | tf_op jit(solution)/shard_map/ppermute | solution.py:32
  10.0 19.3 %collective-permute-start.1 = (f32[32,1024]{1,0:T(8,128)S(1)}, f32[32,1024]{1,0:T(8,128)S(1)}, u32[]{:S(2)}, u32[]{:S(2)}) collective-permute-start(f32[32,1024]{1,0:T(8,128)S(1)} %get-tuple-element.61), channel_id=1, source_target_pairs={{0,24},{8,0},{16,8},{24,16},{1,25},{9,1},{17,9},{25,17},{2,26},{10... | collective-permute-start | bytes 393224 | tf_op jit(solution)/shard_map/ppermute | solution.py:32
  11.7 0.9 copy-start.2
  29.2 17.4 %collective-permute-start.8 = (f32[3,32,1024]{2,1,0:T(8,128)S(1)}, f32[3,32,1024]{2,1,0:T(8,128)S(1)}, u32[]{:S(2)}, u32[]{:S(2)}) collective-permute-start(f32[3,32,1024]{2,1,0:T(8,128)S(1)} %get-tuple-element.73), channel_id=1, source_target_pairs={{0,8},{8,16},{16,24},{24,0},{1,9},{9,17},{17,25},{25,1},{2,10},{10... | collective-permute-start | bytes 1179656 | tf_op jit(solution)/shard_map/ppermute | solution.py:32
  29.3 19.1 %collective-permute-start.9 = (f32[3,32,1024]{2,1,0:T(8,128)S(1)}, f32[3,32,1024]{2,1,0:T(8,128)S(1)}, u32[]{:S(2)}, u32[]{:S(2)}) collective-permute-start(f32[3,32,1024]{2,1,0:T(8,128)S(1)} %get-tuple-element.73), channel_id=1, source_target_pairs={{0,24},{8,0},{16,8},{24,16},{1,25},{9,1},{17,9},{25,17},{2,26},{10... | collective-permute-start | bytes 1179656 | tf_op jit(solution)/shard_map/ppermute | solution.py:32
  31.0 17.3 %collective-permute-start.10 = (f32[3,256,128]{2,1,0:T(8,128)S(1)}, f32[3,256,128]{2,1,0:T(8,128)S(1)}, u32[]{:S(2)}, u32[]{:S(2)}) collective-permute-start(f32[3,256,128]{2,1,0:T(8,128)S(1)} %get-tuple-element.74), channel_id=1, source_target_pairs={{0,1},{1,2},{2,3},{3,4},{4,5},{5,6},{6,7},{7,0},{8,9},{9,10},{10,1... | collective-permute-start | bytes 1179656 | tf_op jit(solution)/shard_map/ppermute | solution.py:32
  31.0 22.4 %collective-permute-start.11 = (f32[3,256,128]{2,1,0:T(8,128)S(1)}, f32[3,256,128]{2,1,0:T(8,128)S(1)}, u32[]{:S(2)}, u32[]{:S(2)}) collective-permute-start(f32[3,256,128]{2,1,0:T(8,128)S(1)} %get-tuple-element.75), channel_id=1, source_target_pairs={{0,7},{1,0},{2,1},{3,2},{4,3},{5,4},{6,5},{7,6},{8,15},{9,8},{10,9... | collective-permute-start | bytes 1179656 | tf_op jit(solution)/shard_map/ppermute | solution.py:32
  46.5 25.0 %copy-start = (f32[258,48,128]{2,1,0:T(8,128)}, f32[258,48,128]{2,1,0:T(8,128)S(1)}, u32[]{:S(2)}) copy-start(f32[258,48,128]{2,1,0:T(8,128)S(1)} %get-tuple-element.98.refs_9_) | copy-start | bytes 19021828
  46.5 7.7 %copy-start.3 = (bf16[256,128]{1,0:T(8,128)(2,1)S(1)}, bf16[256,128]{1,0:T(8,128)(2,1)}, u32[]{:S(2)}) copy-start(bf16[256,128]{1,0:T(8,128)(2,1)} %constant.73.clone.table) | copy-start | bytes 196612
  46.6 8.3 %collective-permute-start.4 = (f32[32,1024]{1,0:T(8,128)S(1)}, f32[32,1024]{1,0:T(8,128)S(1)}, u32[]{:S(2)}, u32[]{:S(2)}) collective-permute-start(f32[32,1024]{1,0:T(8,128)S(1)} %get-tuple-element.68), channel_id=1, source_target_pairs={{0,8},{8,16},{16,24},{24,0},{1,9},{9,17},{17,25},{25,1},{2,10},{10... | collective-permute-start | bytes 393224 | tf_op jit(solution)/shard_map/ppermute | solution.py:32
  46.6 8.2 %collective-permute-start.5 = (f32[32,1024]{1,0:T(8,128)S(1)}, f32[32,1024]{1,0:T(8,128)S(1)}, u32[]{:S(2)}, u32[]{:S(2)}) collective-permute-start(f32[32,1024]{1,0:T(8,128)S(1)} %get-tuple-element.68), channel_id=1, source_target_pairs={{0,24},{8,0},{16,8},{24,16},{1,25},{9,1},{17,9},{25,17},{2,26},{10... | collective-permute-start | bytes 393224 | tf_op jit(solution)/shard_map/ppermute | solution.py:32
  48.4 8.2 %collective-permute-start.6 = (f32[256,128]{1,0:T(8,128)S(1)}, f32[256,128]{1,0:T(8,128)S(1)}, u32[]{:S(2)}, u32[]{:S(2)}) collective-permute-start(f32[256,128]{1,0:T(8,128)S(1)} %get-tuple-element.69), channel_id=1, source_target_pairs={{0,1},{1,2},{2,3},{3,4},{4,5},{5,6},{6,7},{7,0},{8,9},{9,10},{10,1... | collective-permute-start | bytes 393224 | tf_op jit(solution)/shard_map/ppermute | solution.py:32
  48.4 8.3 %collective-permute-start.7 = (f32[256,128]{1,0:T(8,128)S(1)}, f32[256,128]{1,0:T(8,128)S(1)}, u32[]{:S(2)}, u32[]{:S(2)}) collective-permute-start(f32[256,128]{1,0:T(8,128)S(1)} %get-tuple-element.70), channel_id=1, source_target_pairs={{0,7},{1,0},{2,1},{3,2},{4,3},{5,4},{6,5},{7,6},{8,15},{9,8},{10,9... | collective-permute-start | bytes 393224 | tf_op jit(solution)/shard_map/ppermute | solution.py:32
  56.7 20.4 %collective-permute-start.14 = (f32[3,256,128]{2,1,0:T(8,128)S(1)}, f32[3,256,128]{2,1,0:T(8,128)S(1)}, u32[]{:S(2)}, u32[]{:S(2)}) collective-permute-start(f32[3,256,128]{2,1,0:T(8,128)S(1)} %get-tuple-element.89), channel_id=1, source_target_pairs={{0,1},{1,2},{2,3},{3,4},{4,5},{5,6},{6,7},{7,0},{8,9},{9,10},{10,1... | collective-permute-start | bytes 1179656 | tf_op jit(solution)/shard_map/ppermute | solution.py:32
  56.9 23.0 %collective-permute-start.15 = (f32[3,256,128]{2,1,0:T(8,128)S(1)}, f32[3,256,128]{2,1,0:T(8,128)S(1)}, u32[]{:S(2)}, u32[]{:S(2)}) collective-permute-start(f32[3,256,128]{2,1,0:T(8,128)S(1)} %get-tuple-element.90), channel_id=1, source_target_pairs={{0,7},{1,0},{2,1},{3,2},{4,3},{5,4},{6,5},{7,6},{8,15},{9,8},{10,9... | collective-permute-start | bytes 1179656 | tf_op jit(solution)/shard_map/ppermute | solution.py:32
  71.5 16.8 %collective-permute-start.12 = (f32[256,128]{1,0:T(8,128)S(1)}, f32[256,128]{1,0:T(8,128)S(1)}, u32[]{:S(2)}, u32[]{:S(2)}) collective-permute-start(f32[256,128]{1,0:T(8,128)S(1)} %get-tuple-element.86), channel_id=1, source_target_pairs={{0,1},{1,2},{2,3},{3,4},{4,5},{5,6},{6,7},{7,0},{8,9},{9,10},{10,1... | collective-permute-start | bytes 393224 | tf_op jit(solution)/shard_map/ppermute | solution.py:32
  71.6 16.7 %collective-permute-start.13 = (f32[256,128]{1,0:T(8,128)S(1)}, f32[256,128]{1,0:T(8,128)S(1)}, u32[]{:S(2)}, u32[]{:S(2)}) collective-permute-start(f32[256,128]{1,0:T(8,128)S(1)} %get-tuple-element.87), channel_id=1, source_target_pairs={{0,7},{1,0},{2,1},{3,2},{4,3},{5,4},{6,5},{7,6},{8,15},{9,8},{10,9... | collective-permute-start | bytes 393224 | tf_op jit(solution)/shard_map/ppermute | solution.py:32
  79.9 8.5 %collective-permute-start.16 = (f32[32,1024]{1,0:T(8,128)S(1)}, f32[32,1024]{1,0:T(8,128)S(1)}, u32[]{:S(2)}, u32[]{:S(2)}) collective-permute-start(f32[32,1024]{1,0:T(8,128)S(1)} %get-tuple-element.91), channel_id=1, source_target_pairs={{0,8},{8,16},{16,24},{24,0},{1,9},{9,17},{17,25},{25,1},{2,10},{10... | collective-permute-start | bytes 393224 | tf_op jit(solution)/shard_map/ppermute | solution.py:32
  79.9 8.5 %collective-permute-start.17 = (f32[32,1024]{1,0:T(8,128)S(1)}, f32[32,1024]{1,0:T(8,128)S(1)}, u32[]{:S(2)}, u32[]{:S(2)}) collective-permute-start(f32[32,1024]{1,0:T(8,128)S(1)} %get-tuple-element.91), channel_id=1, source_target_pairs={{0,24},{8,0},{16,8},{24,16},{1,25},{9,1},{17,9},{25,17},{2,26},{10... | collective-permute-start | bytes 393224 | tf_op jit(solution)/shard_map/ppermute | solution.py:32
  81.6 6.7 %slice-start = ((s8[6340608]{0:T(1024)(128)(4,1)}), s8[2146304]{0:T(1024)(128)(4,1)S(1)}, s32[]{:S(2)}) async-start(s8[6340608]{0:T(1024)(128)(4,1)} %bitcast.34), calls=%async_computation.2 | async-start | bytes 4292608
  81.9 6.4 %slice-start.1 = ((s8[6340608]{0:T(1024)(128)(4,1)}), s8[4194304]{0:T(1024)(128)(4,1)S(1)}, s32[]{:S(2)}) async-start(s8[6340608]{0:T(1024)(128)(4,1)} %bitcast.34), calls=%async_computation.3 | async-start | bytes 8388608
  81.9 6.4 %copy-start.4 = (bf16[256,32]{1,0:T(8,128)(2,1)S(1)}, bf16[256,32]{1,0:T(8,128)(2,1)}, u32[]{:S(2)}) copy-start(bf16[256,32]{1,0:T(8,128)(2,1)} %constant.74.clone.refs_12_) | copy-start | bytes 49156
  88.4 16.2 %copy-start.6 = (f32[64,64,1,1]{1,0,3,2:T(8,128)S(1)}, f32[64,64,1,1]{1,0,3,2:T(8,128)}, u32[]{:S(2)}) copy-start(f32[64,64,1,1]{1,0,3,2:T(8,128)} %constant.84) | copy-start | bytes 49156
  88.4 21.9 %copy-start.9 = (f32[64]{0:T(128)S(1)}, f32[64]{0:T(128)}, u32[]{:S(2)}) copy-start(f32[64]{0:T(128)} %constant.77.clone) | copy-start | bytes 772
  88.4 33.0 %copy-start.7 = (f32[64,64,1]{1,0,2:T(8,128)S(1)}, f32[64,64,1]{1,0,2:T(8,128)}, u32[]{:S(2)}) copy-start(f32[64,64,1]{1,0,2:T(8,128)} %constant.85) | copy-start | bytes 49156
  88.4 33.3 %copy-start.8 = (f32[128,128,1]{1,0,2:T(8,128)S(1)}, f32[128,128,1]{1,0,2:T(8,128)}, u32[]{:S(2)}) copy-start(f32[128,128,1]{1,0,2:T(8,128)} %constant.86) | copy-start | bytes 196612
  88.4 33.3 %copy-start.10 = (f32[128]{0:T(128)S(1)}, f32[128]{0:T(128)}, u32[]{:S(2)}) copy-start(f32[128]{0:T(128)} %constant.78.clone) | copy-start | bytes 1540
  107.4 30.6 %copy-start.5 = (bf16[64,128]{1,0:T(8,128)(2,1)S(1)}, bf16[64,128]{1,0:T(8,128)(2,1)}, u32[]{:S(2)}) copy-start(bf16[64,128]{1,0:T(8,128)(2,1)} %constant.79.clone.refs_2_) | copy-start | bytes 49156
  107.4 11.3 %all-to-all-start = ((f32[32,1,1536]{2,1,0:T(1,128)}), f32[32,1,1536]{2,1,0:T(1,128)S(1)}, u32[]{:S(2)}, u32[]{:S(2)}) async-start(f32[32,1,1536]{2,1,0:T(1,128)} %reshape.69), calls=%async_computation | async-start | bytes 393216 | tf_op jit(solution)/shard_map/all_to_all | solution.py:746

commit v5 on v4

--- a/solution.py
+++ b/solution.py
@@ -819,9 +819,7 @@
     f_packed, f_low, f_high, adjoint = second_state(
         velocity, source, state, s_below, s_above, s_left, s_right
     )
-    f_packed, low_curves, high_curves = lax.optimization_barrier(
-        (f_packed, low_curves, high_curves)
-    )
+    f_packed, low_curves = lax.optimization_barrier((f_packed, low_curves))
     f_left = shifted(f_packed, "gz", 1)
     f_right = shifted(f_packed, "gz", -1)
     f_below = shifted(f_high, "gy", 1)

time: 150 us -> 150 us (level)
  waiting for transfers between devices: 13.3 us -> 11.2 us
    ppermute x18, waiting for transfers between devices: 5.18 us -> 3.12 us  [shifted(): lax.ppermute(value, axis, [(i, (i + by) % peers) for i in range(peers)])]
where the time goes in v5:
time: 150 us; the launch traced here: 149 us
  Pallas kernels  75.9 us (51%)
  starting transfers between devices  36.8 us (25%)
  blocking collectives  11.4 us (8%)
  waiting for transfers between devices  11.2 us (7%)
  local copies, waits for them, and re-layouts  6.19 us (4%)
  matrix products  4.07 us (3%)
  other arithmetic  2.95 us (2%)
    pallas_call x7, Pallas kernels, call(): pl.pallas_call(kernel, in_specs=[far] * counts[0] + [near] * counts[1], o...  75.3 us
    ppermute x18, starting transfers between devices, shifted(): lax.ppermute(value, axis, [(i, (i + by) % peers) for i in range(peers)])  32.5 us
    all_to_all x1, blocking collectives, coarse_spread(): coeffs = lax.all_to_all(planes, both, 0, 0, tiled=True)[:3 * cxlen]  11.4 us
    all_to_all x1, waiting for transfers between devices, coarse_spread(): planes = lax.all_to_all(coeffs, both, 0, 0, tiled=True)  8.1 us
    all_to_all x1, starting transfers between devices, coarse_spread(): planes = lax.all_to_all(coeffs, both, 0, 0, tiled=True)  4.37 us
    ppermute x18, waiting for transfers between devices, shifted(): lax.ppermute(value, axis, [(i, (i + by) % peers) for i in range(peers)])  3.12 us
  transfers between devices with their start and end apart: 19, of which 5 were waited for; matrix products, arithmetic and copies ran while one was open for 1% of the time, Pallas kernels for 30%

profile of v5, /device:TPU:0, one launch (start us, length us, event | category | flops | bytes accessed | tf_op | source)
XLA Modules:
  0.0 149.0 jit_solution(18233651548739810741)
XLA Ops:
  0.0 3.8 %shard_map.145 = (f32[32,1024]{1,0:T(8,128)S(1)}, f32[2,256,128]{2,1,0:T(8,128)S(1)}, f32[2,256,128]{2,1,0:T(8,128)S(1)}) custom-call(bf16[256,32,128]{2,1,0:T(8,128)(2,1)} %refs_3_.1, bf16[256,32,128]{2,1,0:T(8,128)(2,1)} %refs_6_.1), custom_call_target="tpu_custom_call" | custom-call | flops 8388608 | bytes 4194304 | tf_op jit(solution)/shard_map/pallas_call | solution.py:122
  3.8 3.0 %collective-permute-start.2 = (f32[2,256,128]{2,1,0:T(8,128)S(1)}, f32[2,256,128]{2,1,0:T(8,128)S(1)}, u32[]{:S(2)}, u32[]{:S(2)}) collective-permute-start(f32[2,256,128]{2,1,0:T(8,128)S(1)} %get-tuple-element.61), channel_id=1, source_target_pairs={{0,1},{1,2},{2,3},{3,4},{4,5},{5,6},{6,7},{7,0},{8,9},{9,10},{10,1... | collective-permute-start | bytes 786440 | tf_op jit(solution)/shard_map/ppermute | solution.py:32
  6.9 3.1 %collective-permute-start.3 = (f32[2,256,128]{2,1,0:T(8,128)S(1)}, f32[2,256,128]{2,1,0:T(8,128)S(1)}, u32[]{:S(2)}, u32[]{:S(2)}) collective-permute-start(f32[2,256,128]{2,1,0:T(8,128)S(1)} %get-tuple-element.62), channel_id=1, source_target_pairs={{0,7},{1,0},{2,1},{3,2},{4,3},{5,4},{6,5},{7,6},{8,15},{9,8},{10,9... | collective-permute-start | bytes 786440 | tf_op jit(solution)/shard_map/ppermute | solution.py:32
  10.0 1.7 %collective-permute-start.1 = (f32[32,1024]{1,0:T(8,128)S(1)}, f32[32,1024]{1,0:T(8,128)S(1)}, u32[]{:S(2)}, u32[]{:S(2)}) collective-permute-start(f32[32,1024]{1,0:T(8,128)S(1)} %get-tuple-element.60), channel_id=1, source_target_pairs={{0,24},{8,0},{16,8},{24,16},{1,25},{9,1},{17,9},{25,17},{2,26},{10... | collective-permute-start | bytes 393224 | tf_op jit(solution)/shard_map/ppermute | solution.py:32
  11.7 0.9 copy-done.2
  12.6 16.6 %shard_map.146 = (f32[3,32,1024]{2,1,0:T(8,128)S(1)}, f32[3,256,128]{2,1,0:T(8,128)S(1)}, f32[3,256,128]{2,1,0:T(8,128)S(1)}, f32[3,256,128]{2,1,0:T(8,128)S(1)}...) custom-call(f32[3,256,32,128]{3,2,1,0:T(8,128)} %refs_0_.7, f32[3,256,32,128]{3,2,1,0:T(8,128)} %refs_0_.7, ...), custom_call_target="tpu_custom_call" | custom-call | flops 75497472 | bytes 12582912 | tf_op jit(solution)/shard_map/pallas_call | solution.py:122
  29.3 1.7 %collective-permute-start.9 = (f32[3,32,1024]{2,1,0:T(8,128)S(1)}, f32[3,32,1024]{2,1,0:T(8,128)S(1)}, u32[]{:S(2)}, u32[]{:S(2)}) collective-permute-start(f32[3,32,1024]{2,1,0:T(8,128)S(1)} %get-tuple-element.72), channel_id=1, source_target_pairs={{0,24},{8,0},{16,8},{24,16},{1,25},{9,1},{17,9},{25,17},{2,26},{10... | collective-permute-start | bytes 1179656 | tf_op jit(solution)/shard_map/ppermute | solution.py:32
  31.0 4.7 %collective-permute-start.11 = (f32[3,256,128]{2,1,0:T(8,128)S(1)}, f32[3,256,128]{2,1,0:T(8,128)S(1)}, u32[]{:S(2)}, u32[]{:S(2)}) collective-permute-start(f32[3,256,128]{2,1,0:T(8,128)S(1)} %get-tuple-element.74), channel_id=1, source_target_pairs={{0,7},{1,0},{2,1},{3,2},{4,3},{5,4},{6,5},{7,6},{8,15},{9,8},{10,9... | collective-permute-start | bytes 1179656 | tf_op jit(solution)/shard_map/ppermute | solution.py:32
  35.8 10.7 %shard_map.147 = (f32[32,1024]{1,0:T(8,128)S(1)}, f32[256,128]{1,0:T(8,128)S(1)}, f32[256,128]{1,0:T(8,128)S(1)}, f32[256,32,128]{2,1,0:T(8,128)S(1)}, f32[256,3...) custom-call(f32[3,256,32,128]{3,2,1,0:T(8,128)} %refs_0_.7, ...), custom_call_target="tpu_custom_call" | custom-call | flops 25165824 | bytes 16777216 | tf_op jit(solution)/shard_map/pallas_call | solution.py:122
  46.6 1.7 %collective-permute-start.5 = (f32[32,1024]{1,0:T(8,128)S(1)}, f32[32,1024]{1,0:T(8,128)S(1)}, u32[]{:S(2)}, u32[]{:S(2)}) collective-permute-start(f32[32,1024]{1,0:T(8,128)S(1)} %get-tuple-element.67), channel_id=1, source_target_pairs={{0,24},{8,0},{16,8},{24,16},{1,25},{9,1},{17,9},{25,17},{2,26},{10... | collective-permute-start | bytes 393224 | tf_op jit(solution)/shard_map/ppermute | solution.py:32
  48.4 5.1 %collective-permute-start.7 = (f32[256,128]{1,0:T(8,128)S(1)}, f32[256,128]{1,0:T(8,128)S(1)}, u32[]{:S(2)}, u32[]{:S(2)}) collective-permute-start(f32[256,128]{1,0:T(8,128)S(1)} %get-tuple-element.69), channel_id=1, source_target_pairs={{0,7},{1,0},{2,1},{3,2},{4,3},{5,4},{6,5},{7,6},{8,15},{9,8},{10,9... | collective-permute-start | bytes 393224 | tf_op jit(solution)/shard_map/ppermute | solution.py:32
  53.8 0.2 fusion.25
  54.0 0.5 shard_map.148
  54.5 0.2 fusion.13
  54.8 0.2 fusion.20
  55.0 1.6 %collective-permute-done.6.refs_1_ = f32[256,128]{1,0:T(8,128)S(1)} collective-permute-done((f32[256,128]{1,0:T(8,128)S(1)}, f32[256,128]{1,0:T(8,128)S(1)}, u32[]{:S(2)}, u32[]{:S(2)}) %collective-permute-start.6) | collective-permute-done | bytes 131104 | tf_op jit(solution)/shard_map/ppermute | solution.py:32
  56.7 0.2 collective-permute-start.14
  56.9 4.5 %collective-permute-start.17 = (f32[3,256,128]{2,1,0:T(8,128)S(1)}, f32[3,256,128]{2,1,0:T(8,128)S(1)}, u32[]{:S(2)}, u32[]{:S(2)}) collective-permute-start(f32[3,256,128]{2,1,0:T(8,128)S(1)} %get-tuple-element.93), channel_id=1, source_target_pairs={{0,7},{1,0},{2,1},{3,2},{4,3},{5,4},{6,5},{7,6},{8,15},{9,8},{10,9... | collective-permute-start | bytes 1179656 | tf_op jit(solution)/shard_map/ppermute | solution.py:32
  61.4 10.1 %shard_map.149 = (f32[32,1024]{1,0:T(8,128)S(1)}, f32[256,128]{1,0:T(8,128)S(1)}, f32[256,128]{1,0:T(8,128)S(1)}, f32[256,32,128]{2,1,0:T(8,128)S(1)}) custom-call(f32[3,256,32,128]{3,2,1,0:T(8,128)} %refs_2_.6, f32[256,128]{1,0:T(8,128)S(1)} %collective-permute-done.6.refs_1_, ...), custom_call_target="tpu_custom_call", output_to_operand_aliasing={{3}: (6, {})} | custom-call | flops 31457280 | bytes 12582912 | tf_op jit(solution)/shard_map/pallas_call | solution.py:122
  71.6 4.7 %collective-permute-start.13 = (f32[256,128]{1,0:T(8,128)S(1)}, f32[256,128]{1,0:T(8,128)S(1)}, u32[]{:S(2)}, u32[]{:S(2)}) collective-permute-start(f32[256,128]{1,0:T(8,128)S(1)} %get-tuple-element.86), channel_id=1, source_target_pairs={{0,7},{1,0},{2,1},{3,2},{4,3},{5,4},{6,5},{7,6},{8,15},{9,8},{10,9... | collective-permute-start | bytes 393224 | tf_op jit(solution)/shard_map/ppermute | solution.py:32
  76.4 0.7 collective-permute-done.14.refs_2_
  77.1 1.7 %collective-permute-start.16 = (f32[32,1024]{1,0:T(8,128)S(1)}, f32[32,1024]{1,0:T(8,128)S(1)}, u32[]{:S(2)}, u32[]{:S(2)}) collective-permute-start(f32[32,1024]{1,0:T(8,128)S(1)} %get-tuple-element.89), channel_id=1, source_target_pairs={{0,24},{8,0},{16,8},{24,16},{1,25},{9,1},{17,9},{25,17},{2,26},{10... | collective-permute-start | bytes 393224 | tf_op jit(solution)/shard_map/ppermute | solution.py:32
  78.9 0.3 fusion.9.refs_4_
  79.2 0.7 collective-permute-done.17.refs_3_
  79.9 6.3 %shard_map.150.refs_7_ = f32[3,256,32,128]{3,2,1,0:T(8,128)S(1)} custom-call(f32[3,256,128]{2,1,0:T(8,128)S(1)} %collective-permute-done.10.refs_0_, f32[3,256,128]{2,1,0:T(8,128)S(1)} %collective-permute-done.11.refs_1_, f32[3,256,128]{2,1,0:T(8,128)S(1)} %collective-permute-done.14.refs_2_, ...), custom_call_target="tpu_custom_call", output_to_operand_aliasing={{}: (5, {})} | custom-call | flops 12582912 | bytes 3145728 | tf_op jit(solution)/shard_map/pallas_call | solution.py:122
  86.4 16.2 %shard_map.151 = (f32[3,256,32,128]{3,2,1,0:T(8,128)}, f32[3,512,32]{2,1,0:T(8,128)S(1)}) custom-call(f32[3,256,32,128]{3,2,1,0:T(8,128)} %refs_2_.6, f32[3,256,32,128]{3,2,1,0:T(8,128)} %refs_2_.6, f32[3,256,32,128]{3,2,1,0:T(8,128)} %refs_2_.6, f32[256,128]{1,0:T(8,128)S(1)} %collective-permute-done.12.refs_3_, ...), custom_call_target="tpu_custom_call" | custom-call | flops 73400320 | bytes 25165824 | tf_op jit(solution)/shard_map/pallas_call | solution.py:122
  102.5 1.4 convolution_bitcast_fusion
  103.9 0.3 copy.44
  104.2 1.0 reshape.69
  105.3 4.4 %all-to-all-start = ((f32[32,1,1536]{2,1,0:T(1,128)}), f32[32,1,1536]{2,1,0:T(1,128)S(1)}, u32[]{:S(2)}, u32[]{:S(2)}) async-start(f32[32,1,1536]{2,1,0:T(1,128)} %reshape.69), calls=%async_computation | async-start | bytes 393216 | tf_op jit(solution)/shard_map/all_to_all | solution.py:746
  109.9 8.1 %all-to-all-done = f32[32,1,1536]{2,1,0:T(1,128)S(1)} async-done(((f32[32,1,1536]{2,1,0:T(1,128)}), f32[32,1,1536]{2,1,0:T(1,128)S(1)}, u32[]{:S(2)}, u32[]{:S(2)}) %all-to-all-start) | async-done | bytes 196640 | tf_op jit(solution)/shard_map/all_to_all | solution.py:746
  118.0 0.5 broadcast.57
  118.5 1.1 reduce
  119.6 0.2 reshape.70
  119.9 0.5 copy.38
  120.4 0.4 reshape.61
  120.8 0.3 convolution_bitcast_fusion.2
  121.1 0.3 convolution_divide_fusion
  121.4 0.3 fusion.26
  121.8 0.3 convolution_bitcast_fusion.1
  122.1 0.3 reshape.62
  122.5 0.4 reshape.71
  122.9 11.4 %all_to_all.10 = f32[32,1,1536]{2,1,0:T(1,128)S(1)} all-to-all(f32[32,1,1536]{2,1,0:T(1,128)S(1)} %reshape.71), channel_id=1, replica_groups=mesh['gz'=4,'gy'=8] {'gz','gy'}, dimensions={0} | all-to-all | bytes 393216 | tf_op jit(solution)/shard_map/all_to_all | solution.py:761
  134.3 1.1 reduce.1
  135.4 0.2 reshape.72
  135.6 1.4 fusion
  137.0 0.3 copy.42
  137.5 11.6 %shard_map.152 = f32[3,256,32,128]{3,2,1,0:T(8,128)} custom-call(f32[3,512,32]{2,1,0:T(8,128)S(1)} %bitcast_subtract_fusion.refs_0_, f32[3,256,32,128]{3,2,1,0:T(8,128)} %get-tuple-element.100.refs_1_, bf16[64,128]{1,0:T(8,128)(2,1)S(1)} %copy-done.5), custom_call_target="tpu_custom_call" | custom-call | flops 6291456 | bytes 25165824 | tf_op jit(solution)/shard_map/pallas_call | solution.py:122
  (63 shorter events, 1.3 us)
Async XLA Ops:
  3.8 32.0 %copy-start.1 = (bf16[384,256]{1,0:T(8,128)(2,1)S(1)}, bf16[384,256]{1,0:T(8,128)(2,1)}, u32[]{:S(2)}) copy-start(bf16[384,256]{1,0:T(8,128)(2,1)} %constant.72.clone.refs_11_) | copy-start | bytes 589828
  3.8 25.4 %collective-permute-start.2 = (f32[2,256,128]{2,1,0:T(8,128)S(1)}, f32[2,256,128]{2,1,0:T(8,128)S(1)}, u32[]{:S(2)}, u32[]{:S(2)}) collective-permute-start(f32[2,256,128]{2,1,0:T(8,128)S(1)} %get-tuple-element.61), channel_id=1, source_target_pairs={{0,1},{1,2},{2,3},{3,4},{4,5},{5,6},{6,7},{7,0},{8,9},{9,10},{10,1... | collective-permute-start | bytes 786440 | tf_op jit(solution)/shard_map/ppermute | solution.py:32
  6.9 22.4 %collective-permute-start.3 = (f32[2,256,128]{2,1,0:T(8,128)S(1)}, f32[2,256,128]{2,1,0:T(8,128)S(1)}, u32[]{:S(2)}, u32[]{:S(2)}) collective-permute-start(f32[2,256,128]{2,1,0:T(8,128)S(1)} %get-tuple-element.62), channel_id=1, source_target_pairs={{0,7},{1,0},{2,1},{3,2},{4,3},{5,4},{6,5},{7,6},{8,15},{9,8},{10,9... | collective-permute-start | bytes 786440 | tf_op jit(solution)/shard_map/ppermute | solution.py:32
  10.0 19.2 %collective-permute-start = (f32[32,1024]{1,0:T(8,128)S(1)}, f32[32,1024]{1,0:T(8,128)S(1)}, u32[]{:S(2)}, u32[]{:S(2)}) collective-permute-start(f32[32,1024]{1,0:T(8,128)S(1)} %get-tuple-element.60), channel_id=1, source_target_pairs={{0,8},{8,16},{16,24},{24,0},{1,9},{9,17},{17,25},{25,1},{2,10},{10... | collective-permute-start | bytes 393224 | tf_op jit(solution)/shard_map/ppermute | solution.py:32
  10.0 19.3 %collective-permute-start.1 = (f32[32,1024]{1,0:T(8,128)S(1)}, f32[32,1024]{1,0:T(8,128)S(1)}, u32[]{:S(2)}, u32[]{:S(2)}) collective-permute-start(f32[32,1024]{1,0:T(8,128)S(1)} %get-tuple-element.60), channel_id=1, source_target_pairs={{0,24},{8,0},{16,8},{24,16},{1,25},{9,1},{17,9},{25,17},{2,26},{10... | collective-permute-start | bytes 393224 | tf_op jit(solution)/shard_map/ppermute | solution.py:32
  11.7 0.9 copy-start.2
  29.2 17.4 %collective-permute-start.8 = (f32[3,32,1024]{2,1,0:T(8,128)S(1)}, f32[3,32,1024]{2,1,0:T(8,128)S(1)}, u32[]{:S(2)}, u32[]{:S(2)}) collective-permute-start(f32[3,32,1024]{2,1,0:T(8,128)S(1)} %get-tuple-element.72), channel_id=1, source_target_pairs={{0,8},{8,16},{16,24},{24,0},{1,9},{9,17},{17,25},{25,1},{2,10},{10... | collective-permute-start | bytes 1179656 | tf_op jit(solution)/shard_map/ppermute | solution.py:32
  29.3 19.1 %collective-permute-start.9 = (f32[3,32,1024]{2,1,0:T(8,128)S(1)}, f32[3,32,1024]{2,1,0:T(8,128)S(1)}, u32[]{:S(2)}, u32[]{:S(2)}) collective-permute-start(f32[3,32,1024]{2,1,0:T(8,128)S(1)} %get-tuple-element.72), channel_id=1, source_target_pairs={{0,24},{8,0},{16,8},{24,16},{1,25},{9,1},{17,9},{25,17},{2,26},{10... | collective-permute-start | bytes 1179656 | tf_op jit(solution)/shard_map/ppermute | solution.py:32
  31.0 17.3 %collective-permute-start.10 = (f32[3,256,128]{2,1,0:T(8,128)S(1)}, f32[3,256,128]{2,1,0:T(8,128)S(1)}, u32[]{:S(2)}, u32[]{:S(2)}) collective-permute-start(f32[3,256,128]{2,1,0:T(8,128)S(1)} %get-tuple-element.73), channel_id=1, source_target_pairs={{0,1},{1,2},{2,3},{3,4},{4,5},{5,6},{6,7},{7,0},{8,9},{9,10},{10,1... | collective-permute-start | bytes 1179656 | tf_op jit(solution)/shard_map/ppermute | solution.py:32
  31.0 22.4 %collective-permute-start.11 = (f32[3,256,128]{2,1,0:T(8,128)S(1)}, f32[3,256,128]{2,1,0:T(8,128)S(1)}, u32[]{:S(2)}, u32[]{:S(2)}) collective-permute-start(f32[3,256,128]{2,1,0:T(8,128)S(1)} %get-tuple-element.74), channel_id=1, source_target_pairs={{0,7},{1,0},{2,1},{3,2},{4,3},{5,4},{6,5},{7,6},{8,15},{9,8},{10,9... | collective-permute-start | bytes 1179656 | tf_op jit(solution)/shard_map/ppermute | solution.py:32
  35.8 18.2 %copy-start.3 = (bf16[256,128]{1,0:T(8,128)(2,1)S(1)}, bf16[256,128]{1,0:T(8,128)(2,1)}, u32[]{:S(2)}) copy-start(bf16[256,128]{1,0:T(8,128)(2,1)} %constant.73.clone.table) | copy-start | bytes 196612
  46.5 25.0 %copy-start = (f32[258,48,128]{2,1,0:T(8,128)}, f32[258,48,128]{2,1,0:T(8,128)S(1)}, u32[]{:S(2)}) copy-start(f32[258,48,128]{2,1,0:T(8,128)S(1)} %get-tuple-element.96.refs_9_) | copy-start | bytes 19021828
  46.6 8.4 %collective-permute-start.4 = (f32[32,1024]{1,0:T(8,128)S(1)}, f32[32,1024]{1,0:T(8,128)S(1)}, u32[]{:S(2)}, u32[]{:S(2)}) collective-permute-start(f32[32,1024]{1,0:T(8,128)S(1)} %get-tuple-element.67), channel_id=1, source_target_pairs={{0,8},{8,16},{16,24},{24,0},{1,9},{9,17},{17,25},{25,1},{2,10},{10... | collective-permute-start | bytes 393224 | tf_op jit(solution)/shard_map/ppermute | solution.py:32
  46.6 8.3 %collective-permute-start.5 = (f32[32,1024]{1,0:T(8,128)S(1)}, f32[32,1024]{1,0:T(8,128)S(1)}, u32[]{:S(2)}, u32[]{:S(2)}) collective-permute-start(f32[32,1024]{1,0:T(8,128)S(1)} %get-tuple-element.67), channel_id=1, source_target_pairs={{0,24},{8,0},{16,8},{24,16},{1,25},{9,1},{17,9},{25,17},{2,26},{10... | collective-permute-start | bytes 393224 | tf_op jit(solution)/shard_map/ppermute | solution.py:32
  48.4 8.2 %collective-permute-start.6 = (f32[256,128]{1,0:T(8,128)S(1)}, f32[256,128]{1,0:T(8,128)S(1)}, u32[]{:S(2)}, u32[]{:S(2)}) collective-permute-start(f32[256,128]{1,0:T(8,128)S(1)} %get-tuple-element.68), channel_id=1, source_target_pairs={{0,1},{1,2},{2,3},{3,4},{4,5},{5,6},{6,7},{7,0},{8,9},{9,10},{10,1... | collective-permute-start | bytes 393224 | tf_op jit(solution)/shard_map/ppermute | solution.py:32
  48.4 8.3 %collective-permute-start.7 = (f32[256,128]{1,0:T(8,128)S(1)}, f32[256,128]{1,0:T(8,128)S(1)}, u32[]{:S(2)}, u32[]{:S(2)}) collective-permute-start(f32[256,128]{1,0:T(8,128)S(1)} %get-tuple-element.69), channel_id=1, source_target_pairs={{0,7},{1,0},{2,1},{3,2},{4,3},{5,4},{6,5},{7,6},{8,15},{9,8},{10,9... | collective-permute-start | bytes 393224 | tf_op jit(solution)/shard_map/ppermute | solution.py:32
  56.7 20.4 %collective-permute-start.14 = (f32[3,256,128]{2,1,0:T(8,128)S(1)}, f32[3,256,128]{2,1,0:T(8,128)S(1)}, u32[]{:S(2)}, u32[]{:S(2)}) collective-permute-start(f32[3,256,128]{2,1,0:T(8,128)S(1)} %get-tuple-element.88), channel_id=1, source_target_pairs={{0,1},{1,2},{2,3},{3,4},{4,5},{5,6},{6,7},{7,0},{8,9},{9,10},{10,1... | collective-permute-start | bytes 1179656 | tf_op jit(solution)/shard_map/ppermute | solution.py:32
  56.9 23.0 %collective-permute-start.17 = (f32[3,256,128]{2,1,0:T(8,128)S(1)}, f32[3,256,128]{2,1,0:T(8,128)S(1)}, u32[]{:S(2)}, u32[]{:S(2)}) collective-permute-start(f32[3,256,128]{2,1,0:T(8,128)S(1)} %get-tuple-element.93), channel_id=1, source_target_pairs={{0,7},{1,0},{2,1},{3,2},{4,3},{5,4},{6,5},{7,6},{8,15},{9,8},{10,9... | collective-permute-start | bytes 1179656 | tf_op jit(solution)/shard_map/ppermute | solution.py:32
  71.5 14.7 %collective-permute-start.12 = (f32[256,128]{1,0:T(8,128)S(1)}, f32[256,128]{1,0:T(8,128)S(1)}, u32[]{:S(2)}, u32[]{:S(2)}) collective-permute-start(f32[256,128]{1,0:T(8,128)S(1)} %get-tuple-element.85), channel_id=1, source_target_pairs={{0,1},{1,2},{2,3},{3,4},{4,5},{5,6},{6,7},{7,0},{8,9},{9,10},{10,1... | collective-permute-start | bytes 393224 | tf_op jit(solution)/shard_map/ppermute | solution.py:32
  71.6 14.7 %collective-permute-start.13 = (f32[256,128]{1,0:T(8,128)S(1)}, f32[256,128]{1,0:T(8,128)S(1)}, u32[]{:S(2)}, u32[]{:S(2)}) collective-permute-start(f32[256,128]{1,0:T(8,128)S(1)} %get-tuple-element.86), channel_id=1, source_target_pairs={{0,7},{1,0},{2,1},{3,2},{4,3},{5,4},{6,5},{7,6},{8,15},{9,8},{10,9... | collective-permute-start | bytes 393224 | tf_op jit(solution)/shard_map/ppermute | solution.py:32
  77.1 9.1 %collective-permute-start.15 = (f32[32,1024]{1,0:T(8,128)S(1)}, f32[32,1024]{1,0:T(8,128)S(1)}, u32[]{:S(2)}, u32[]{:S(2)}) collective-permute-start(f32[32,1024]{1,0:T(8,128)S(1)} %get-tuple-element.89), channel_id=1, source_target_pairs={{0,8},{8,16},{16,24},{24,0},{1,9},{9,17},{17,25},{25,1},{2,10},{10... | collective-permute-start | bytes 393224 | tf_op jit(solution)/shard_map/ppermute | solution.py:32
  77.1 9.1 %collective-permute-start.16 = (f32[32,1024]{1,0:T(8,128)S(1)}, f32[32,1024]{1,0:T(8,128)S(1)}, u32[]{:S(2)}, u32[]{:S(2)}) collective-permute-start(f32[32,1024]{1,0:T(8,128)S(1)} %get-tuple-element.89), channel_id=1, source_target_pairs={{0,24},{8,0},{16,8},{24,16},{1,25},{9,1},{17,9},{25,17},{2,26},{10... | collective-permute-start | bytes 393224 | tf_op jit(solution)/shard_map/ppermute | solution.py:32
  78.9 7.4 %slice-start = ((s8[6340608]{0:T(1024)(128)(4,1)}), s8[2146304]{0:T(1024)(128)(4,1)S(1)}, s32[]{:S(2)}) async-start(s8[6340608]{0:T(1024)(128)(4,1)} %bitcast.34), calls=%async_computation.2 | async-start | bytes 4292608
  79.9 6.4 %slice-start.1 = ((s8[6340608]{0:T(1024)(128)(4,1)}), s8[4194304]{0:T(1024)(128)(4,1)S(1)}, s32[]{:S(2)}) async-start(s8[6340608]{0:T(1024)(128)(4,1)} %bitcast.34), calls=%async_computation.3 | async-start | bytes 8388608
  79.9 6.4 %copy-start.4 = (bf16[256,32]{1,0:T(8,128)(2,1)S(1)}, bf16[256,32]{1,0:T(8,128)(2,1)}, u32[]{:S(2)}) copy-start(bf16[256,32]{1,0:T(8,128)(2,1)} %constant.74.clone.refs_12_) | copy-start | bytes 49156
  86.3 16.2 %copy-start.6 = (f32[64,64,1,1]{1,0,3,2:T(8,128)S(1)}, f32[64,64,1,1]{1,0,3,2:T(8,128)}, u32[]{:S(2)}) copy-start(f32[64,64,1,1]{1,0,3,2:T(8,128)} %constant.84) | copy-start | bytes 49156
  86.3 23.4 %copy-start.9 = (f32[64]{0:T(128)S(1)}, f32[64]{0:T(128)}, u32[]{:S(2)}) copy-start(f32[64]{0:T(128)} %constant.77.clone) | copy-start | bytes 772
  86.3 34.4 %copy-start.7 = (f32[64,64,1]{1,0,2:T(8,128)S(1)}, f32[64,64,1]{1,0,2:T(8,128)}, u32[]{:S(2)}) copy-start(f32[64,64,1]{1,0,2:T(8,128)} %constant.85) | copy-start | bytes 49156
  86.3 34.8 %copy-start.8 = (f32[128,128,1]{1,0,2:T(8,128)S(1)}, f32[128,128,1]{1,0,2:T(8,128)}, u32[]{:S(2)}) copy-start(f32[128,128,1]{1,0,2:T(8,128)} %constant.86) | copy-start | bytes 196612
  86.3 34.8 %copy-start.10 = (f32[128]{0:T(128)S(1)}, f32[128]{0:T(128)}, u32[]{:S(2)}) copy-start(f32[128]{0:T(128)} %constant.78.clone) | copy-start | bytes 1540
  105.3 32.2 %copy-start.5 = (bf16[64,128]{1,0:T(8,128)(2,1)S(1)}, bf16[64,128]{1,0:T(8,128)(2,1)}, u32[]{:S(2)}) copy-start(bf16[64,128]{1,0:T(8,128)(2,1)} %constant.79.clone.refs_2_) | copy-start | bytes 49156
  105.3 12.7 %all-to-all-start = ((f32[32,1,1536]{2,1,0:T(1,128)}), f32[32,1,1536]{2,1,0:T(1,128)S(1)}, u32[]{:S(2)}, u32[]{:S(2)}) async-start(f32[32,1,1536]{2,1,0:T(1,128)} %reshape.69), calls=%async_computation | async-start | bytes 393216 | tf_op jit(solution)/shard_map/all_to_all | solution.py:746
